TPU v7x, 512 devices: a whole 4x8x8 slice. The times are simulated.
512 devices in a mesh: node: 32 (over y, x_hi, core), group: 16 (over z, x_lo).
Axes of the slice: x: 4 (x_hi: 2, x_lo: 2; x = x_hi * 2 + x_lo), y: 8, z: 8, core: 2. Of those that a mesh axis runs over, the one named last changes fastest.
Arguments:
- hidden_in: bfloat16 [98304, 8192], P(('node', 'group')), may hold values from -24 to 24
- key_grad: bfloat16 [98304, 512], P(('node', 'group')), may hold values from -0.19042969 to 0.19042969
- gain_second: bfloat16 [8192], P('group'), may hold values from 0.099609375 to 1.8984375
- weight_second: bfloat16 [8192, 512], P('group'), may hold values from -0.0625 to 0.0625
- weight_main: float32 [8192, 512], P(('node', 'group')), may hold values from -0.0625 to 0.0625
- weight_m: float32 [8192, 512], P(('node', 'group')), may hold values from -6 to 6
- weight_v: float32 [8192, 512], P(('node', 'group')), may hold values from 0.05 to 20
- gain_main: float32 [8192], P(('node', 'group')), may hold values from 0.5 to 1.5
- gain_m: float32 [8192], P(('node', 'group')), may hold values from -6 to 6
- gain_v: float32 [8192], P(('node', 'group')), may hold values from 0.05 to 20
Outputs:
- weight_main_new: float32 [8192, 512], P(('node', 'group'))
- weight_m_new: float32 [8192, 512], P(('node', 'group'))
- weight_v_new: float32 [8192, 512], P(('node', 'group'))
- gain_main_new: float32 [8192], P(('node', 'group'))
- gain_m_new: float32 [8192], P(('node', 'group'))
- gain_v_new: float32 [8192], P(('node', 'group'))
All inputs are finite; a program needn't handle non-finite values.
Results may differ from a plain program's by a relative error of at most 0.0039.
Values may be sent and summed in bfloat16 or wider, within the bound.
No kernel may reach another device: no remote copies, remote signals or barrier semaphores. Data moves between devices by JAX's collectives and lax.ppermute only.
A program may use at most 128 MiB of HBM per device.

v0:
```python
import jax
import jax.numpy as jnp
from jax import lax
from jax.sharding import PartitionSpec as P

norm_eps = 1e-05
beta_one = 0.9
beta_two = 0.999
adam_eps = 1e-08
learn_rate = 0.0003
weight_decay = 0.1
bias_one = 1.0 - 2.6561398887587544e-05
bias_two = 1.0 - 0.9047921471137096


def adam_update(weights, moment_one, moment_two, gradient):
    moment_new = beta_one * moment_one + (1.0 - beta_one) * gradient
    square_new = beta_two * moment_two + (1.0 - beta_two) * gradient * gradient
    direction = moment_new / bias_one / (jnp.sqrt(square_new / bias_two) + adam_eps)
    return (weights - learn_rate * (direction + weight_decay * weights), moment_new, square_new)


def on_device(
    hidden_in,
    key_grad,
    gain_second,
    weight_second,
    weight_main,
    weight_m,
    weight_v,
    gain_main,
    gain_m,
    gain_v,
):
    groups = lax.axis_size("group")
    nodes = lax.axis_size("node")
    owned_rows = weight_main.shape[0]
    proj_width = key_grad.shape[1]
    wide_in = hidden_in.astype(jnp.float32)
    inverse = lax.rsqrt(jnp.mean(wide_in * wide_in, axis=1, keepdims=True) + norm_eps)
    scaled = wide_in * inverse
    weight_full, gain_full = (
        lax.all_gather(weight_second, "group", axis=0, tiled=True),
        lax.all_gather(gain_second, "group", axis=0, tiled=True),
    )
    normed = (scaled * gain_full.astype(jnp.float32)).astype(jnp.bfloat16)
    input_grad = lax.dot_general(
        key_grad, weight_full, (((1,), (1,)), ((), ())), preferred_element_type=jnp.float32
    ).astype(jnp.bfloat16)
    partial_value = lax.dot_general(
        normed, key_grad, (((0,), (0,)), ((), ())), preferred_element_type=jnp.float32
    ).astype(jnp.bfloat16)
    split_grad = partial_value.reshape(nodes, groups, owned_rows, proj_width)
    arrived = lax.all_to_all(split_grad, "group", split_axis=1, concat_axis=1, tiled=True)
    group_total = jnp.sum(arrived.astype(jnp.float32), axis=1).astype(jnp.bfloat16)
    node_pieces = lax.all_to_all(group_total, "node", split_axis=0, concat_axis=0, tiled=True)
    weight_grad = jnp.sum(node_pieces.astype(jnp.float32), axis=0)
    gain_term = jnp.sum(input_grad.astype(jnp.float32) * scaled, axis=0)
    gain_grad = lax.psum_scatter(gain_term, ("node", "group"), scatter_dimension=0, tiled=True)
    weight_new, weight_first, weight_square = adam_update(
        weight_main, weight_m, weight_v, weight_grad
    )
    gain_new, gain_first, gain_square = adam_update(gain_main, gain_m, gain_v, gain_grad)
    return (weight_new, weight_first, weight_square, gain_new, gain_first, gain_square)


def solution(mesh):
    placed = (
        P(("node", "group"), None),
        P(("node", "group"), None),
        P("group"),
        P("group", None),
        P(("node", "group"), None),
        P(("node", "group"), None),
        P(("node", "group"), None),
        P(("node", "group")),
        P(("node", "group")),
        P(("node", "group")),
    )
    return jax.shard_map(
        on_device,
        mesh=mesh,
        in_specs=placed,
        out_specs=(
            P(("node", "group"), None),
            P(("node", "group"), None),
            P(("node", "group"), None),
            P(("node", "group")),
            P(("node", "group")),
            P(("node", "group")),
        ),
        check_vma=False,
    )
```

profile of v0, /device:TPU:1, one launch (start us, length us, event | category | flops | bytes accessed | tf_op | source)
XLA Modules:
  0.0 504.4 jit_solution(6566252791148068901)
XLA Ops:
  7.2 0.0 copy-start
  7.2 2.6 fusion.4
  9.8 0.7 reshape.25
  10.5 33.5 %all-gather = bf16[16,1,512]{2,1,0:T(2,128)(2,1)S(1)} all-gather(bf16[1,1,512]{2,1,0:T(2,128)(2,1)S(1)} %reshape.25), channel_id=1, replica_groups=mesh['node'=32,'group'=16] {'group'}, dimensions={0}, use_global_device_ids=true | all-gather | bytes 17408 | tf_op jit(solution)/shard_map/all_gather | solution.py:44
  44.1 7.6 %convolution_convert_fusion = bf16[8192,512]{1,0:T(8,128)(2,1)} fusion(bf16[192,512]{1,0:T(8,128)(2,1)S(1)} %copy-done, bf16[192,8192]{1,0:T(8,128)(2,1)} %param.10, f32[8192]{0:T(1024)S(1)} %bitcast.6, f32[192]{0:T(256)S(1)} %add_rsqrt_fusion), kind=kOutput, calls=%fused_computation | convolution fusion | flops 1621098496 | bytes 11764480 | tf_op jit(solution)/shard_map/dot_general | solution.py:50
  51.7 8.0 %copy.17 = bf16[32,16,16,512]{3,2,0,1:T(8,128)(2,1)} copy(bf16[32,16,16,512]{3,2,1,0:T(8,128)(2,1)} %bitcast.5) | data formatting | bytes 16777216 | tf_op jit(solution)/shard_map/reshape | solution.py:53
  59.7 4.8 all-to-all-start
  64.5 0.0 copy-start.1
  64.5 0.0 all-gather.3.cloned.1.call-start
  64.6 0.7 all-gather.3.cloned.1.call-update
  65.3 220.8 %all-to-all-done = bf16[32,16,16,512]{3,2,0,1:T(8,128)(2,1)} async-done(((bf16[32,16,16,512]{3,2,0,1:T(8,128)(2,1)}), bf16[32,16,16,512]{3,2,0,1:T(8,128)(2,1)}, u32[]{:S(2)}, u32[]{:S(2)}) %all-to-all-start) | async-done | bytes 8388640 | tf_op jit(solution)/shard_map/all_to_all | solution.py:54
  286.1 6.3 %reduce_sum.40 = bf16[32,16,512]{2,1,0:T(8,128)(2,1)} reduce(bf16[32,16,16,512]{3,2,0,1:T(8,128)(2,1)} %all-to-all-done, bf16[]{:T(256)} %constant.16.clone.1), dimensions={1}, to_apply=%region_1.0 | reduce | flops 3932160 | bytes 8912898 | tf_op jit(solution)/shard_map/reduce_sum | solution.py:55
  292.4 11.1 %all-to-all-start.1 = ((bf16[32,16,512]{2,1,0:T(8,128)(2,1)}), bf16[32,16,512]{2,1,0:T(8,128)(2,1)}, u32[]{:S(2)}, u32[]{:S(2)}) async-start(bf16[32,16,512]{2,1,0:T(8,128)(2,1)} %reduce_sum.40), calls=%async_computation.1 | async-start | bytes 1048576 | tf_op jit(solution)/shard_map/all_to_all | solution.py:56
  303.6 0.0 copy-start.5
  303.6 0.0 copy-start.6
  303.6 0.0 copy-start.7
  303.6 0.0 copy-start.2
  303.7 0.0 copy-start.4
  303.7 86.4 %all-gather.3.cloned.1.call-done = bf16[8192,512]{1,0:T(8,128)(2,1)} async-done(((bf16[512,512]{1,0:T(8,128)(2,1)}), bf16[8192,512]{1,0:T(8,128)(2,1)}) %all-gather.3.cloned.1.call-update) | async-done | bytes 8388624 | tf_op jit(solution)/shard_map/all_gather | solution.py:43
  390.0 6.3 %fusion.8 = f32[8192]{0:T(1024)S(1)} fusion(f32[192]{0:T(256)S(1)} %add_rsqrt_fusion, bf16[192,8192]{1,0:T(8,128)(2,1)S(1)} %copy-done.1, bf16[192,512]{1,0:T(8,128)(2,1)S(1)} %copy-done, bf16[8192,512]{1,0:T(8,128)(2,1)} %all-gather.3.cloned.1.call-done), kind=kOutput, calls=%fused_computation.11 | convolution fusion | flops 1620041728 | bytes 11764480 | tf_op jit(solution)/shard_map/dot_general | solution.py:47
  396.4 98.7 %all-reduce = f32[8192]{0:T(1024)S(1)} all-reduce(f32[8192]{0:T(1024)S(1)} %fusion.8), channel_id=2, replica_groups=mesh['node'=32,'group'=16] {'node','group'}, use_global_device_ids=true, to_apply=%region_4.0.clone | all-reduce | flops 8192 | bytes 65536
  495.1 0.6 multiply_subtract_fusion.1
  495.7 1.1 convert_reduce_fusion
  496.9 0.7 multiply_subtract_fusion
  (12 shorter events, 0.1 us)
Async XLA Ops:
  7.2 36.9 %copy-start = (bf16[192,512]{1,0:T(8,128)(2,1)S(1)}, bf16[192,512]{1,0:T(8,128)(2,1)}, u32[]{:S(2)}) copy-start(bf16[192,512]{1,0:T(8,128)(2,1)} %param.11) | copy-start | bytes 589828
  59.7 226.4 %all-to-all-start = ((bf16[32,16,16,512]{3,2,0,1:T(8,128)(2,1)}), bf16[32,16,16,512]{3,2,0,1:T(8,128)(2,1)}, u32[]{:S(2)}, u32[]{:S(2)}) async-start(bf16[32,16,16,512]{3,2,0,1:T(8,128)(2,1)} %copy.17), calls=%async_computation | async-start | bytes 16777216 | tf_op jit(solution)/shard_map/all_to_all | solution.py:54
  64.5 325.5 %copy-start.1 = (bf16[192,8192]{1,0:T(8,128)(2,1)S(1)}, bf16[192,8192]{1,0:T(8,128)(2,1)}, u32[]{:S(2)}) copy-start(bf16[192,8192]{1,0:T(8,128)(2,1)} %param.10) | copy-start | bytes 9437188
  64.5 325.5 %all-gather.3.cloned.1.call-start = ((), (), s32[]{:S(2)}) async-start(), calls=%async_computation.2 | async-start | bytes 8912896 | tf_op jit(solution)/shard_map/all_gather | solution.py:43
  292.4 203.3 %all-to-all-start.1 = ((bf16[32,16,512]{2,1,0:T(8,128)(2,1)}), bf16[32,16,512]{2,1,0:T(8,128)(2,1)}, u32[]{:S(2)}, u32[]{:S(2)}) async-start(bf16[32,16,512]{2,1,0:T(8,128)(2,1)} %reduce_sum.40), calls=%async_computation.1 | async-start | bytes 1048576 | tf_op jit(solution)/shard_map/all_to_all | solution.py:56
  303.6 191.5 %copy-start.5 = (f32[16]{0:T(128)S(1)}, f32[16]{0:T(128)}, u32[]{:S(2)}) copy-start(f32[16]{0:T(128)} %param.17) | copy-start | bytes 196
  303.6 191.5 %copy-start.6 = (f32[16]{0:T(128)S(1)}, f32[16]{0:T(128)}, u32[]{:S(2)}) copy-start(f32[16]{0:T(128)} %param.18) | copy-start | bytes 196
  303.6 191.5 %copy-start.7 = (f32[16]{0:T(128)S(1)}, f32[16]{0:T(128)}, u32[]{:S(2)}) copy-start(f32[16]{0:T(128)} %param.19) | copy-start | bytes 196
  303.6 193.2 %copy-start.2 = (f32[16,512]{1,0:T(8,128)S(1)}, f32[16,512]{1,0:T(8,128)}, u32[]{:S(2)}) copy-start(f32[16,512]{1,0:T(8,128)} %param.14) | copy-start | bytes 98308
  303.6 193.2 %copy-start.3 = (f32[16,512]{1,0:T(8,128)S(1)}, f32[16,512]{1,0:T(8,128)}, u32[]{:S(2)}) copy-start(f32[16,512]{1,0:T(8,128)} %param.15) | copy-start | bytes 98308
  303.7 193.2 %copy-start.4 = (f32[16,512]{1,0:T(8,128)S(1)}, f32[16,512]{1,0:T(8,128)}, u32[]{:S(2)}) copy-start(f32[16,512]{1,0:T(8,128)} %param.16) | copy-start | bytes 98308
Sparse Core Ops, SparseCore 0:
  67.5 322.5 all-gather.2
where the time goes:
time: 505 us; the launch traced here: 504 us
  waiting for transfers between devices  308 us (61%)
  blocking collectives  132 us (26%)
  starting transfers between devices  16 us (3%)
  between operations  14.2 us (3%)
  matrix products  14 us (3%)
  other arithmetic  11.4 us (2%)
  local copies, waits for them, and re-layouts  8.77 us (2%)
    all_to_all x1, waiting for transfers between devices, on_device(): lax.all_to_all(split_grad, 'group', split_axis=1, concat_axis=1, tiled=True)  221 us
    unnamed x1, blocking collectives  98.7 us
    all_gather x1, waiting for transfers between devices, on_device(): lax.all_gather(weight_second, 'group', axis=0, tiled=True)  86.4 us
    all_gather x1, blocking collectives, on_device(): lax.all_gather(gain_second, 'group', axis=0, tiled=True)  33.5 us
    all_to_all x1, starting transfers between devices, on_device(): lax.all_to_all(group_total, 'node', split_axis=0, concat_axis=0, tiled=True)  11.1 us
  transfers between devices with their start and end apart: 3, of which 2 were waited for; matrix products, arithmetic and copies ran while one was open for 3% of the time, Pallas kernels for 0%

commit v1 on v0

v1 whole, which is shorter than its diff:
```python
import jax
import jax.numpy as jnp
from jax import lax
from jax.experimental import pallas as pl
from jax.experimental.pallas import tpu as pltpu
from jax.sharding import Mesh, PartitionSpec as P

norm_eps = 1e-05
beta_one = 0.9
beta_two = 0.999
adam_eps = 1e-08
learn_rate = 0.0003
weight_decay = 0.1
bias_one = 1.0 - 2.6561398887587544e-05
bias_two = 1.0 - 0.9047921471137096

SIZES = (8, 2, 2, 8, 2)
ALL = ("y", "xh", "core", "z", "xl")
GROUP = ("z", "xl")
X = ("xh", "xl")
WIDE, NARROW = 256, 128


def adam_update(weights, moment_one, moment_two, gradient):
    moment_new = beta_one * moment_one + (1.0 - beta_one) * gradient
    square_new = beta_two * moment_two + (1.0 - beta_two) * gradient * gradient
    direction = moment_new / bias_one / (jnp.sqrt(square_new / bias_two) + adam_eps)
    return (weights - learn_rate * (direction + weight_decay * weights), moment_new, square_new)


def partial_kernel(core_ref, own_ref, got_ref, own_key_ref, got_key_ref, a_ref, b_ref, c_ref, keys):
    step = pl.program_id(0)
    tokens, width = own_ref.shape

    @pl.when(step == 0)
    def _():
        for half, (rows, key) in enumerate(((own_ref, own_key_ref), (got_ref, got_key_ref))):
            def add(i, total):
                block = rows[:, pl.ds(pl.multiple_of(i * 512, 512), 512)].astype(jnp.float32)
                block = block * block
                return total + (block[:, :128] + block[:, 128:256]) + (block[:, 256:384] + block[:, 384:])

            total = lax.fori_loop(0, width // 512, add, jnp.zeros((tokens, 128), jnp.float32))
            mean = jnp.sum(total, axis=1, keepdims=True) * (1.0 / width)
            inverse = lax.rsqrt(mean + norm_eps)
            keys[half * tokens : (half + 1) * tokens, :] = (
                key[...].astype(jnp.float32) * inverse
            ).astype(jnp.bfloat16)

    for xh in range(2):
        start = pl.multiple_of(step * 1024 + xh * 512 + core_ref[0] * 256, 256)
        total = lax.dot_general(
            own_ref[:, pl.ds(start, 256)],
            keys[:tokens, :],
            (((0,), (0,)), ((), ())),
            preferred_element_type=jnp.float32,
        ) + lax.dot_general(
            got_ref[:, pl.ds(start, 256)],
            keys[tokens:, :],
            (((0,), (0,)), ((), ())),
            preferred_element_type=jnp.float32,
        )
        rounded = total.astype(jnp.bfloat16).reshape(8, 2, 16, 512)
        for xl in range(2):
            a_ref[xh, xl, 0] = rounded[:, xl, :, :WIDE]
        b_ref[0, xh] = rounded[:, :, :, WIDE : WIDE + NARROW]
        c_ref[:, 0, xh] = rounded[:, :, :, WIDE + NARROW :]


def partial_grad(core, own, got, own_key, got_key):
    whole = lambda shape: pl.BlockSpec(shape, lambda i, c: (0, 0))
    return pl.pallas_call(
        partial_kernel,
        grid_spec=pltpu.PrefetchScalarGridSpec(
            num_scalar_prefetch=1,
            grid=(8,),
            in_specs=[whole(own.shape), whole(got.shape), whole(own_key.shape), whole(got_key.shape)],
            out_specs=[
                pl.BlockSpec((2, 2, 1, 8, 16, WIDE), lambda i, c: (0, 0, i, 0, 0, 0)),
                pl.BlockSpec((1, 2, 8, 2, 16, NARROW), lambda i, c: (i, 0, 0, 0, 0, 0)),
                pl.BlockSpec((8, 1, 2, 2, 16, NARROW), lambda i, c: (0, i, 0, 0, 0, 0)),
            ],
            scratch_shapes=[pltpu.VMEM((2 * own.shape[0], own_key.shape[1]), jnp.bfloat16)],
        ),
        out_shape=[
            jax.ShapeDtypeStruct((2, 2, 8, 8, 16, WIDE), jnp.bfloat16),
            jax.ShapeDtypeStruct((8, 2, 8, 2, 16, NARROW), jnp.bfloat16),
            jax.ShapeDtypeStruct((8, 8, 2, 2, 16, NARROW), jnp.bfloat16),
        ],
        compiler_params=pltpu.CompilerParams(vmem_limit_bytes=40 * 1024 * 1024),
        cost_estimate=pl.CostEstimate(
            flops=2 * 384 * 4096 * 512, bytes_accessed=11 * 1024 * 1024, transcendentals=0
        ),
    )(core, own, got, own_key, got_key)


def exchange(value, axes):
    return lax.all_to_all(value, axes, split_axis=0, concat_axis=0, tiled=True)


def summed(value):
    return jnp.sum(value.astype(jnp.float32), axis=0)


def on_device(
    hidden_in,
    key_grad,
    gain_second,
    weight_second,
    weight_main,
    weight_m,
    weight_v,
    gain_main,
    gain_m,
    gain_v,
):
    swap = [(0, 1), (1, 0)]
    got = lax.ppermute(hidden_in, "core", swap)
    got_key = lax.ppermute(key_grad, "core", swap)

    node = lax.axis_index(("y", "xh", "core"))
    rows = lax.dynamic_slice_in_dim(weight_second, node * 16, 16, 0)
    gains = lax.dynamic_slice_in_dim(gain_second, node * 16, 16, 0)
    pairs = [
        (m * 16 + g, (2 * g + m // 16) * 16 + m % 16) for m in range(32) for g in range(16)
    ]
    packed = jnp.concatenate([rows, jnp.broadcast_to(gains[:, None], (16, 128))], axis=1)
    packed = lax.ppermute(packed, ALL, pairs).astype(jnp.float32)
    rows, gains = packed[:, :512], packed[:, 512:513]

    core = lax.axis_index("core").astype(jnp.int32).reshape(1)
    wide, left, right = partial_grad(core, hidden_in, got, key_grad, got_key)
    wide = exchange(wide.reshape(4, 64, 16, WIDE), X)
    left = exchange(left.reshape(8, 32, 16, NARROW), "y")
    right = exchange(right.reshape(8, 32, 16, NARROW), "z")
    wide, left, right = (summed(v).astype(jnp.bfloat16) for v in (wide, left, right))
    wide = exchange(wide, ("y", "z"))
    left = exchange(left, ("xh", "z", "xl"))
    right = exchange(right, ("y", "xh", "xl"))
    scaled_grad = jnp.concatenate([summed(wide), summed(left), summed(right)], axis=1)

    weight_grad = scaled_grad * gains
    gain_grad = jnp.sum(scaled_grad * rows, axis=1)
    weight_new, weight_first, weight_square = adam_update(
        weight_main, weight_m, weight_v, weight_grad
    )
    gain_new, gain_first, gain_square = adam_update(gain_main, gain_m, gain_v, gain_grad)
    return (weight_new, weight_first, weight_square, gain_new, gain_first, gain_square)


def solution(mesh):
    fine = Mesh(mesh.devices.reshape(SIZES), ALL)
    placed = (
        P(ALL, None),
        P(ALL, None),
        P(GROUP),
        P(GROUP, None),
        P(ALL, None),
        P(ALL, None),
        P(ALL, None),
        P(ALL),
        P(ALL),
        P(ALL),
    )
    return jax.shard_map(
        on_device,
        mesh=fine,
        in_specs=placed,
        out_specs=(P(ALL, None),) * 3 + (P(ALL),) * 3,
        check_vma=False,
    )
```

time: 505 us -> 177 us (0.35)
  waiting for transfers between devices: 308 us -> 56.6 us
  blocking collectives: 132 us -> 58.7 us
  starting transfers between devices: 16 us -> 40.1 us
  matrix products: 14 us -> 0 us
  between operations: 14.2 us -> 0.81 us
  Pallas kernels: 0 us -> 9 us
  local copies, waits for them, and re-layouts: 8.77 us -> 3.13 us
    all_to_all x2 -> x4, waiting for transfers between devices: 221 us -> 40.1 us  [exchange(): return lax.all_to_all(value, axes, split_axis=0, concat_axis=0, tiled=True)]
    unnamed x1 -> x0, blocking collectives: 98.7 us -> none
    all_gather x1 -> x0, waiting for transfers between devices: 86.4 us -> none  [on_device(): lax.all_gather(weight_second, 'group', axis=0, tiled=True)]
    all_to_all x0 -> x2, blocking collectives: none -> 58.7 us  [exchange(): return lax.all_to_all(value, axes, split_axis=0, concat_axis=0, tiled=True)]
    all_gather x1 -> x0, blocking collectives: 33.5 us -> none  [on_device(): lax.all_gather(gain_second, 'group', axis=0, tiled=True)]
    ppermute x0 -> x3, waiting for transfers between devices: none -> 16.5 us  [the longest x1 12.7 us: on_device(): packed = lax.ppermute(packed, ALL, pairs).astype(jnp.float32)]
    ppermute x0 -> x3, starting transfers between devices: none -> 15.7 us  [the longest x1 8.92 us: on_device(): got = lax.ppermute(hidden_in, 'core', swap)]
    dot_general x2 -> x0, matrix products: 14 us -> none  [the longest x1 7.64 us: on_device(): lax.dot_general(normed, key_grad, (((0,), (0,)), ((), ())), preferred_ele...]
  transfers between devices with their start and end apart: 3 -> 7, of which waited for: 2 -> 5; matrix products, arithmetic and copies ran while one was open for 3% -> 3% of each run, Pallas kernels for 0% -> 0%
where the time goes in v1:
time: 177 us; the launch traced here: 175 us
  blocking collectives  58.7 us (33%)
  waiting for transfers between devices  56.6 us (32%)
  starting transfers between devices  40.1 us (23%)
  Pallas kernels  9 us (5%)
  other arithmetic  6.9 us (4%)
  local copies, waits for them, and re-layouts  3.13 us (2%)
    all_to_all x2, blocking collectives, exchange(): return lax.all_to_all(value, axes, split_axis=0, concat_axis=0, tiled=True)  58.7 us
    all_to_all x4, waiting for transfers between devices, exchange(): return lax.all_to_all(value, axes, split_axis=0, concat_axis=0, tiled=True)  40.1 us
    all_to_all x4, starting transfers between devices, exchange(): return lax.all_to_all(value, axes, split_axis=0, concat_axis=0, tiled=True)  24.4 us
    ppermute x1, waiting for transfers between devices, on_device(): packed = lax.ppermute(packed, ALL, pairs).astype(jnp.float32)  12.7 us
    pallas_call x1, Pallas kernels, partial_grad(): pl.pallas_call(partial_kernel, grid_spec=pltpu.PrefetchScalarGridSpec(num...  9 us
    ppermute x1, starting transfers between devices, on_device(): got = lax.ppermute(hidden_in, 'core', swap)  8.92 us
    reduce_sum x6, other arithmetic, summed(): return jnp.sum(value.astype(jnp.float32), axis=0)  5.52 us
    ppermute x1, starting transfers between devices, on_device(): packed = lax.ppermute(packed, ALL, pairs).astype(jnp.float32)  4.84 us
  transfers between devices with their start and end apart: 7, of which 5 were waited for; matrix products, arithmetic and copies ran while one was open for 3% of the time, Pallas kernels for 0%

profile of v1, /device:TPU:1, one launch (start us, length us, event | category | flops | bytes accessed | tf_op | source)
XLA Modules:
  0.0 175.3 jit_solution(11347306242330961643)
XLA Ops:
  0.6 8.9 %collective-permute-start = (bf16[192,8192]{1,0:T(8,128)(2,1)}, bf16[192,8192]{1,0:T(8,128)(2,1)}, u32[]{:S(2)}, u32[]{:S(2)}) collective-permute-start(bf16[192,8192]{1,0:T(8,128)(2,1)} %own_ref.1), channel_id=1, source_target_pairs={{0,16},{16,0},{1,17},{17,1},{2,18},{18,2},{3,19},{19,3},{4,20},{20... | collective-permute-start | bytes 9437192 | tf_op jit(solution)/shard_map/ppermute | solution.py:118
  9.6 1.9 %collective-permute-start.1 = (bf16[192,512]{1,0:T(8,128)(2,1)}, bf16[192,512]{1,0:T(8,128)(2,1)S(1)}, u32[]{:S(2)}, u32[]{:S(2)}) collective-permute-start(bf16[192,512]{1,0:T(8,128)(2,1)} %own_key_ref.1), channel_id=1, source_target_pairs={{0,16},{16,0},{1,17},{17,1},{2,18},{18,2},{3,19},{19,3},{4,20},{20... | collective-permute-start | bytes 589832 | tf_op jit(solution)/shard_map/ppermute | solution.py:119
  11.5 3.8 %collective-permute-done.1.got_key_ref = bf16[192,512]{1,0:T(8,128)(2,1)S(1)} collective-permute-done((bf16[192,512]{1,0:T(8,128)(2,1)}, bf16[192,512]{1,0:T(8,128)(2,1)S(1)}, u32[]{:S(2)}, u32[]{:S(2)}) %collective-permute-start.1) | collective-permute-done | bytes 196640 | tf_op jit(solution)/shard_map/ppermute | solution.py:119
  15.3 1.9 %copy-done.1 = bf16[192,8192]{1,0:T(8,128)(2,1)S(1)} copy-done((bf16[192,8192]{1,0:T(8,128)(2,1)S(1)}, bf16[192,8192]{1,0:T(8,128)(2,1)}, u32[]{:S(2)}) %copy-start.1) | copy-done | bytes 3145752
  17.2 0.9 copy-done.2
  18.2 9.0 %shard_map.145 = (bf16[2,2,8,8,16,256]{5,4,3,2,1,0:T(8,128)(2,1)S(1)}, bf16[8,2,8,2,16,128]{5,4,3,2,1,0:T(8,128)(2,1)S(1)}, bf16[8,8,2,2,16,128]{5,4,3,2,1,0:T(8,128)(2,1)}) custom-call(s32[1]{0:T(128)} %bitcast.core_ref, bf16[192,8192]{1,0:T(8,128)(2,1)S(1)} %copy-done.1, bf16[192,8192]{1,0:T(8,128)(2,1)} %collective-permute-done.got_ref, ...), custom_call_target="tpu_custom_call" | custom-call | flops 1610612736 | bytes 11534336 | tf_op jit(solution)/shard_map/pallas_call | solution.py:72
  27.2 28.6 %all_to_all.30 = bf16[4,64,16,256]{3,2,1,0:T(8,128)(2,1)S(1)} all-to-all(bf16[4,64,16,256]{3,2,1,0:T(8,128)(2,1)S(1)} %bitcast.4), channel_id=1, replica_groups=mesh['y'=8,'xh'=2,'core'=2,'z'=8,'xl'=2] {'xh','xl'}, dimensions={0} | all-to-all | bytes 4194304 | tf_op jit(solution)/shard_map/all_to_all | solution.py:98
  55.8 30.1 %all_to_all.31 = bf16[8,32,16,128]{3,2,1,0:T(8,128)(2,1)} all-to-all(bf16[8,32,16,128]{3,2,1,0:T(8,128)(2,1)S(1)} %bitcast.5), channel_id=1, replica_groups=mesh['y'=8,'xh'=2,'core'=2,'z'=8,'xl'=2] {'y'}, dimensions={0} | all-to-all | bytes 2097152 | tf_op jit(solution)/shard_map/all_to_all | solution.py:98
  85.9 8.6 %all-to-all-start.4 = ((bf16[8,32,16,128]{3,2,1,0:T(8,128)(2,1)}), bf16[8,32,16,128]{3,2,1,0:T(8,128)(2,1)}, u32[]{:S(2)}, u32[]{:S(2)}) async-start(bf16[8,32,16,128]{3,2,1,0:T(8,128)(2,1)} %bitcast.3), calls=%async_computation.4 | async-start | bytes 2097152 | tf_op jit(solution)/shard_map/all_to_all | solution.py:98
  94.5 2.1 %reduce_sum.74 = bf16[32,16,128]{2,1,0:T(8,128)(2,1)} reduce(bf16[8,32,16,128]{3,2,1,0:T(8,128)(2,1)} %all_to_all.31, bf16[]{:T(256)} %constant.23.clone.1), dimensions={0}, to_apply=%region_2.0 | reduce | flops 458752 | bytes 1179650 | tf_op jit(solution)/shard_map/reduce_sum | solution.py:102
  96.6 24.0 %all-to-all-done.4 = bf16[8,32,16,128]{3,2,1,0:T(8,128)(2,1)} async-done(((bf16[8,32,16,128]{3,2,1,0:T(8,128)(2,1)}), bf16[8,32,16,128]{3,2,1,0:T(8,128)(2,1)}, u32[]{:S(2)}, u32[]{:S(2)}) %all-to-all-start.4) | async-done | bytes 1048608 | tf_op jit(solution)/shard_map/all_to_all | solution.py:98
  120.6 3.8 %all-to-all-start.3 = ((bf16[32,16,128]{2,1,0:T(8,128)(2,1)}), bf16[32,16,128]{2,1,0:T(8,128)(2,1)S(1)}, u32[]{:S(2)}, u32[]{:S(2)}) async-start(bf16[32,16,128]{2,1,0:T(8,128)(2,1)} %reduce_sum.74), calls=%async_computation.3 | async-start | bytes 262144 | tf_op jit(solution)/shard_map/all_to_all | solution.py:98
  124.5 2.1 %reduce_sum.76 = bf16[32,16,128]{2,1,0:T(8,128)(2,1)} reduce(bf16[8,32,16,128]{3,2,1,0:T(8,128)(2,1)} %all-to-all-done.4, bf16[]{:T(256)} %constant.23.clone.1), dimensions={0}, to_apply=%region_4.0 | reduce | flops 458752 | bytes 1179650 | tf_op jit(solution)/shard_map/reduce_sum | solution.py:102
  126.5 7.8 %all-to-all-done.3 = bf16[32,16,128]{2,1,0:T(8,128)(2,1)S(1)} async-done(((bf16[32,16,128]{2,1,0:T(8,128)(2,1)}), bf16[32,16,128]{2,1,0:T(8,128)(2,1)S(1)}, u32[]{:S(2)}, u32[]{:S(2)}) %all-to-all-start.3) | async-done | bytes 131104 | tf_op jit(solution)/shard_map/all_to_all | solution.py:98
  134.4 7.3 %all-to-all-start.5 = ((bf16[32,16,128]{2,1,0:T(8,128)(2,1)}), bf16[32,16,128]{2,1,0:T(8,128)(2,1)S(1)}, u32[]{:S(2)}, u32[]{:S(2)}) async-start(bf16[32,16,128]{2,1,0:T(8,128)(2,1)} %reduce_sum.76), calls=%async_computation.5 | async-start | bytes 262144 | tf_op jit(solution)/shard_map/all_to_all | solution.py:98
  141.7 1.2 reduce_sum.72
  142.9 8.2 %all-to-all-done.5 = bf16[32,16,128]{2,1,0:T(8,128)(2,1)S(1)} async-done(((bf16[32,16,128]{2,1,0:T(8,128)(2,1)}), bf16[32,16,128]{2,1,0:T(8,128)(2,1)S(1)}, u32[]{:S(2)}, u32[]{:S(2)}) %all-to-all-start.5) | async-done | bytes 131104 | tf_op jit(solution)/shard_map/all_to_all | solution.py:98
  151.2 4.6 %all-to-all-start.1 = ((bf16[64,16,256]{2,1,0:T(8,128)(2,1)}), bf16[64,16,256]{2,1,0:T(8,128)(2,1)S(1)}, u32[]{:S(2)}, u32[]{:S(2)}) async-start(bf16[64,16,256]{2,1,0:T(8,128)(2,1)} %reduce_sum.72), calls=%async_computation.1 | async-start | bytes 1048576 | tf_op jit(solution)/shard_map/all_to_all | solution.py:98
  156.0 4.8 %collective-permute-start.2 = (bf16[16,640]{1,0:T(8,128)(2,1)S(1)}, bf16[16,640]{1,0:T(8,128)(2,1)S(1)}, u32[]{:S(2)}, u32[]{:S(2)}) collective-permute-start(bf16[16,640]{1,0:T(8,128)(2,1)S(1)} %pad_maximum_fusion.1), channel_id=1, source_target_pairs={{0,0},{1,32},{2,64},{3,96},{4,128},{5,160},{6,192},{7,224},{8,256}... | collective-permute-start | bytes 61448 | tf_op jit(solution)/shard_map/ppermute | solution.py:128
  160.8 12.7 %collective-permute-done.2 = bf16[16,640]{1,0:T(8,128)(2,1)S(1)} collective-permute-done((bf16[16,640]{1,0:T(8,128)(2,1)S(1)}, bf16[16,640]{1,0:T(8,128)(2,1)S(1)}, u32[]{:S(2)}, u32[]{:S(2)}) %collective-permute-start.2) | collective-permute-done | bytes 20512 | tf_op jit(solution)/shard_map/ppermute | solution.py:128
  173.5 0.1 slice_reduce_fusion
  173.8 0.1 convert_reduce_fusion
  173.9 0.8 multiply_subtract_fusion
  174.7 0.5 multiply_subtract_fusion.1
  (27 shorter events, 0.3 us)
Async XLA Ops:
  0.6 155.3 %copy-start = (bf16[512,512]{1,0:T(8,128)(2,1)S(1)}, bf16[512,512]{1,0:T(8,128)(2,1)}, u32[]{:S(2)}) copy-start(bf16[512,512]{1,0:T(8,128)(2,1)} %param.13) | copy-start | bytes 1572868
  0.6 14.7 %collective-permute-start = (bf16[192,8192]{1,0:T(8,128)(2,1)}, bf16[192,8192]{1,0:T(8,128)(2,1)}, u32[]{:S(2)}, u32[]{:S(2)}) collective-permute-start(bf16[192,8192]{1,0:T(8,128)(2,1)} %own_ref.1), channel_id=1, source_target_pairs={{0,16},{16,0},{1,17},{17,1},{2,18},{18,2},{3,19},{19,3},{4,20},{20... | collective-permute-start | bytes 9437192 | tf_op jit(solution)/shard_map/ppermute | solution.py:118
  9.6 5.8 %collective-permute-start.1 = (bf16[192,512]{1,0:T(8,128)(2,1)}, bf16[192,512]{1,0:T(8,128)(2,1)S(1)}, u32[]{:S(2)}, u32[]{:S(2)}) collective-permute-start(bf16[192,512]{1,0:T(8,128)(2,1)} %own_key_ref.1), channel_id=1, source_target_pairs={{0,16},{16,0},{1,17},{17,1},{2,18},{18,2},{3,19},{19,3},{4,20},{20... | collective-permute-start | bytes 589832 | tf_op jit(solution)/shard_map/ppermute | solution.py:119
  15.3 1.9 %copy-start.1 = (bf16[192,8192]{1,0:T(8,128)(2,1)S(1)}, bf16[192,8192]{1,0:T(8,128)(2,1)}, u32[]{:S(2)}) copy-start(bf16[192,8192]{1,0:T(8,128)(2,1)} %own_ref.1) | copy-start | bytes 9437188
  17.2 0.9 copy-start.2
  85.9 34.7 %all-to-all-start.4 = ((bf16[8,32,16,128]{3,2,1,0:T(8,128)(2,1)}), bf16[8,32,16,128]{3,2,1,0:T(8,128)(2,1)}, u32[]{:S(2)}, u32[]{:S(2)}) async-start(bf16[8,32,16,128]{3,2,1,0:T(8,128)(2,1)} %bitcast.3), calls=%async_computation.4 | async-start | bytes 2097152 | tf_op jit(solution)/shard_map/all_to_all | solution.py:98
  94.5 61.3 %copy-start.9 = (bf16[512]{0:T(512)(128)(2,1)S(1)}, bf16[512]{0:T(512)(128)(2,1)}, u32[]{:S(2)}) copy-start(bf16[512]{0:T(512)(128)(2,1)} %param.12) | copy-start | bytes 3076
  96.6 77.3 %copy-start.3 = (f32[16,512]{1,0:T(8,128)S(1)}, f32[16,512]{1,0:T(8,128)}, u32[]{:S(2)}) copy-start(f32[16,512]{1,0:T(8,128)} %param.14) | copy-start | bytes 98308
  96.6 77.3 %copy-start.4 = (f32[16,512]{1,0:T(8,128)S(1)}, f32[16,512]{1,0:T(8,128)}, u32[]{:S(2)}) copy-start(f32[16,512]{1,0:T(8,128)} %param.15) | copy-start | bytes 98308
  96.6 77.3 %copy-start.5 = (f32[16,512]{1,0:T(8,128)S(1)}, f32[16,512]{1,0:T(8,128)}, u32[]{:S(2)}) copy-start(f32[16,512]{1,0:T(8,128)} %param.16) | copy-start | bytes 98308
  120.6 13.8 %all-to-all-start.3 = ((bf16[32,16,128]{2,1,0:T(8,128)(2,1)}), bf16[32,16,128]{2,1,0:T(8,128)(2,1)S(1)}, u32[]{:S(2)}, u32[]{:S(2)}) async-start(bf16[32,16,128]{2,1,0:T(8,128)(2,1)} %reduce_sum.74), calls=%async_computation.3 | async-start | bytes 262144 | tf_op jit(solution)/shard_map/all_to_all | solution.py:98
  124.5 50.2 %copy-start.6 = (f32[16]{0:T(128)S(1)}, f32[16]{0:T(128)}, u32[]{:S(2)}) copy-start(f32[16]{0:T(128)} %param.17) | copy-start | bytes 196
  124.5 50.2 %copy-start.7 = (f32[16]{0:T(128)S(1)}, f32[16]{0:T(128)}, u32[]{:S(2)}) copy-start(f32[16]{0:T(128)} %param.18) | copy-start | bytes 196
  124.5 50.2 %copy-start.8 = (f32[16]{0:T(128)S(1)}, f32[16]{0:T(128)}, u32[]{:S(2)}) copy-start(f32[16]{0:T(128)} %param.19) | copy-start | bytes 196
  134.4 16.8 %all-to-all-start.5 = ((bf16[32,16,128]{2,1,0:T(8,128)(2,1)}), bf16[32,16,128]{2,1,0:T(8,128)(2,1)S(1)}, u32[]{:S(2)}, u32[]{:S(2)}) async-start(bf16[32,16,128]{2,1,0:T(8,128)(2,1)} %reduce_sum.76), calls=%async_computation.5 | async-start | bytes 262144 | tf_op jit(solution)/shard_map/all_to_all | solution.py:98
  151.2 22.6 %all-to-all-start.1 = ((bf16[64,16,256]{2,1,0:T(8,128)(2,1)}), bf16[64,16,256]{2,1,0:T(8,128)(2,1)S(1)}, u32[]{:S(2)}, u32[]{:S(2)}) async-start(bf16[64,16,256]{2,1,0:T(8,128)(2,1)} %reduce_sum.72), calls=%async_computation.1 | async-start | bytes 1048576 | tf_op jit(solution)/shard_map/all_to_all | solution.py:98
  156.0 17.6 %collective-permute-start.2 = (bf16[16,640]{1,0:T(8,128)(2,1)S(1)}, bf16[16,640]{1,0:T(8,128)(2,1)S(1)}, u32[]{:S(2)}, u32[]{:S(2)}) collective-permute-start(bf16[16,640]{1,0:T(8,128)(2,1)S(1)} %pad_maximum_fusion.1), channel_id=1, source_target_pairs={{0,0},{1,32},{2,64},{3,96},{4,128},{5,160},{6,192},{7,224},{8,256}... | collective-permute-start | bytes 61448 | tf_op jit(solution)/shard_map/ppermute | solution.py:128

commit v2 on v1

--- a/solution.py
+++ b/solution.py
@@ -14,11 +14,10 @@
 bias_one = 1.0 - 2.6561398887587544e-05
 bias_two = 1.0 - 0.9047921471137096
 
-SIZES = (8, 2, 2, 8, 2)
-ALL = ("y", "xh", "core", "z", "xl")
-GROUP = ("z", "xl")
-X = ("xh", "xl")
-WIDE, NARROW = 256, 128
+SIZES = (4, 2, 2, 2, 4, 2, 2)
+ALL = ("yh", "yl", "xh", "core", "zh", "zl", "xl")
+NODE, GROUP = ALL[:4], ALL[4:]
+NEAR, FAR = ("yl", "xh", "zl", "xl"), ("yh", "zh")
 
 
 def adam_update(weights, moment_one, moment_two, gradient):
@@ -28,7 +27,7 @@
     return (weights - learn_rate * (direction + weight_decay * weights), moment_new, square_new)
 
 
-def partial_kernel(core_ref, own_ref, got_ref, own_key_ref, got_key_ref, a_ref, b_ref, c_ref, keys):
+def partial_kernel(core_ref, own_ref, got_ref, own_key_ref, got_key_ref, out_ref, keys):
     step = pl.program_id(0)
     tokens, width = own_ref.shape
 
@@ -60,11 +59,10 @@
             (((0,), (0,)), ((), ())),
             preferred_element_type=jnp.float32,
         )
-        rounded = total.astype(jnp.bfloat16).reshape(8, 2, 16, 512)
-        for xl in range(2):
-            a_ref[xh, xl, 0] = rounded[:, xl, :, :WIDE]
-        b_ref[0, xh] = rounded[:, :, :, WIDE : WIDE + NARROW]
-        c_ref[:, 0, xh] = rounded[:, :, :, WIDE + NARROW :]
+        rounded = total.astype(jnp.bfloat16).reshape(4, 2, 2, 16, 512)
+        for zl in range(2):
+            for xl in range(2):
+                out_ref[0, xh, zl, xl, 0] = rounded[:, zl, xl]
 
 
 def partial_grad(core, own, got, own_key, got_key):
@@ -75,18 +73,12 @@
             num_scalar_prefetch=1,
             grid=(8,),
             in_specs=[whole(own.shape), whole(got.shape), whole(own_key.shape), whole(got_key.shape)],
-            out_specs=[
-                pl.BlockSpec((2, 2, 1, 8, 16, WIDE), lambda i, c: (0, 0, i, 0, 0, 0)),
-                pl.BlockSpec((1, 2, 8, 2, 16, NARROW), lambda i, c: (i, 0, 0, 0, 0, 0)),
-                pl.BlockSpec((8, 1, 2, 2, 16, NARROW), lambda i, c: (0, i, 0, 0, 0, 0)),
-            ],
+            out_specs=pl.BlockSpec(
+                (1, 2, 2, 2, 1, 4, 16, 512), lambda i, c: (i % 2, 0, 0, 0, i // 2, 0, 0, 0)
+            ),
             scratch_shapes=[pltpu.VMEM((2 * own.shape[0], own_key.shape[1]), jnp.bfloat16)],
         ),
-        out_shape=[
-            jax.ShapeDtypeStruct((2, 2, 8, 8, 16, WIDE), jnp.bfloat16),
-            jax.ShapeDtypeStruct((8, 2, 8, 2, 16, NARROW), jnp.bfloat16),
-            jax.ShapeDtypeStruct((8, 8, 2, 2, 16, NARROW), jnp.bfloat16),
-        ],
+        out_shape=jax.ShapeDtypeStruct((2, 2, 2, 2, 4, 4, 16, 512), jnp.bfloat16),
         compiler_params=pltpu.CompilerParams(vmem_limit_bytes=40 * 1024 * 1024),
         cost_estimate=pl.CostEstimate(
             flops=2 * 384 * 4096 * 512, bytes_accessed=11 * 1024 * 1024, transcendentals=0
@@ -118,7 +110,7 @@
     got = lax.ppermute(hidden_in, "core", swap)
     got_key = lax.ppermute(key_grad, "core", swap)
 
-    node = lax.axis_index(("y", "xh", "core"))
+    node = lax.axis_index(NODE)
     rows = lax.dynamic_slice_in_dim(weight_second, node * 16, 16, 0)
     gains = lax.dynamic_slice_in_dim(gain_second, node * 16, 16, 0)
     pairs = [
@@ -129,15 +121,10 @@
     rows, gains = packed[:, :512], packed[:, 512:513]
 
     core = lax.axis_index("core").astype(jnp.int32).reshape(1)
-    wide, left, right = partial_grad(core, hidden_in, got, key_grad, got_key)
-    wide = exchange(wide.reshape(4, 64, 16, WIDE), X)
-    left = exchange(left.reshape(8, 32, 16, NARROW), "y")
-    right = exchange(right.reshape(8, 32, 16, NARROW), "z")
-    wide, left, right = (summed(v).astype(jnp.bfloat16) for v in (wide, left, right))
-    wide = exchange(wide, ("y", "z"))
-    left = exchange(left, ("xh", "z", "xl"))
-    right = exchange(right, ("y", "xh", "xl"))
-    scaled_grad = jnp.concatenate([summed(wide), summed(left), summed(right)], axis=1)
+    partial_value = partial_grad(core, hidden_in, got, key_grad, got_key)
+    near = exchange(partial_value.reshape(16, 16, 16, 512), NEAR)
+    far = exchange(summed(near).astype(jnp.bfloat16), FAR)
+    scaled_grad = summed(far)
 
     weight_grad = scaled_grad * gains
     gain_grad = jnp.sum(scaled_grad * rows, axis=1)

time: 177 us -> 112 us (0.63)
  the two profiles are of different devices: /device:TPU:1 before, /device:TPU:32 now
where the time goes in v2:
time: 112 us
  blocking collectives  57.2 us (51%)
  starting transfers between devices  21.1 us (19%)
  waiting for transfers between devices  16.2 us (14%)
  Pallas kernels  8.08 us (7%)
  other arithmetic  5.32 us (5%)
  local copies, waits for them, and re-layouts  3.13 us (3%)
    all_to_all x1, blocking collectives, exchange(): return lax.all_to_all(value, axes, split_axis=0, concat_axis=0, tiled=True)  57.2 us
    all_to_all x1, starting transfers between devices, exchange(): return lax.all_to_all(value, axes, split_axis=0, concat_axis=0, tiled=True)  14.8 us
    ppermute x1, waiting for transfers between devices, on_device(): packed = lax.ppermute(packed, ALL, pairs).astype(jnp.float32)  12.5 us
    pallas_call x1, Pallas kernels, partial_grad(): pl.pallas_call(partial_kernel, grid_spec=pltpu.PrefetchScalarGridSpec(num...  8.08 us
    reduce_sum x2, other arithmetic, summed(): return jnp.sum(value.astype(jnp.float32), axis=0)  3.94 us
    ppermute x1, waiting for transfers between devices, on_device(): got_key = lax.ppermute(key_grad, 'core', swap)  3.7 us
    unnamed x20, local copies, waits for them, and re-layouts  2.86 us
    ppermute x1, starting transfers between devices, on_device(): got_key = lax.ppermute(key_grad, 'core', swap)  2.41 us
  transfers between devices with their start and end apart: 4, of which 2 were waited for; matrix products, arithmetic and copies ran while one was open for 0% of the time, Pallas kernels for 0%

profile of v2, /device:TPU:32, one launch (start us, length us, event | category | flops | bytes accessed | tf_op | source)
XLA Modules:
  0.0 111.8 jit_solution(7758136237324399344)
XLA Ops:
  0.6 0.0 copy-start
  0.6 2.1 %collective-permute-start = (bf16[192,8192]{1,0:T(8,128)(2,1)}, bf16[192,8192]{1,0:T(8,128)(2,1)}, u32[]{:S(2)}, u32[]{:S(2)}) collective-permute-start(bf16[192,8192]{1,0:T(8,128)(2,1)} %own_ref.1), channel_id=1, source_target_pairs={{0,16},{16,0},{1,17},{17,1},{2,18},{18,2},{3,19},{19,3},{4,20},{20... | collective-permute-start | bytes 9437192 | tf_op jit(solution)/shard_map/ppermute | solution.py:110
  2.7 2.4 %collective-permute-start.1 = (bf16[192,512]{1,0:T(8,128)(2,1)}, bf16[192,512]{1,0:T(8,128)(2,1)S(1)}, u32[]{:S(2)}, u32[]{:S(2)}) collective-permute-start(bf16[192,512]{1,0:T(8,128)(2,1)} %own_key_ref.1), channel_id=1, source_target_pairs={{0,16},{16,0},{1,17},{17,1},{2,18},{18,2},{3,19},{19,3},{4,20},{20... | collective-permute-start | bytes 589832 | tf_op jit(solution)/shard_map/ppermute | solution.py:111
  5.1 3.7 %collective-permute-done.1.got_key_ref = bf16[192,512]{1,0:T(8,128)(2,1)S(1)} collective-permute-done((bf16[192,512]{1,0:T(8,128)(2,1)}, bf16[192,512]{1,0:T(8,128)(2,1)S(1)}, u32[]{:S(2)}, u32[]{:S(2)}) %collective-permute-start.1) | collective-permute-done | bytes 196640 | tf_op jit(solution)/shard_map/ppermute | solution.py:111
  8.8 0.0 collective-permute-done.got_ref
  8.8 1.9 %copy-done.1 = bf16[192,8192]{1,0:T(8,128)(2,1)S(1)} copy-done((bf16[192,8192]{1,0:T(8,128)(2,1)S(1)}, bf16[192,8192]{1,0:T(8,128)(2,1)}, u32[]{:S(2)}) %copy-start.1) | copy-done | bytes 3145752
  10.7 0.9 copy-done.2
  11.6 8.1 %shard_map.145 = bf16[2,2,2,2,4,4,16,512]{7,6,5,4,3,2,1,0:T(8,128)(2,1)S(1)} custom-call(s32[1]{0:T(128)} %bitcast.core_ref, bf16[192,8192]{1,0:T(8,128)(2,1)S(1)} %copy-done.1, bf16[192,8192]{1,0:T(8,128)(2,1)} %collective-permute-done.got_ref, bf16[192,512]{1,0:T(8,128)(2,1)S(1)} %copy-done.2, bf16[192,512]{1,0:T(8,128)(2,1)S(1)} %collective-permute-done.1.got_key_ref), custom_call_target="tpu_custom_call" | custom-call | flops 1610612736 | bytes 11534336 | tf_op jit(solution)/shard_map/pallas_call | solution.py:70
  19.7 57.2 %all_to_all.10 = bf16[16,16,16,512]{3,2,1,0:T(8,128)(2,1)} all-to-all(bf16[16,16,16,512]{3,2,1,0:T(8,128)(2,1)S(1)} %bitcast.2), channel_id=1, replica_groups=mesh['yh'=4,'yl'=2,'xh'=2,'core'=2,'zh'=4,'zl'=2,'xl'=2] {'yl','xh','zl'..., dimensions={0} | all-to-all | bytes 8388608 | tf_op jit(solution)/shard_map/all_to_all | solution.py:90
  77.0 0.0 copy-start.6
  77.0 0.0 copy-start.7
  77.0 0.0 copy-start.8
  77.0 3.9 %reduce_sum.30 = bf16[16,16,512]{2,1,0:T(8,128)(2,1)} reduce(bf16[16,16,16,512]{3,2,1,0:T(8,128)(2,1)} %all_to_all.10, bf16[]{:T(256)} %constant.25.clone.1), dimensions={0}, to_apply=%region_0.0 | reduce | flops 1966080 | bytes 4456450 | tf_op jit(solution)/shard_map/reduce_sum | solution.py:94
  80.9 14.8 %all-to-all-start.1 = ((bf16[16,16,512]{2,1,0:T(8,128)(2,1)}), bf16[16,16,512]{2,1,0:T(8,128)(2,1)S(1)}, u32[]{:S(2)}, u32[]{:S(2)}) async-start(bf16[16,16,512]{2,1,0:T(8,128)(2,1)} %reduce_sum.30), calls=%async_computation.1 | async-start | bytes 524288 | tf_op jit(solution)/shard_map/all_to_all | solution.py:90
  95.7 0.0 copy-done.9
  95.7 0.1 dynamic_slice.7
  95.8 0.1 broadcast_in_dim.2
  95.9 1.9 %collective-permute-start.2 = (bf16[16,640]{1,0:T(8,128)(2,1)S(1)}, bf16[16,640]{1,0:T(8,128)(2,1)S(1)}, u32[]{:S(2)}, u32[]{:S(2)}) collective-permute-start(bf16[16,640]{1,0:T(8,128)(2,1)S(1)} %pad_maximum_fusion), channel_id=1, source_target_pairs={{0,0},{1,32},{2,64},{3,96},{4,128},{5,160},{6,192},{7,224},{8,256}... | collective-permute-start | bytes 61448 | tf_op jit(solution)/shard_map/ppermute | solution.py:120
  97.8 12.5 %collective-permute-done.2 = bf16[16,640]{1,0:T(8,128)(2,1)S(1)} collective-permute-done((bf16[16,640]{1,0:T(8,128)(2,1)S(1)}, bf16[16,640]{1,0:T(8,128)(2,1)S(1)}, u32[]{:S(2)}, u32[]{:S(2)}) %collective-permute-start.2) | collective-permute-done | bytes 20512 | tf_op jit(solution)/shard_map/ppermute | solution.py:120
  110.2 0.1 slice_reduce_fusion
  110.4 0.0 all-to-all-done.1
  110.4 0.8 multiply_subtract_fusion
  111.3 0.0 copy-done.6
  111.3 0.5 multiply_subtract_fusion.1
  (16 shorter events, 0.1 us)
Async XLA Ops:
  0.6 95.1 %copy-start = (bf16[512,512]{1,0:T(8,128)(2,1)S(1)}, bf16[512,512]{1,0:T(8,128)(2,1)}, u32[]{:S(2)}) copy-start(bf16[512,512]{1,0:T(8,128)(2,1)} %param.13) | copy-start | bytes 1572868
  0.6 8.2 %collective-permute-start = (bf16[192,8192]{1,0:T(8,128)(2,1)}, bf16[192,8192]{1,0:T(8,128)(2,1)}, u32[]{:S(2)}, u32[]{:S(2)}) collective-permute-start(bf16[192,8192]{1,0:T(8,128)(2,1)} %own_ref.1), channel_id=1, source_target_pairs={{0,16},{16,0},{1,17},{17,1},{2,18},{18,2},{3,19},{19,3},{4,20},{20... | collective-permute-start | bytes 9437192 | tf_op jit(solution)/shard_map/ppermute | solution.py:110
  2.7 6.1 %collective-permute-start.1 = (bf16[192,512]{1,0:T(8,128)(2,1)}, bf16[192,512]{1,0:T(8,128)(2,1)S(1)}, u32[]{:S(2)}, u32[]{:S(2)}) collective-permute-start(bf16[192,512]{1,0:T(8,128)(2,1)} %own_key_ref.1), channel_id=1, source_target_pairs={{0,16},{16,0},{1,17},{17,1},{2,18},{18,2},{3,19},{19,3},{4,20},{20... | collective-permute-start | bytes 589832 | tf_op jit(solution)/shard_map/ppermute | solution.py:111
  8.8 1.9 %copy-start.1 = (bf16[192,8192]{1,0:T(8,128)(2,1)S(1)}, bf16[192,8192]{1,0:T(8,128)(2,1)}, u32[]{:S(2)}) copy-start(bf16[192,8192]{1,0:T(8,128)(2,1)} %own_ref.1) | copy-start | bytes 9437188
  10.7 0.9 copy-start.2
  77.0 18.7 %copy-start.9 = (bf16[512]{0:T(512)(128)(2,1)S(1)}, bf16[512]{0:T(512)(128)(2,1)}, u32[]{:S(2)}) copy-start(bf16[512]{0:T(512)(128)(2,1)} %param.12) | copy-start | bytes 3076
  77.0 33.4 %copy-start.3 = (f32[16,512]{1,0:T(8,128)S(1)}, f32[16,512]{1,0:T(8,128)}, u32[]{:S(2)}) copy-start(f32[16,512]{1,0:T(8,128)} %param.14) | copy-start | bytes 98308
  77.0 33.4 %copy-start.4 = (f32[16,512]{1,0:T(8,128)S(1)}, f32[16,512]{1,0:T(8,128)}, u32[]{:S(2)}) copy-start(f32[16,512]{1,0:T(8,128)} %param.15) | copy-start | bytes 98308
  77.0 33.4 %copy-start.5 = (f32[16,512]{1,0:T(8,128)S(1)}, f32[16,512]{1,0:T(8,128)}, u32[]{:S(2)}) copy-start(f32[16,512]{1,0:T(8,128)} %param.16) | copy-start | bytes 98308
  77.0 34.3 %copy-start.6 = (f32[16]{0:T(128)S(1)}, f32[16]{0:T(128)}, u32[]{:S(2)}) copy-start(f32[16]{0:T(128)} %param.17) | copy-start | bytes 196
  77.0 34.3 %copy-start.7 = (f32[16]{0:T(128)S(1)}, f32[16]{0:T(128)}, u32[]{:S(2)}) copy-start(f32[16]{0:T(128)} %param.18) | copy-start | bytes 196
  77.0 34.3 %copy-start.8 = (f32[16]{0:T(128)S(1)}, f32[16]{0:T(128)}, u32[]{:S(2)}) copy-start(f32[16]{0:T(128)} %param.19) | copy-start | bytes 196
  80.9 29.4 %all-to-all-start.1 = ((bf16[16,16,512]{2,1,0:T(8,128)(2,1)}), bf16[16,16,512]{2,1,0:T(8,128)(2,1)S(1)}, u32[]{:S(2)}, u32[]{:S(2)}) async-start(bf16[16,16,512]{2,1,0:T(8,128)(2,1)} %reduce_sum.30), calls=%async_computation.1 | async-start | bytes 524288 | tf_op jit(solution)/shard_map/all_to_all | solution.py:90
  95.9 14.4 %collective-permute-start.2 = (bf16[16,640]{1,0:T(8,128)(2,1)S(1)}, bf16[16,640]{1,0:T(8,128)(2,1)S(1)}, u32[]{:S(2)}, u32[]{:S(2)}) collective-permute-start(bf16[16,640]{1,0:T(8,128)(2,1)S(1)} %pad_maximum_fusion), channel_id=1, source_target_pairs={{0,0},{1,32},{2,64},{3,96},{4,128},{5,160},{6,192},{7,224},{8,256}... | collective-permute-start | bytes 61448 | tf_op jit(solution)/shard_map/ppermute | solution.py:120

commit v3 on v2

--- a/solution.py
+++ b/solution.py
@@ -17,7 +17,25 @@
 SIZES = (4, 2, 2, 2, 4, 2, 2)
 ALL = ("yh", "yl", "xh", "core", "zh", "zl", "xl")
 NODE, GROUP = ALL[:4], ALL[4:]
-NEAR, FAR = ("yl", "xh", "zl", "xl"), ("yh", "zh")
+FAR = ("yh", "xh", "zh")
+
+
+def near_groups():
+    groups = []
+    for core in range(2):
+        for ky in range(core, 8, 2):
+            for kx in range(core, 4, 2):
+                for kz in range(core, 8, 2):
+                    members = []
+                    for yl in range(2):
+                        for xl in range(2):
+                            for zl in range(2):
+                                y = (ky + (yl != core)) % 8
+                                x = (kx + (xl != core)) % 4
+                                z = (kz + (zl != core)) % 8
+                                members.append((((y * 2 + x // 2) * 2 + core) * 8 + z) * 2 + x % 2)
+                    groups.append(members)
+    return groups
 
 
 def adam_update(weights, moment_one, moment_two, gradient):
@@ -62,7 +80,7 @@
         rounded = total.astype(jnp.bfloat16).reshape(4, 2, 2, 16, 512)
         for zl in range(2):
             for xl in range(2):
-                out_ref[0, xh, zl, xl, 0] = rounded[:, zl, xl]
+                out_ref[0, xl, zl, 0, xh] = rounded[:, zl, xl]
 
 
 def partial_grad(core, own, got, own_key, got_key):
@@ -74,11 +92,11 @@
             grid=(8,),
             in_specs=[whole(own.shape), whole(got.shape), whole(own_key.shape), whole(got_key.shape)],
             out_specs=pl.BlockSpec(
-                (1, 2, 2, 2, 1, 4, 16, 512), lambda i, c: (i % 2, 0, 0, 0, i // 2, 0, 0, 0)
+                (1, 2, 2, 1, 2, 4, 16, 512), lambda i, c: (i % 2, 0, 0, i // 2, 0, 0, 0, 0)
             ),
             scratch_shapes=[pltpu.VMEM((2 * own.shape[0], own_key.shape[1]), jnp.bfloat16)],
         ),
-        out_shape=jax.ShapeDtypeStruct((2, 2, 2, 2, 4, 4, 16, 512), jnp.bfloat16),
+        out_shape=jax.ShapeDtypeStruct((2, 2, 2, 4, 2, 4, 16, 512), jnp.bfloat16),
         compiler_params=pltpu.CompilerParams(vmem_limit_bytes=40 * 1024 * 1024),
         cost_estimate=pl.CostEstimate(
             flops=2 * 384 * 4096 * 512, bytes_accessed=11 * 1024 * 1024, transcendentals=0
@@ -86,8 +104,10 @@
     )(core, own, got, own_key, got_key)
 
 
-def exchange(value, axes):
-    return lax.all_to_all(value, axes, split_axis=0, concat_axis=0, tiled=True)
+def exchange(value, axes, groups=None):
+    return lax.all_to_all(
+        value, axes, split_axis=0, concat_axis=0, axis_index_groups=groups, tiled=True
+    )
 
 
 def summed(value):
@@ -122,7 +142,7 @@
 
     core = lax.axis_index("core").astype(jnp.int32).reshape(1)
     partial_value = partial_grad(core, hidden_in, got, key_grad, got_key)
-    near = exchange(partial_value.reshape(16, 16, 16, 512), NEAR)
+    near = exchange(partial_value.reshape(8, 32, 16, 512), ALL, near_groups())
     far = exchange(summed(near).astype(jnp.bfloat16), FAR)
     scaled_grad = summed(far)
 

time: 112 us -> 99.3 us (0.89)
  the two profiles are of different devices: /device:TPU:32 before, /device:TPU:1 now
where the time goes in v3:
time: 99.3 us; the launch traced here: 98.8 us
  blocking collectives  39.8 us (40%)
  waiting for transfers between devices  23.5 us (24%)
  starting transfers between devices  17.9 us (18%)
  Pallas kernels  8.25 us (8%)
  other arithmetic  5.48 us (6%)
  local copies, waits for them, and re-layouts  3.13 us (3%)
    all_to_all x1, blocking collectives, exchange(): lax.all_to_all(value, axes, split_axis=0, concat_axis=0, axis_index_group...  39.8 us
    ppermute x1, waiting for transfers between devices, on_device(): packed = lax.ppermute(packed, ALL, pairs).astype(jnp.float32)  13.8 us
    ppermute x1, starting transfers between devices, on_device(): got = lax.ppermute(hidden_in, 'core', swap)  8.92 us
    pallas_call x1, Pallas kernels, partial_grad(): pl.pallas_call(partial_kernel, grid_spec=pltpu.PrefetchScalarGridSpec(num...  8.25 us
    all_to_all x1, waiting for transfers between devices, exchange(): lax.all_to_all(value, axes, split_axis=0, concat_axis=0, axis_index_group...  5.83 us
    all_to_all x1, starting transfers between devices, exchange(): lax.all_to_all(value, axes, split_axis=0, concat_axis=0, axis_index_group...  5.16 us
    reduce_sum x2, other arithmetic, summed(): return jnp.sum(value.astype(jnp.float32), axis=0)  4.1 us
    ppermute x1, waiting for transfers between devices, on_device(): got_key = lax.ppermute(key_grad, 'core', swap)  3.82 us
  transfers between devices with their start and end apart: 4, of which 3 were waited for; matrix products, arithmetic and copies ran while one was open for 0% of the time, Pallas kernels for 0%

profile of v3, /device:TPU:1, one launch (start us, length us, event | category | flops | bytes accessed | tf_op | source)
XLA Modules:
  0.0 98.8 jit_solution(7474834889100657805)
XLA Ops:
  0.6 0.0 copy-start
  0.6 8.9 %collective-permute-start = (bf16[192,8192]{1,0:T(8,128)(2,1)}, bf16[192,8192]{1,0:T(8,128)(2,1)}, u32[]{:S(2)}, u32[]{:S(2)}) collective-permute-start(bf16[192,8192]{1,0:T(8,128)(2,1)} %own_ref.1), channel_id=1, source_target_pairs={{0,16},{16,0},{1,17},{17,1},{2,18},{18,2},{3,19},{19,3},{4,20},{20... | collective-permute-start | bytes 9437192 | tf_op jit(solution)/shard_map/ppermute | solution.py:130
  9.6 1.9 %collective-permute-start.1 = (bf16[192,512]{1,0:T(8,128)(2,1)}, bf16[192,512]{1,0:T(8,128)(2,1)S(1)}, u32[]{:S(2)}, u32[]{:S(2)}) collective-permute-start(bf16[192,512]{1,0:T(8,128)(2,1)} %own_key_ref.1), channel_id=1, source_target_pairs={{0,16},{16,0},{1,17},{17,1},{2,18},{18,2},{3,19},{19,3},{4,20},{20... | collective-permute-start | bytes 589832 | tf_op jit(solution)/shard_map/ppermute | solution.py:131
  11.5 3.8 %collective-permute-done.1.got_key_ref = bf16[192,512]{1,0:T(8,128)(2,1)S(1)} collective-permute-done((bf16[192,512]{1,0:T(8,128)(2,1)}, bf16[192,512]{1,0:T(8,128)(2,1)S(1)}, u32[]{:S(2)}, u32[]{:S(2)}) %collective-permute-start.1) | collective-permute-done | bytes 196640 | tf_op jit(solution)/shard_map/ppermute | solution.py:131
  15.3 0.0 collective-permute-done.got_ref
  15.3 1.9 %copy-done.1 = bf16[192,8192]{1,0:T(8,128)(2,1)S(1)} copy-done((bf16[192,8192]{1,0:T(8,128)(2,1)S(1)}, bf16[192,8192]{1,0:T(8,128)(2,1)}, u32[]{:S(2)}) %copy-start.1) | copy-done | bytes 3145752
  17.2 0.9 copy-done.2
  18.2 8.3 %shard_map.145 = bf16[2,2,2,4,2,4,16,512]{7,6,5,4,3,2,1,0:T(8,128)(2,1)S(1)} custom-call(s32[1]{0:T(128)} %bitcast.core_ref, bf16[192,8192]{1,0:T(8,128)(2,1)S(1)} %copy-done.1, bf16[192,8192]{1,0:T(8,128)(2,1)} %collective-permute-done.got_ref, bf16[192,512]{1,0:T(8,128)(2,1)S(1)} %copy-done.2, bf16[192,512]{1,0:T(8,128)(2,1)S(1)} %collective-permute-done.1.got_key_ref), custom_call_target="tpu_custom_call" | custom-call | flops 1610612736 | bytes 11534336 | tf_op jit(solution)/shard_map/pallas_call | solution.py:88
  26.4 39.8 %all_to_all.10 = bf16[8,32,16,512]{3,2,1,0:T(8,128)(2,1)} all-to-all(bf16[8,32,16,512]{3,2,1,0:T(8,128)(2,1)S(1)} %bitcast.2), channel_id=1, replica_groups={{0,2,1,3,64,66,65,67},{4,6,5,7,68,70,69,71},{8,10,9,11,72,74,73,75},{12..., dimensions={0} | all-to-all | bytes 8388608 | tf_op jit(solution)/shard_map/all_to_all | solution.py:108
  66.2 0.0 copy-start.6
  66.3 0.0 copy-start.7
  66.3 0.0 copy-start.8
  66.3 4.0 %reduce_sum.30 = bf16[32,16,512]{2,1,0:T(8,128)(2,1)} reduce(bf16[8,32,16,512]{3,2,1,0:T(8,128)(2,1)} %all_to_all.10, bf16[]{:T(256)} %constant.25.clone.1), dimensions={0}, to_apply=%region_0.0 | reduce | flops 1835008 | bytes 4718594 | tf_op jit(solution)/shard_map/reduce_sum | solution.py:114
  70.3 5.2 %all-to-all-start.1 = ((bf16[32,16,512]{2,1,0:T(8,128)(2,1)}), bf16[32,16,512]{2,1,0:T(8,128)(2,1)S(1)}, u32[]{:S(2)}, u32[]{:S(2)}) async-start(bf16[32,16,512]{2,1,0:T(8,128)(2,1)} %reduce_sum.30), calls=%async_computation.1 | async-start | bytes 1048576 | tf_op jit(solution)/shard_map/all_to_all | solution.py:108
  75.5 0.1 dynamic_slice.7
  75.6 0.1 broadcast_in_dim.2
  75.6 1.9 %collective-permute-start.2 = (bf16[16,640]{1,0:T(8,128)(2,1)S(1)}, bf16[16,640]{1,0:T(8,128)(2,1)S(1)}, u32[]{:S(2)}, u32[]{:S(2)}) collective-permute-start(bf16[16,640]{1,0:T(8,128)(2,1)S(1)} %pad_maximum_fusion), channel_id=1, source_target_pairs={{0,0},{1,32},{2,64},{3,96},{4,128},{5,160},{6,192},{7,224},{8,256}... | collective-permute-start | bytes 61448 | tf_op jit(solution)/shard_map/ppermute | solution.py:140
  77.6 13.8 %collective-permute-done.2 = bf16[16,640]{1,0:T(8,128)(2,1)S(1)} collective-permute-done((bf16[16,640]{1,0:T(8,128)(2,1)S(1)}, bf16[16,640]{1,0:T(8,128)(2,1)S(1)}, u32[]{:S(2)}, u32[]{:S(2)}) %collective-permute-start.2) | collective-permute-done | bytes 20512 | tf_op jit(solution)/shard_map/ppermute | solution.py:140
  91.4 0.1 slice_reduce_fusion
  91.5 5.8 %all-to-all-done.1 = bf16[32,16,512]{2,1,0:T(8,128)(2,1)S(1)} async-done(((bf16[32,16,512]{2,1,0:T(8,128)(2,1)}), bf16[32,16,512]{2,1,0:T(8,128)(2,1)S(1)}, u32[]{:S(2)}, u32[]{:S(2)}) %all-to-all-start.1) | async-done | bytes 524320 | tf_op jit(solution)/shard_map/all_to_all | solution.py:108
  97.3 0.1 convert_reduce_fusion
  97.4 0.0 copy-done.4
  97.5 0.8 multiply_subtract_fusion
  98.3 0.5 multiply_subtract_fusion.1
  (16 shorter events, 0.0 us)
Async XLA Ops:
  0.6 74.9 %copy-start = (bf16[512,512]{1,0:T(8,128)(2,1)S(1)}, bf16[512,512]{1,0:T(8,128)(2,1)}, u32[]{:S(2)}) copy-start(bf16[512,512]{1,0:T(8,128)(2,1)} %param.13) | copy-start | bytes 1572868
  0.6 14.7 %collective-permute-start = (bf16[192,8192]{1,0:T(8,128)(2,1)}, bf16[192,8192]{1,0:T(8,128)(2,1)}, u32[]{:S(2)}, u32[]{:S(2)}) collective-permute-start(bf16[192,8192]{1,0:T(8,128)(2,1)} %own_ref.1), channel_id=1, source_target_pairs={{0,16},{16,0},{1,17},{17,1},{2,18},{18,2},{3,19},{19,3},{4,20},{20... | collective-permute-start | bytes 9437192 | tf_op jit(solution)/shard_map/ppermute | solution.py:130
  9.6 5.8 %collective-permute-start.1 = (bf16[192,512]{1,0:T(8,128)(2,1)}, bf16[192,512]{1,0:T(8,128)(2,1)S(1)}, u32[]{:S(2)}, u32[]{:S(2)}) collective-permute-start(bf16[192,512]{1,0:T(8,128)(2,1)} %own_key_ref.1), channel_id=1, source_target_pairs={{0,16},{16,0},{1,17},{17,1},{2,18},{18,2},{3,19},{19,3},{4,20},{20... | collective-permute-start | bytes 589832 | tf_op jit(solution)/shard_map/ppermute | solution.py:131
  15.3 1.9 %copy-start.1 = (bf16[192,8192]{1,0:T(8,128)(2,1)S(1)}, bf16[192,8192]{1,0:T(8,128)(2,1)}, u32[]{:S(2)}) copy-start(bf16[192,8192]{1,0:T(8,128)(2,1)} %own_ref.1) | copy-start | bytes 9437188
  17.2 0.9 copy-start.2
  66.2 9.2 %copy-start.9 = (bf16[512]{0:T(512)(128)(2,1)S(1)}, bf16[512]{0:T(512)(128)(2,1)}, u32[]{:S(2)}) copy-start(bf16[512]{0:T(512)(128)(2,1)} %param.12) | copy-start | bytes 3076
  66.2 31.2 %copy-start.3 = (f32[16,512]{1,0:T(8,128)S(1)}, f32[16,512]{1,0:T(8,128)}, u32[]{:S(2)}) copy-start(f32[16,512]{1,0:T(8,128)} %param.14) | copy-start | bytes 98308
  66.2 31.2 %copy-start.4 = (f32[16,512]{1,0:T(8,128)S(1)}, f32[16,512]{1,0:T(8,128)}, u32[]{:S(2)}) copy-start(f32[16,512]{1,0:T(8,128)} %param.15) | copy-start | bytes 98308
  66.2 31.2 %copy-start.5 = (f32[16,512]{1,0:T(8,128)S(1)}, f32[16,512]{1,0:T(8,128)}, u32[]{:S(2)}) copy-start(f32[16,512]{1,0:T(8,128)} %param.16) | copy-start | bytes 98308
  66.2 32.0 %copy-start.6 = (f32[16]{0:T(128)S(1)}, f32[16]{0:T(128)}, u32[]{:S(2)}) copy-start(f32[16]{0:T(128)} %param.17) | copy-start | bytes 196
  66.3 32.0 %copy-start.7 = (f32[16]{0:T(128)S(1)}, f32[16]{0:T(128)}, u32[]{:S(2)}) copy-start(f32[16]{0:T(128)} %param.18) | copy-start | bytes 196
  66.3 32.0 %copy-start.8 = (f32[16]{0:T(128)S(1)}, f32[16]{0:T(128)}, u32[]{:S(2)}) copy-start(f32[16]{0:T(128)} %param.19) | copy-start | bytes 196
  70.3 27.0 %all-to-all-start.1 = ((bf16[32,16,512]{2,1,0:T(8,128)(2,1)}), bf16[32,16,512]{2,1,0:T(8,128)(2,1)S(1)}, u32[]{:S(2)}, u32[]{:S(2)}) async-start(bf16[32,16,512]{2,1,0:T(8,128)(2,1)} %reduce_sum.30), calls=%async_computation.1 | async-start | bytes 1048576 | tf_op jit(solution)/shard_map/all_to_all | solution.py:108
  75.6 15.7 %collective-permute-start.2 = (bf16[16,640]{1,0:T(8,128)(2,1)S(1)}, bf16[16,640]{1,0:T(8,128)(2,1)S(1)}, u32[]{:S(2)}, u32[]{:S(2)}) collective-permute-start(bf16[16,640]{1,0:T(8,128)(2,1)S(1)} %pad_maximum_fusion), channel_id=1, source_target_pairs={{0,0},{1,32},{2,64},{3,96},{4,128},{5,160},{6,192},{7,224},{8,256}... | collective-permute-start | bytes 61448 | tf_op jit(solution)/shard_map/ppermute | solution.py:140

commit v4 on v3

v4 whole, which is shorter than its diff:
```python
import jax
import jax.numpy as jnp
from jax import lax
from jax.experimental import pallas as pl
from jax.experimental.pallas import tpu as pltpu
from jax.sharding import Mesh, PartitionSpec as P

norm_eps = 1e-05
beta_one = 0.9
beta_two = 0.999
adam_eps = 1e-08
learn_rate = 0.0003
weight_decay = 0.1
bias_one = 1.0 - 2.6561398887587544e-05
bias_two = 1.0 - 0.9047921471137096

SIZES = (4, 2, 2, 2, 4, 2, 2)
ALL = ("yh", "yl", "xh", "core", "zh", "zl", "xl")
NODE, GROUP = ALL[:4], ALL[4:]
FAR = ("yh", "xh", "zh")


def near_groups():
    groups = []
    for core in range(2):
        for ky in range(core, 8, 2):
            for kx in range(core, 4, 2):
                for kz in range(core, 8, 2):
                    members = []
                    for yl in range(2):
                        for xl in range(2):
                            for zl in range(2):
                                y = (ky + (yl != core)) % 8
                                x = (kx + (xl != core)) % 4
                                z = (kz + (zl != core)) % 8
                                members.append((((y * 2 + x // 2) * 2 + core) * 8 + z) * 2 + x % 2)
                    groups.append(members)
    return groups


def adam_update(weights, moment_one, moment_two, gradient):
    moment_new = beta_one * moment_one + (1.0 - beta_one) * gradient
    square_new = beta_two * moment_two + (1.0 - beta_two) * gradient * gradient
    direction = moment_new / bias_one / (jnp.sqrt(square_new / bias_two) + adam_eps)
    return (weights - learn_rate * (direction + weight_decay * weights), moment_new, square_new)


PIECES = 4


def square_sums(ref, first, count, total):
    def add(i, total):
        block = ref[:, pl.ds(pl.multiple_of(first + i * 512, 512), 512)].astype(jnp.float32)
        block = block * block
        return total + (block[:, :128] + block[:, 128:256]) + (block[:, 256:384] + block[:, 384:])

    return lax.fori_loop(0, count // 512, add, total)


def normed_key(key_ref, total, width):
    mean = jnp.sum(total, axis=1, keepdims=True) * (1.0 / width)
    return (key_ref[...].astype(jnp.float32) * lax.rsqrt(mean + norm_eps)).astype(jnp.bfloat16)


def fetch(source, target, semaphores, piece):
    width = source.shape[1] // PIECES
    columns = pl.ds(piece * width, width)
    return pltpu.make_async_copy(
        source.at[:, columns], target.at[:, columns], semaphores.at[piece]
    )


def own_kernel(core_ref, own_ref, key_ref, half_ref, scaled_ref, own, semaphores):
    tokens, width = own.shape
    for piece in range(PIECES):
        fetch(own_ref, own, semaphores, piece).start()
    total = jnp.zeros((tokens, 128), jnp.float32)
    for piece in range(PIECES):
        fetch(own_ref, own, semaphores, piece).wait()
        total = square_sums(own, piece * (width // PIECES), width // PIECES, total)
        for k in range(piece * 4, piece * 4 + 4):
            start = pl.multiple_of(k * 512 + core_ref[0] * 256, 256)
            half_ref[:, k * 256 : k * 256 + 256] = own[:, pl.ds(start, 256)]
    scaled_ref[...] = normed_key(key_ref, total, width)


def pair_kernel(
    core_ref, half_ref, scaled_ref, got_ref, key_ref, out_ref, got, keys, out, semaphores, out_sems
):
    tokens, width = got.shape
    for piece in range(PIECES):
        fetch(got_ref, got, semaphores, piece).start()
    keys[:tokens, :] = scaled_ref[...]
    total = jnp.zeros((tokens, 128), jnp.float32)
    for piece in range(PIECES):
        fetch(got_ref, got, semaphores, piece).wait()
        total = square_sums(got, piece * (width // PIECES), width // PIECES, total)
    keys[tokens:, :] = normed_key(key_ref, total, width)

    def store(yh, yl):
        return pltpu.make_async_copy(
            out.at[yl, :, :, yh], out_ref.at[yl, :, :, yh], out_sems.at[yl, yh]
        )

    def step(yh, carry):
        for yl in range(2):
            for xh in range(2):
                start = (yh * 2 + yl) * 512 + xh * 256
                other = 2 * start + core_ref[0] * 256
                rows = jnp.concatenate(
                    [
                        half_ref[:, pl.ds(pl.multiple_of(start, 256), 256)],
                        got[:, pl.ds(pl.multiple_of(other, 256), 256)],
                    ],
                    axis=0,
                )
                product = lax.dot_general(
                    rows, keys[...], (((0,), (0,)), ((), ())), preferred_element_type=jnp.float32
                )
                product = product.astype(jnp.bfloat16).reshape(4, 2, 2, 16, 512)
                for zl in range(2):
                    for xl in range(2):
                        out[yl, xl, zl, yh, xh] = product[:, zl, xl]
            store(yh, yl).start()
        return carry

    lax.fori_loop(0, 4, step, 0)
    for yh in range(4):
        for yl in range(2):
            store(yh, yl).wait()


VMEM = pl.BlockSpec(memory_space=pltpu.MemorySpace.VMEM)
SMEM = pl.BlockSpec(memory_space=pltpu.MemorySpace.SMEM)
HBM = pl.BlockSpec(memory_space=pltpu.MemorySpace.HBM)


def own_part(core, own, key):
    tokens, width = own.shape
    return pl.pallas_call(
        own_kernel,
        in_specs=[SMEM, HBM, VMEM],
        out_specs=[VMEM, VMEM],
        out_shape=[
            jax.ShapeDtypeStruct((tokens, width // 2), jnp.bfloat16),
            jax.ShapeDtypeStruct(key.shape, jnp.bfloat16),
        ],
        scratch_shapes=[pltpu.VMEM(own.shape, jnp.bfloat16), pltpu.SemaphoreType.DMA((PIECES,))],
        compiler_params=pltpu.CompilerParams(vmem_limit_bytes=12 * 1024 * 1024),
        cost_estimate=pl.CostEstimate(
            flops=4 * tokens * width, bytes_accessed=5 * 1024 * 1024, transcendentals=0
        ),
    )(core, own, key)


def pair_partial(core, half, scaled, got, key):
    tokens, width = got.shape
    proj = key.shape[1]
    shape = (2, 2, 2, 4, 2, 4, 16, proj)
    return pl.pallas_call(
        pair_kernel,
        in_specs=[SMEM, VMEM, VMEM, HBM, VMEM],
        out_specs=HBM,
        out_shape=jax.ShapeDtypeStruct(shape, jnp.bfloat16),
        scratch_shapes=[
            pltpu.VMEM(got.shape, jnp.bfloat16),
            pltpu.VMEM((2 * tokens, proj), jnp.bfloat16),
            pltpu.VMEM(shape, jnp.bfloat16),
            pltpu.SemaphoreType.DMA((PIECES,)),
            pltpu.SemaphoreType.DMA((2, 4)),
        ],
        compiler_params=pltpu.CompilerParams(vmem_limit_bytes=48 * 1024 * 1024),
        cost_estimate=pl.CostEstimate(
            flops=2 * tokens * width * proj, bytes_accessed=9 * 1024 * 1024, transcendentals=0
        ),
    )(core, half, scaled, got, key)


def sum_kernel(value_ref, out_ref):
    total = value_ref[0].astype(jnp.float32)
    for source in range(1, value_ref.shape[0]):
        total = total + value_ref[source].astype(jnp.float32)
    out_ref[...] = total.astype(jnp.bfloat16)


def near_sum(value):
    sources, blocks, rows, proj = value.shape
    return pl.pallas_call(
        sum_kernel,
        grid=(4,),
        in_specs=[pl.BlockSpec((sources, blocks // 4, rows, proj), lambda i: (0, i, 0, 0))],
        out_specs=pl.BlockSpec((blocks // 4, rows, proj), lambda i: (i, 0, 0)),
        out_shape=jax.ShapeDtypeStruct((blocks, rows, proj), jnp.bfloat16),
        compiler_params=pltpu.CompilerParams(vmem_limit_bytes=16 * 1024 * 1024),
    )(value)


def exchange(value, axes, groups=None):
    return lax.all_to_all(
        value, axes, split_axis=0, concat_axis=0, axis_index_groups=groups, tiled=True
    )


def summed(value):
    return jnp.sum(value.astype(jnp.float32), axis=0)


def on_device(
    hidden_in,
    key_grad,
    gain_second,
    weight_second,
    weight_main,
    weight_m,
    weight_v,
    gain_main,
    gain_m,
    gain_v,
):
    swap = [(0, 1), (1, 0)]
    got = lax.ppermute(hidden_in, "core", swap)
    got_key = lax.ppermute(key_grad, "core", swap)

    node = lax.axis_index(NODE)
    rows = lax.dynamic_slice_in_dim(weight_second, node * 16, 16, 0)
    gains = lax.dynamic_slice_in_dim(gain_second, node * 16, 16, 0)
    pairs = [
        (m * 16 + g, (2 * g + m // 16) * 16 + m % 16) for m in range(32) for g in range(16)
    ]
    packed = jnp.concatenate([rows, jnp.broadcast_to(gains[:, None], (16, 128))], axis=1)
    packed = lax.ppermute(packed, ALL, pairs).astype(jnp.float32)

    core = lax.axis_index("core").astype(jnp.int32).reshape(1)
    half, scaled_key = own_part(core, hidden_in, key_grad)
    partial_value = pair_partial(core, half, scaled_key, got, got_key)
    near = exchange(partial_value.reshape(8, 32, 16, 512), ALL, near_groups())
    near, packed = lax.optimization_barrier((near, packed))
    rows, gains = packed[:, :512], packed[:, 512:513]
    scaled_grad = summed(exchange(near_sum(near), FAR))

    weight_grad = scaled_grad * gains
    gain_grad = jnp.sum(scaled_grad * rows, axis=1)
    weight_new, weight_first, weight_square = adam_update(
        weight_main, weight_m, weight_v, weight_grad
    )
    gain_new, gain_first, gain_square = adam_update(gain_main, gain_m, gain_v, gain_grad)
    return (weight_new, weight_first, weight_square, gain_new, gain_first, gain_square)


def solution(mesh):
    fine = Mesh(mesh.devices.reshape(SIZES), ALL)
    placed = (
        P(ALL, None),
        P(ALL, None),
        P(GROUP),
        P(GROUP, None),
        P(ALL, None),
        P(ALL, None),
        P(ALL, None),
        P(ALL),
        P(ALL),
        P(ALL),
    )
    return jax.shard_map(
        on_device,
        mesh=fine,
        in_specs=placed,
        out_specs=(P(ALL, None),) * 3 + (P(ALL),) * 3,
        check_vma=False,
    )
```

time: 99.3 us -> 98.7 us (level)
  the two profiles are of different devices: /device:TPU:1 before, /device:TPU:10 now
where the time goes in v4:
time: 98.7 us; the launch traced here: 98.2 us
  waiting for transfers between devices  46.6 us (47%)
  starting transfers between devices  34.5 us (35%)
  Pallas kernels  11.7 us (12%)
  local copies, waits for them, and re-layouts  3.12 us (3%)
  other arithmetic  1.46 us (1%)
    all_to_all x2, starting transfers between devices, exchange(): lax.all_to_all(value, axes, split_axis=0, concat_axis=0, axis_index_group...  28 us
    all_to_all x2, waiting for transfers between devices, exchange(): lax.all_to_all(value, axes, split_axis=0, concat_axis=0, axis_index_group...  23.5 us
    ppermute x1, waiting for transfers between devices, on_device(): packed = lax.ppermute(packed, ALL, pairs).astype(jnp.float32)  23.1 us
    pallas_call x1, Pallas kernels, pair_partial(): pl.pallas_call(pair_kernel, in_specs=[SMEM, VMEM, VMEM, HBM, VMEM], out_s...  6.1 us
    pallas_call x1, Pallas kernels, near_sum(): pl.pallas_call(sum_kernel, grid=(4,), in_specs=[pl.BlockSpec((sources, bl...  4.09 us
    unnamed x20, local copies, waits for them, and re-layouts  2.86 us
    ppermute x1, starting transfers between devices, on_device(): got_key = lax.ppermute(key_grad, 'core', swap)  2.41 us
    ppermute x1, starting transfers between devices, on_device(): got = lax.ppermute(hidden_in, 'core', swap)  2.05 us
  transfers between devices with their start and end apart: 5, of which 3 were waited for; matrix products, arithmetic and copies ran while one was open for 0% of the time, Pallas kernels for 2%

profile of v4, /device:TPU:10, one launch (start us, length us, event | category | flops | bytes accessed | tf_op | source)
XLA Modules:
  0.0 98.2 jit_solution(13461056807494328451)
XLA Ops:
  0.6 0.0 copy-start
  0.6 2.1 %collective-permute-start = (bf16[192,8192]{1,0:T(8,128)(2,1)}, bf16[192,8192]{1,0:T(8,128)(2,1)}, u32[]{:S(2)}, u32[]{:S(2)}) collective-permute-start(bf16[192,8192]{1,0:T(8,128)(2,1)} %own_ref.1), channel_id=1, source_target_pairs={{0,16},{16,0},{1,17},{17,1},{2,18},{18,2},{3,19},{19,3},{4,20},{20... | collective-permute-start | bytes 9437192 | tf_op jit(solution)/shard_map/ppermute | solution.py:221
  2.7 2.4 %collective-permute-start.1 = (bf16[192,512]{1,0:T(8,128)(2,1)}, bf16[192,512]{1,0:T(8,128)(2,1)S(1)}, u32[]{:S(2)}, u32[]{:S(2)}) collective-permute-start(bf16[192,512]{1,0:T(8,128)(2,1)} %key_ref.1), channel_id=1, source_target_pairs={{0,16},{16,0},{1,17},{17,1},{2,18},{18,2},{3,19},{19,3},{4,20},{20... | collective-permute-start | bytes 589832 | tf_op jit(solution)/shard_map/ppermute | solution.py:222
  5.1 1.9 %copy-done.1 = bf16[192,8192]{1,0:T(8,128)(2,1)S(1)} copy-done((bf16[192,8192]{1,0:T(8,128)(2,1)S(1)}, bf16[192,8192]{1,0:T(8,128)(2,1)}, u32[]{:S(2)}) %copy-start.1) | copy-done | bytes 3145752
  7.0 0.9 copy-done.2
  7.9 1.5 %shard_map.145 = (bf16[192,4096]{1,0:T(8,128)(2,1)S(1)}, bf16[192,512]{1,0:T(8,128)(2,1)S(1)}) custom-call(s32[1]{0:T(128)} %bitcast.core_ref, bf16[192,8192]{1,0:T(8,128)(2,1)S(1)} %copy-done.1, bf16[192,512]{1,0:T(8,128)(2,1)S(1)} %copy-done.2), custom_call_target="tpu_custom_call" | custom-call | flops 6291456 | bytes 5242880 | tf_op jit(solution)/shard_map/pallas_call | solution.py:140
  9.5 6.1 %shard_map.146 = bf16[2,2,2,4,2,4,16,512]{7,6,5,4,3,2,1,0:T(8,128)(2,1)} custom-call(s32[1]{0:T(128)} %bitcast.core_ref, bf16[192,4096]{1,0:T(8,128)(2,1)S(1)} %get-tuple-element.10.half_ref, bf16[192,512]{1,0:T(8,128)(2,1)S(1)} %get-tuple-element.11.scaled_ref, bf16[192,8192]{1,0:T(8,128)(2,1)} %collective-permute-done.got_ref, ...), custom_call_target="tpu_custom_call" | custom-call | flops 1610612736 | bytes 9437184 | tf_op jit(solution)/shard_map/pallas_call | solution.py:160
  15.6 0.0 copy-start.9
  15.6 10.3 %all-to-all-start = ((bf16[8,32,16,512]{3,2,1,0:T(8,128)(2,1)}), bf16[8,32,16,512]{3,2,1,0:T(8,128)(2,1)}, u32[]{:S(2)}, u32[]{:S(2)}) async-start(bf16[8,32,16,512]{3,2,1,0:T(8,128)(2,1)} %bitcast.2), calls=%async_computation | async-start | bytes 8388608 | tf_op jit(solution)/shard_map/all_to_all | solution.py:199
  25.9 0.1 dynamic_slice.7
  26.0 0.1 broadcast_in_dim.2
  26.1 1.9 %collective-permute-start.2 = (bf16[16,640]{1,0:T(8,128)(2,1)S(1)}, bf16[16,640]{1,0:T(8,128)(2,1)S(1)}, u32[]{:S(2)}, u32[]{:S(2)}) collective-permute-start(bf16[16,640]{1,0:T(8,128)(2,1)S(1)} %pad_maximum_fusion), channel_id=1, source_target_pairs={{0,0},{1,32},{2,64},{3,96},{4,128},{5,160},{6,192},{7,224},{8,256}... | collective-permute-start | bytes 61448 | tf_op jit(solution)/shard_map/ppermute | solution.py:231
  28.0 23.1 %collective-permute-done.2 = bf16[16,640]{1,0:T(8,128)(2,1)S(1)} collective-permute-done((bf16[16,640]{1,0:T(8,128)(2,1)S(1)}, bf16[16,640]{1,0:T(8,128)(2,1)S(1)}, u32[]{:S(2)}, u32[]{:S(2)}) %collective-permute-start.2) | collective-permute-done | bytes 20512 | tf_op jit(solution)/shard_map/ppermute | solution.py:231
  51.1 0.0 copy-start.5
  51.1 0.0 copy-start.7
  51.2 0.0 copy-start.8
  51.2 1.4 %all-to-all-done.value_ref = bf16[8,32,16,512]{3,2,1,0:T(8,128)(2,1)} async-done(((bf16[8,32,16,512]{3,2,1,0:T(8,128)(2,1)}), bf16[8,32,16,512]{3,2,1,0:T(8,128)(2,1)}, u32[]{:S(2)}, u32[]{:S(2)}) %all-to-all-start) | async-done | bytes 4194336 | tf_op jit(solution)/shard_map/all_to_all | solution.py:199
  52.5 4.1 %shard_map.147 = bf16[32,16,512]{2,1,0:T(8,128)(2,1)} custom-call(bf16[8,32,16,512]{3,2,1,0:T(8,128)(2,1)} %all-to-all-done.value_ref), custom_call_target="tpu_custom_call" | custom-call | tf_op jit(solution)/shard_map/pallas_call | solution.py:188
  56.6 17.8 %all-to-all-start.1 = ((bf16[32,16,512]{2,1,0:T(8,128)(2,1)}), bf16[32,16,512]{2,1,0:T(8,128)(2,1)S(1)}, u32[]{:S(2)}, u32[]{:S(2)}) async-start(bf16[32,16,512]{2,1,0:T(8,128)(2,1)} %shard_map.147), calls=%async_computation.1 | async-start | bytes 1048576 | tf_op jit(solution)/shard_map/all_to_all | solution.py:199
  74.4 0.1 slice_reduce_fusion
  74.5 22.2 %all-to-all-done.1 = bf16[32,16,512]{2,1,0:T(8,128)(2,1)S(1)} async-done(((bf16[32,16,512]{2,1,0:T(8,128)(2,1)}), bf16[32,16,512]{2,1,0:T(8,128)(2,1)S(1)}, u32[]{:S(2)}, u32[]{:S(2)}) %all-to-all-start.1) | async-done | bytes 524320 | tf_op jit(solution)/shard_map/all_to_all | solution.py:199
  96.7 0.1 convert_reduce_fusion
  96.8 0.8 multiply_subtract_fusion
  97.7 0.5 multiply_subtract_fusion.1
  (18 shorter events, 0.0 us)
Async XLA Ops:
  0.6 25.3 %copy-start = (bf16[512,512]{1,0:T(8,128)(2,1)S(1)}, bf16[512,512]{1,0:T(8,128)(2,1)}, u32[]{:S(2)}) copy-start(bf16[512,512]{1,0:T(8,128)(2,1)} %param.13) | copy-start | bytes 1572868
  0.6 8.9 %collective-permute-start = (bf16[192,8192]{1,0:T(8,128)(2,1)}, bf16[192,8192]{1,0:T(8,128)(2,1)}, u32[]{:S(2)}, u32[]{:S(2)}) collective-permute-start(bf16[192,8192]{1,0:T(8,128)(2,1)} %own_ref.1), channel_id=1, source_target_pairs={{0,16},{16,0},{1,17},{17,1},{2,18},{18,2},{3,19},{19,3},{4,20},{20... | collective-permute-start | bytes 9437192 | tf_op jit(solution)/shard_map/ppermute | solution.py:221
  2.7 6.8 %collective-permute-start.1 = (bf16[192,512]{1,0:T(8,128)(2,1)}, bf16[192,512]{1,0:T(8,128)(2,1)S(1)}, u32[]{:S(2)}, u32[]{:S(2)}) collective-permute-start(bf16[192,512]{1,0:T(8,128)(2,1)} %key_ref.1), channel_id=1, source_target_pairs={{0,16},{16,0},{1,17},{17,1},{2,18},{18,2},{3,19},{19,3},{4,20},{20... | collective-permute-start | bytes 589832 | tf_op jit(solution)/shard_map/ppermute | solution.py:222
  5.1 1.9 %copy-start.1 = (bf16[192,8192]{1,0:T(8,128)(2,1)S(1)}, bf16[192,8192]{1,0:T(8,128)(2,1)}, u32[]{:S(2)}) copy-start(bf16[192,8192]{1,0:T(8,128)(2,1)} %own_ref.1) | copy-start | bytes 9437188
  7.0 0.9 copy-start.2
  15.6 10.3 %copy-start.9 = (bf16[512]{0:T(512)(128)(2,1)S(1)}, bf16[512]{0:T(512)(128)(2,1)}, u32[]{:S(2)}) copy-start(bf16[512]{0:T(512)(128)(2,1)} %param.12) | copy-start | bytes 3076
  15.6 36.9 %all-to-all-start = ((bf16[8,32,16,512]{3,2,1,0:T(8,128)(2,1)}), bf16[8,32,16,512]{3,2,1,0:T(8,128)(2,1)}, u32[]{:S(2)}, u32[]{:S(2)}) async-start(bf16[8,32,16,512]{3,2,1,0:T(8,128)(2,1)} %bitcast.2), calls=%async_computation | async-start | bytes 8388608 | tf_op jit(solution)/shard_map/all_to_all | solution.py:199
  26.1 25.0 %collective-permute-start.2 = (bf16[16,640]{1,0:T(8,128)(2,1)S(1)}, bf16[16,640]{1,0:T(8,128)(2,1)S(1)}, u32[]{:S(2)}, u32[]{:S(2)}) collective-permute-start(bf16[16,640]{1,0:T(8,128)(2,1)S(1)} %pad_maximum_fusion), channel_id=1, source_target_pairs={{0,0},{1,32},{2,64},{3,96},{4,128},{5,160},{6,192},{7,224},{8,256}... | collective-permute-start | bytes 61448 | tf_op jit(solution)/shard_map/ppermute | solution.py:231
  51.1 45.7 %copy-start.3 = (f32[16,512]{1,0:T(8,128)S(1)}, f32[16,512]{1,0:T(8,128)}, u32[]{:S(2)}) copy-start(f32[16,512]{1,0:T(8,128)} %param.14) | copy-start | bytes 98308
  51.1 45.7 %copy-start.4 = (f32[16,512]{1,0:T(8,128)S(1)}, f32[16,512]{1,0:T(8,128)}, u32[]{:S(2)}) copy-start(f32[16,512]{1,0:T(8,128)} %param.15) | copy-start | bytes 98308
  51.1 45.7 %copy-start.5 = (f32[16,512]{1,0:T(8,128)S(1)}, f32[16,512]{1,0:T(8,128)}, u32[]{:S(2)}) copy-start(f32[16,512]{1,0:T(8,128)} %param.16) | copy-start | bytes 98308
  51.1 46.5 %copy-start.6 = (f32[16]{0:T(128)S(1)}, f32[16]{0:T(128)}, u32[]{:S(2)}) copy-start(f32[16]{0:T(128)} %param.17) | copy-start | bytes 196
  51.1 46.5 %copy-start.7 = (f32[16]{0:T(128)S(1)}, f32[16]{0:T(128)}, u32[]{:S(2)}) copy-start(f32[16]{0:T(128)} %param.18) | copy-start | bytes 196
  51.2 46.5 %copy-start.8 = (f32[16]{0:T(128)S(1)}, f32[16]{0:T(128)}, u32[]{:S(2)}) copy-start(f32[16]{0:T(128)} %param.19) | copy-start | bytes 196
  56.6 40.1 %all-to-all-start.1 = ((bf16[32,16,512]{2,1,0:T(8,128)(2,1)}), bf16[32,16,512]{2,1,0:T(8,128)(2,1)S(1)}, u32[]{:S(2)}, u32[]{:S(2)}) async-start(bf16[32,16,512]{2,1,0:T(8,128)(2,1)} %shard_map.147), calls=%async_computation.1 | async-start | bytes 1048576 | tf_op jit(solution)/shard_map/all_to_all | solution.py:199

commit v5 on v4

v5 whole, which is shorter than its diff:
```python
import jax
import jax.numpy as jnp
from jax import lax
from jax.experimental import pallas as pl
from jax.experimental.pallas import tpu as pltpu
from jax.sharding import Mesh, PartitionSpec as P

norm_eps = 1e-05
beta_one = 0.9
beta_two = 0.999
adam_eps = 1e-08
learn_rate = 0.0003
weight_decay = 0.1
bias_one = 1.0 - 2.6561398887587544e-05
bias_two = 1.0 - 0.9047921471137096

SIZES = (4, 2, 2, 2, 4, 2, 2)
ALL = ("yh", "yl", "xh", "core", "zh", "zl", "xl")
NODE, GROUP = ALL[:4], ALL[4:]
FAR = ("yh", "xh", "zh")


def near_groups():
    groups = []
    for core in range(2):
        for ky in range(core, 8, 2):
            for kx in range(core, 4, 2):
                for kz in range(core, 8, 2):
                    members = []
                    for yl in range(2):
                        for xl in range(2):
                            for zl in range(2):
                                y = (ky + (yl != core)) % 8
                                x = (kx + (xl != core)) % 4
                                z = (kz + (zl != core)) % 8
                                members.append((((y * 2 + x // 2) * 2 + core) * 8 + z) * 2 + x % 2)
                    groups.append(members)
    return groups


def adam_update(weights, moment_one, moment_two, gradient):
    moment_new = beta_one * moment_one + (1.0 - beta_one) * gradient
    square_new = beta_two * moment_two + (1.0 - beta_two) * gradient * gradient
    direction = moment_new / bias_one / (jnp.sqrt(square_new / bias_two) + adam_eps)
    return (weights - learn_rate * (direction + weight_decay * weights), moment_new, square_new)


PIECES = 4


def own_kernel(
    core_ref,
    own_ref,
    key_ref,
    send_ref,
    kept_ref,
    scaled_ref,
    own,
    key,
    send,
    own_sems,
    send_sems,
):
    tokens, width = own.shape
    kept = width // 2
    part = width // PIECES

    def fetch(piece):
        columns = pl.ds(piece * part, part)
        return pltpu.make_async_copy(
            own_ref.at[:, columns], own.at[:, columns], own_sems.at[piece]
        )

    def store(piece):
        start = piece * (part // 2)
        columns = pl.ds(start, part // 2 if piece < PIECES else send.shape[1] - start)
        return pltpu.make_async_copy(
            send.at[:, columns], send_ref.at[:, columns], send_sems.at[piece]
        )

    fetch_key = pltpu.make_async_copy(key_ref, key, own_sems.at[PIECES])
    for piece in range(PIECES):
        fetch(piece).start()
    fetch_key.start()
    total = jnp.zeros((tokens, 128), jnp.float32)
    for piece in range(PIECES):
        fetch(piece).wait()

        def add(i, total):
            block = own[:, pl.ds(pl.multiple_of(piece * part + i * 512, 512), 512)]
            block = block.astype(jnp.float32)
            block = block * block
            return (
                total
                + (block[:, :128] + block[:, 128:256])
                + (block[:, 256:384] + block[:, 384:])
            )

        total = lax.fori_loop(0, part // 512, add, total)
        for k in range(piece * part // 512, (piece + 1) * part // 512):
            columns = slice(k * 256, k * 256 + 256)
            start = pl.multiple_of(k * 512 + (1 - core_ref[0]) * 256, 256)
            send[:, columns] = own[:, pl.ds(start, 256)]
            start = pl.multiple_of(k * 512 + core_ref[0] * 256, 256)
            kept_ref[:, columns] = own[:, pl.ds(start, 256)]
        store(piece).start()
    mean = jnp.sum(total, axis=1, keepdims=True) * (1.0 / width)
    fetch_key.wait()
    scaled = key[...].astype(jnp.float32) * lax.rsqrt(mean + norm_eps)
    scaled_ref[...] = scaled.astype(jnp.bfloat16)
    send[:, kept:] = scaled_ref[...]
    store(PIECES).start()
    for piece in range(PIECES + 1):
        store(piece).wait()


def pair_kernel(kept_ref, scaled_ref, got_ref, out_ref, keys, out, out_sems):
    tokens, kept = kept_ref.shape

    def store(yh, yl):
        return pltpu.make_async_copy(
            out.at[yl, :, :, yh], out_ref.at[yl, :, :, yh], out_sems.at[yl, yh]
        )

    keys[:tokens, :] = scaled_ref[...]
    keys[tokens:, :] = got_ref[:, kept:]

    def step(yh, carry):
        for yl in range(2):
            for xh in range(2):
                start = pl.multiple_of((yh * 2 + yl) * 512 + xh * 256, 256)
                columns = pl.ds(start, 256)
                product = lax.dot_general(
                    jnp.concatenate([kept_ref[:, columns], got_ref[:, columns]], axis=0),
                    keys[...],
                    (((0,), (0,)), ((), ())),
                    preferred_element_type=jnp.float32,
                )
                product = product.astype(jnp.bfloat16).reshape(4, 2, 2, 16, 512)
                for zl in range(2):
                    for xl in range(2):
                        out[yl, xl, zl, yh, xh] = product[:, zl, xl]
            store(yh, yl).start()
        return carry

    lax.fori_loop(0, 4, step, 0)
    for yh in range(4):
        for yl in range(2):
            store(yh, yl).wait()


SMEM = pl.BlockSpec(memory_space=pltpu.MemorySpace.SMEM)
HBM = pl.BlockSpec(memory_space=pltpu.MemorySpace.HBM)
VMEM = pl.BlockSpec(memory_space=pltpu.MemorySpace.VMEM)


def own_part(core, own, key):
    tokens, width = own.shape
    sent = (tokens, width // 2 + key.shape[1])
    return pl.pallas_call(
        own_kernel,
        in_specs=[SMEM, HBM, HBM],
        out_specs=[HBM, VMEM, VMEM],
        out_shape=[
            jax.ShapeDtypeStruct(sent, jnp.bfloat16),
            jax.ShapeDtypeStruct((tokens, width // 2), jnp.bfloat16),
            jax.ShapeDtypeStruct(key.shape, jnp.bfloat16),
        ],
        scratch_shapes=[
            pltpu.VMEM(own.shape, jnp.bfloat16),
            pltpu.VMEM(key.shape, jnp.bfloat16),
            pltpu.VMEM(sent, jnp.bfloat16),
            pltpu.SemaphoreType.DMA((PIECES + 1,)),
            pltpu.SemaphoreType.DMA((PIECES + 1,)),
        ],
        compiler_params=pltpu.CompilerParams(vmem_limit_bytes=12 * 1024 * 1024),
        cost_estimate=pl.CostEstimate(
            flops=4 * tokens * width, bytes_accessed=5 * 1024 * 1024, transcendentals=0
        ),
    )(core, own, key)


def pair_partial(kept, scaled, got):
    tokens, width = kept.shape
    proj = scaled.shape[1]
    shape = (2, 2, 2, 4, 2, 4, 16, proj)
    return pl.pallas_call(
        pair_kernel,
        in_specs=[VMEM, VMEM, VMEM],
        out_specs=HBM,
        out_shape=jax.ShapeDtypeStruct(shape, jnp.bfloat16),
        scratch_shapes=[
            pltpu.VMEM((2 * tokens, proj), jnp.bfloat16),
            pltpu.VMEM(shape, jnp.bfloat16),
            pltpu.SemaphoreType.DMA((2, 4)),
        ],
        compiler_params=pltpu.CompilerParams(vmem_limit_bytes=48 * 1024 * 1024),
        cost_estimate=pl.CostEstimate(
            flops=4 * tokens * width * proj, bytes_accessed=9 * 1024 * 1024, transcendentals=0
        ),
    )(kept, scaled, got)


def sum_kernel(value_ref, out_ref, out, out_sems):
    sources, blocks = value_ref.shape[:2]
    part = blocks // PIECES

    def store(piece):
        place = pl.ds(piece * part, part)
        return pltpu.make_async_copy(out.at[place], out_ref.at[place], out_sems.at[piece])

    for piece in range(PIECES):

        def add(i, carry):
            place = piece * part + i
            total = value_ref[0, place].astype(jnp.float32)
            for source in range(1, sources):
                total = total + value_ref[source, place].astype(jnp.float32)
            out[place] = total.astype(jnp.bfloat16)
            return carry

        lax.fori_loop(0, part, add, 0)
        store(piece).start()
    for piece in range(PIECES):
        store(piece).wait()


def near_sum(value):
    return pl.pallas_call(
        sum_kernel,
        in_specs=[VMEM],
        out_specs=HBM,
        out_shape=jax.ShapeDtypeStruct(value.shape[1:], jnp.bfloat16),
        scratch_shapes=[
            pltpu.VMEM(value.shape[1:], jnp.bfloat16),
            pltpu.SemaphoreType.DMA((PIECES,)),
        ],
        compiler_params=pltpu.CompilerParams(vmem_limit_bytes=12 * 1024 * 1024),
        cost_estimate=pl.CostEstimate(
            flops=value.size, bytes_accessed=5 * 1024 * 1024, transcendentals=0
        ),
    )(value)


def exchange(value, axes, groups=None):
    return lax.all_to_all(
        value, axes, split_axis=0, concat_axis=0, axis_index_groups=groups, tiled=True
    )


def summed(value):
    return jnp.sum(value.astype(jnp.float32), axis=0)


def on_device(
    hidden_in,
    key_grad,
    gain_second,
    weight_second,
    weight_main,
    weight_m,
    weight_v,
    gain_main,
    gain_m,
    gain_v,
):
    node = lax.axis_index(NODE)
    rows = lax.dynamic_slice_in_dim(weight_second, node * 16, 16, 0)
    gains = lax.dynamic_slice_in_dim(gain_second, node * 16, 16, 0)
    pairs = [
        (m * 16 + g, (2 * g + m // 16) * 16 + m % 16) for m in range(32) for g in range(16)
    ]
    packed = jnp.concatenate([rows, jnp.broadcast_to(gains[:, None], (16, 128))], axis=1)

    core = lax.axis_index("core").astype(jnp.int32).reshape(1)
    sent, kept, scaled = own_part(core, hidden_in, key_grad)
    got = lax.ppermute(sent, "core", [(0, 1), (1, 0)])
    packed = lax.ppermute(packed, ALL, pairs)
    partial_value = pair_partial(kept, scaled, got)
    near = exchange(partial_value.reshape(8, 32, 16, 512), ALL, near_groups())
    scaled_grad = summed(exchange(near_sum(near), FAR))

    packed = packed.astype(jnp.float32)
    rows, gains = packed[:, :512], packed[:, 512:513]
    weight_grad = scaled_grad * gains
    gain_grad = jnp.sum(scaled_grad * rows, axis=1)
    weight_new, weight_first, weight_square = adam_update(
        weight_main, weight_m, weight_v, weight_grad
    )
    gain_new, gain_first, gain_square = adam_update(gain_main, gain_m, gain_v, gain_grad)
    return (weight_new, weight_first, weight_square, gain_new, gain_first, gain_square)


def solution(mesh):
    fine = Mesh(mesh.devices.reshape(SIZES), ALL)
    placed = (
        P(ALL, None),
        P(ALL, None),
        P(GROUP),
        P(GROUP, None),
        P(ALL, None),
        P(ALL, None),
        P(ALL, None),
        P(ALL),
        P(ALL),
        P(ALL),
    )
    return jax.shard_map(
        on_device,
        mesh=fine,
        in_specs=placed,
        out_specs=(P(ALL, None),) * 3 + (P(ALL),) * 3,
        check_vma=False,
    )
```

time: 98.7 us -> 92.6 us (0.938)
  the two profiles are of different devices: /device:TPU:10 before, /device:TPU:1 now
where the time goes in v5:
time: 92.6 us; the launch traced here: 92.3 us
  blocking collectives  39.9 us (43%)
  waiting for transfers between devices  23.3 us (25%)
  starting transfers between devices  16.1 us (17%)
  Pallas kernels  7.5 us (8%)
  local copies, waits for them, and re-layouts  3.18 us (3%)
  other arithmetic  1.46 us (2%)
    all_to_all x1, blocking collectives, exchange(): lax.all_to_all(value, axes, split_axis=0, concat_axis=0, axis_index_group...  39.9 us
    ppermute x1, waiting for transfers between devices, on_device(): packed = lax.ppermute(packed, ALL, pairs)  13.9 us
    ppermute x1, starting transfers between devices, on_device(): got = lax.ppermute(sent, 'core', [(0, 1), (1, 0)])  8.78 us
    all_to_all x1, waiting for transfers between devices, exchange(): lax.all_to_all(value, axes, split_axis=0, concat_axis=0, axis_index_group...  6.14 us
    all_to_all x1, starting transfers between devices, exchange(): lax.all_to_all(value, axes, split_axis=0, concat_axis=0, axis_index_group...  5.39 us
    pallas_call x1, Pallas kernels, pair_partial(): pl.pallas_call(pair_kernel, in_specs=[VMEM, VMEM, VMEM], out_specs=HBM, o...  3.87 us
    ppermute x1, waiting for transfers between devices, on_device(): got = lax.ppermute(sent, 'core', [(0, 1), (1, 0)])  3.3 us
    unnamed x20, local copies, waits for them, and re-layouts  2.91 us
  transfers between devices with their start and end apart: 3, of which 3 were waited for; matrix products, arithmetic and copies ran while one was open for 0% of the time, Pallas kernels for 0%

profile of v5, /device:TPU:1, one launch (start us, length us, event | category | flops | bytes accessed | tf_op | source)
XLA Modules:
  0.0 92.3 jit_solution(17868691628013023430)
XLA Ops:
  0.6 0.0 copy-start
  0.7 0.0 copy-start.1
  0.7 1.9 %copy-done.1 = bf16[192,8192]{1,0:T(8,128)(2,1)S(1)} copy-done((bf16[192,8192]{1,0:T(8,128)(2,1)S(1)}, bf16[192,8192]{1,0:T(8,128)(2,1)}, u32[]{:S(2)}) %copy-start.1) | copy-done | bytes 3145752
  2.6 0.9 %copy-done.2 = bf16[192,512]{1,0:T(8,128)(2,1)S(1)} copy-done((bf16[192,512]{1,0:T(8,128)(2,1)S(1)}, bf16[192,512]{1,0:T(8,128)(2,1)}, u32[]{:S(2)}) %copy-start.2) | copy-done | bytes 196632
  3.5 2.2 %shard_map.145 = (bf16[192,4608]{1,0:T(8,128)(2,1)S(1)}, bf16[192,4096]{1,0:T(8,128)(2,1)S(1)}, bf16[192,512]{1,0:T(8,128)(2,1)S(1)}) custom-call(s32[1]{0:T(128)} %bitcast.core_ref, bf16[192,8192]{1,0:T(8,128)(2,1)S(1)} %copy-done.1, bf16[192,512]{1,0:T(8,128)(2,1)S(1)} %copy-done.2), custom_call_target="tpu_custom_call" | custom-call | flops 6291456 | bytes 5242880 | tf_op jit(solution)/shard_map/pallas_call | solution.py:160
  5.8 8.8 %collective-permute-start = (bf16[192,4608]{1,0:T(8,128)(2,1)S(1)}, bf16[192,4608]{1,0:T(8,128)(2,1)S(1)}, u32[]{:S(2)}, u32[]{:S(2)}) collective-permute-start(bf16[192,4608]{1,0:T(8,128)(2,1)S(1)} %get-tuple-element.11), channel_id=1, source_target_pairs={{0,16},{16,0},{1,17},{17,1},{2,18},{18,2},{3,19},{19,3},{4,20},{20... | collective-permute-start | bytes 5308424 | tf_op jit(solution)/shard_map/ppermute | solution.py:277
  14.6 3.3 %collective-permute-done.got_ref = bf16[192,4608]{1,0:T(8,128)(2,1)S(1)} collective-permute-done((bf16[192,4608]{1,0:T(8,128)(2,1)S(1)}, bf16[192,4608]{1,0:T(8,128)(2,1)S(1)}, u32[]{:S(2)}, u32[]{:S(2)}) %collective-permute-start) | collective-permute-done | bytes 1769504 | tf_op jit(solution)/shard_map/ppermute | solution.py:277
  17.9 3.9 %shard_map.146 = bf16[2,2,2,4,2,4,16,512]{7,6,5,4,3,2,1,0:T(8,128)(2,1)} custom-call(bf16[192,4096]{1,0:T(8,128)(2,1)S(1)} %get-tuple-element.9.kept_ref, bf16[192,512]{1,0:T(8,128)(2,1)S(1)} %get-tuple-element.10.scaled_ref, bf16[192,4608]{1,0:T(8,128)(2,1)S(1)} %collective-permute-done.got_ref), custom_call_target="tpu_custom_call" | custom-call | flops 1610612736 | bytes 9437184 | tf_op jit(solution)/shard_map/pallas_call | solution.py:187
  21.7 39.9 %all_to_all.10.value_ref = bf16[8,32,16,512]{3,2,1,0:T(8,128)(2,1)S(1)} all-to-all(bf16[8,32,16,512]{3,2,1,0:T(8,128)(2,1)} %bitcast.2), channel_id=1, replica_groups={{0,2,1,3,64,66,65,67},{4,6,5,7,68,70,69,71},{8,10,9,11,72,74,73,75},{12..., dimensions={0} | all-to-all | bytes 8388608 | tf_op jit(solution)/shard_map/all_to_all | solution.py:246
  61.7 0.0 copy-start.6
  61.7 0.0 copy-start.7
  61.7 0.0 copy-start.8
  61.7 1.4 %shard_map.147 = bf16[32,16,512]{2,1,0:T(8,128)(2,1)} custom-call(bf16[8,32,16,512]{3,2,1,0:T(8,128)(2,1)S(1)} %all_to_all.10.value_ref), custom_call_target="tpu_custom_call" | custom-call | flops 2097152 | bytes 5242880 | tf_op jit(solution)/shard_map/pallas_call | solution.py:229
  63.1 5.4 %all-to-all-start.1 = ((bf16[32,16,512]{2,1,0:T(8,128)(2,1)}), bf16[32,16,512]{2,1,0:T(8,128)(2,1)S(1)}, u32[]{:S(2)}, u32[]{:S(2)}) async-start(bf16[32,16,512]{2,1,0:T(8,128)(2,1)} %shard_map.147), calls=%async_computation.1 | async-start | bytes 1048576 | tf_op jit(solution)/shard_map/all_to_all | solution.py:246
  68.5 0.1 dynamic_slice.7
  68.6 0.1 broadcast_in_dim.2
  68.7 1.9 %collective-permute-start.1 = (bf16[16,640]{1,0:T(8,128)(2,1)S(1)}, bf16[16,640]{1,0:T(8,128)(2,1)S(1)}, u32[]{:S(2)}, u32[]{:S(2)}) collective-permute-start(bf16[16,640]{1,0:T(8,128)(2,1)S(1)} %pad_maximum_fusion), channel_id=1, source_target_pairs={{0,0},{1,32},{2,64},{3,96},{4,128},{5,160},{6,192},{7,224},{8,256}... | collective-permute-start | bytes 61448 | tf_op jit(solution)/shard_map/ppermute | solution.py:278
  70.6 13.9 %collective-permute-done.1 = bf16[16,640]{1,0:T(8,128)(2,1)S(1)} collective-permute-done((bf16[16,640]{1,0:T(8,128)(2,1)S(1)}, bf16[16,640]{1,0:T(8,128)(2,1)S(1)}, u32[]{:S(2)}, u32[]{:S(2)}) %collective-permute-start.1) | collective-permute-done | bytes 20512 | tf_op jit(solution)/shard_map/ppermute | solution.py:278
  84.5 0.1 slice_reduce_fusion
  84.6 6.1 %all-to-all-done.1 = bf16[32,16,512]{2,1,0:T(8,128)(2,1)S(1)} async-done(((bf16[32,16,512]{2,1,0:T(8,128)(2,1)}), bf16[32,16,512]{2,1,0:T(8,128)(2,1)S(1)}, u32[]{:S(2)}, u32[]{:S(2)}) %all-to-all-start.1) | async-done | bytes 524320 | tf_op jit(solution)/shard_map/all_to_all | solution.py:246
  90.8 0.1 convert_reduce_fusion
  90.9 0.8 multiply_subtract_fusion
  91.7 0.0 copy-done.6
  91.8 0.5 multiply_subtract_fusion.1
  (15 shorter events, 0.0 us)
Async XLA Ops:
  0.6 68.0 %copy-start = (bf16[512,512]{1,0:T(8,128)(2,1)S(1)}, bf16[512,512]{1,0:T(8,128)(2,1)}, u32[]{:S(2)}) copy-start(bf16[512,512]{1,0:T(8,128)(2,1)} %param.13) | copy-start | bytes 1572868
  0.7 1.9 %copy-start.1 = (bf16[192,8192]{1,0:T(8,128)(2,1)S(1)}, bf16[192,8192]{1,0:T(8,128)(2,1)}, u32[]{:S(2)}) copy-start(bf16[192,8192]{1,0:T(8,128)(2,1)} %own_ref.1) | copy-start | bytes 9437188
  2.6 0.9 %copy-start.2 = (bf16[192,512]{1,0:T(8,128)(2,1)S(1)}, bf16[192,512]{1,0:T(8,128)(2,1)}, u32[]{:S(2)}) copy-start(bf16[192,512]{1,0:T(8,128)(2,1)} %key_ref.1) | copy-start | bytes 589828
  5.8 12.1 %collective-permute-start = (bf16[192,4608]{1,0:T(8,128)(2,1)S(1)}, bf16[192,4608]{1,0:T(8,128)(2,1)S(1)}, u32[]{:S(2)}, u32[]{:S(2)}) collective-permute-start(bf16[192,4608]{1,0:T(8,128)(2,1)S(1)} %get-tuple-element.11), channel_id=1, source_target_pairs={{0,16},{16,0},{1,17},{17,1},{2,18},{18,2},{3,19},{19,3},{4,20},{20... | collective-permute-start | bytes 5308424 | tf_op jit(solution)/shard_map/ppermute | solution.py:277
  61.7 6.9 %copy-start.9 = (bf16[512]{0:T(512)(128)(2,1)S(1)}, bf16[512]{0:T(512)(128)(2,1)}, u32[]{:S(2)}) copy-start(bf16[512]{0:T(512)(128)(2,1)} %param.12) | copy-start | bytes 3076
  61.7 29.2 %copy-start.3 = (f32[16,512]{1,0:T(8,128)S(1)}, f32[16,512]{1,0:T(8,128)}, u32[]{:S(2)}) copy-start(f32[16,512]{1,0:T(8,128)} %param.14) | copy-start | bytes 98308
  61.7 29.2 %copy-start.4 = (f32[16,512]{1,0:T(8,128)S(1)}, f32[16,512]{1,0:T(8,128)}, u32[]{:S(2)}) copy-start(f32[16,512]{1,0:T(8,128)} %param.15) | copy-start | bytes 98308
  61.7 29.2 %copy-start.5 = (f32[16,512]{1,0:T(8,128)S(1)}, f32[16,512]{1,0:T(8,128)}, u32[]{:S(2)}) copy-start(f32[16,512]{1,0:T(8,128)} %param.16) | copy-start | bytes 98308
  61.7 30.1 %copy-start.6 = (f32[16]{0:T(128)S(1)}, f32[16]{0:T(128)}, u32[]{:S(2)}) copy-start(f32[16]{0:T(128)} %param.17) | copy-start | bytes 196
  61.7 30.0 %copy-start.7 = (f32[16]{0:T(128)S(1)}, f32[16]{0:T(128)}, u32[]{:S(2)}) copy-start(f32[16]{0:T(128)} %param.18) | copy-start | bytes 196
  61.7 30.0 %copy-start.8 = (f32[16]{0:T(128)S(1)}, f32[16]{0:T(128)}, u32[]{:S(2)}) copy-start(f32[16]{0:T(128)} %param.19) | copy-start | bytes 196
  63.1 27.7 %all-to-all-start.1 = ((bf16[32,16,512]{2,1,0:T(8,128)(2,1)}), bf16[32,16,512]{2,1,0:T(8,128)(2,1)S(1)}, u32[]{:S(2)}, u32[]{:S(2)}) async-start(bf16[32,16,512]{2,1,0:T(8,128)(2,1)} %shard_map.147), calls=%async_computation.1 | async-start | bytes 1048576 | tf_op jit(solution)/shard_map/all_to_all | solution.py:246
  68.7 15.8 %collective-permute-start.1 = (bf16[16,640]{1,0:T(8,128)(2,1)S(1)}, bf16[16,640]{1,0:T(8,128)(2,1)S(1)}, u32[]{:S(2)}, u32[]{:S(2)}) collective-permute-start(bf16[16,640]{1,0:T(8,128)(2,1)S(1)} %pad_maximum_fusion), channel_id=1, source_target_pairs={{0,0},{1,32},{2,64},{3,96},{4,128},{5,160},{6,192},{7,224},{8,256}... | collective-permute-start | bytes 61448 | tf_op jit(solution)/shard_map/ppermute | solution.py:278

commit v6 on v5

--- a/solution.py
+++ b/solution.py
@@ -173,7 +173,7 @@
             pltpu.SemaphoreType.DMA((PIECES + 1,)),
             pltpu.SemaphoreType.DMA((PIECES + 1,)),
         ],
-        compiler_params=pltpu.CompilerParams(vmem_limit_bytes=12 * 1024 * 1024),
+        compiler_params=pltpu.CompilerParams(vmem_limit_bytes=50 * 1024 * 1024),
         cost_estimate=pl.CostEstimate(
             flops=4 * tokens * width, bytes_accessed=5 * 1024 * 1024, transcendentals=0
         ),
@@ -194,7 +194,7 @@
             pltpu.VMEM(shape, jnp.bfloat16),
             pltpu.SemaphoreType.DMA((2, 4)),
         ],
-        compiler_params=pltpu.CompilerParams(vmem_limit_bytes=48 * 1024 * 1024),
+        compiler_params=pltpu.CompilerParams(vmem_limit_bytes=52 * 1024 * 1024),
         cost_estimate=pl.CostEstimate(
             flops=4 * tokens * width * proj, bytes_accessed=9 * 1024 * 1024, transcendentals=0
         ),
@@ -277,6 +277,7 @@
     got = lax.ppermute(sent, "core", [(0, 1), (1, 0)])
     packed = lax.ppermute(packed, ALL, pairs)
     partial_value = pair_partial(kept, scaled, got)
+    partial_value, packed = lax.optimization_barrier((partial_value, packed))
     near = exchange(partial_value.reshape(8, 32, 16, 512), ALL, near_groups())
     scaled_grad = summed(exchange(near_sum(near), FAR))
 

time: 92.6 us -> 95.2 us (1.028)
  starting transfers between devices: 16.1 us -> 20.1 us
  Pallas kernels: 7.5 us -> 10.2 us
  waiting for transfers between devices: 23.3 us -> 21.3 us
  local copies, waits for them, and re-layouts: 3.18 us -> 1.28 us
    ppermute x1, waiting for transfers between devices: 13.9 us -> 0.21 us  [on_device(): packed = lax.ppermute(packed, ALL, pairs)]
    all_to_all x1, waiting for transfers between devices: 6.14 us -> 19.6 us  [exchange(): lax.all_to_all(value, axes, split_axis=0, concat_axis=0, axis_index_group...]
    all_to_all x1, starting transfers between devices: 5.39 us -> 9.41 us  [exchange(): lax.all_to_all(value, axes, split_axis=0, concat_axis=0, axis_index_group...]
    unnamed x20 -> x18, local copies, waits for them, and re-layouts: 2.91 us -> 1.02 us
    ppermute x1, waiting for transfers between devices: 3.3 us -> 1.53 us  [on_device(): got = lax.ppermute(sent, 'core', [(0, 1), (1, 0)])]
    pallas_call x1, Pallas kernels: 3.87 us -> 5.33 us  [pair_partial(): pl.pallas_call(pair_kernel, in_specs=[VMEM, VMEM, VMEM], out_specs=HBM, o...]
    pallas_call x1, Pallas kernels: 2.23 us -> 3.45 us  [own_part(): pl.pallas_call(own_kernel, in_specs=[SMEM, HBM, HBM], out_specs=[HBM, VME...]
  transfers between devices with their start and end apart: 3 -> 3, of which waited for: 3 -> 3; matrix products, arithmetic and copies ran while one was open for 0% -> 0% of each run, Pallas kernels for 0% -> 6%
where the time goes in v6:
time: 95.2 us; the launch traced here: 94.9 us
  blocking collectives  39.7 us (42%)
  waiting for transfers between devices  21.3 us (22%)
  starting transfers between devices  20.1 us (21%)
  Pallas kernels  10.2 us (11%)
  other arithmetic  1.47 us (2%)
  local copies, waits for them, and re-layouts  1.28 us (1%)
    all_to_all x1, blocking collectives, exchange(): lax.all_to_all(value, axes, split_axis=0, concat_axis=0, axis_index_group...  39.7 us
    all_to_all x1, waiting for transfers between devices, exchange(): lax.all_to_all(value, axes, split_axis=0, concat_axis=0, axis_index_group...  19.6 us
    all_to_all x1, starting transfers between devices, exchange(): lax.all_to_all(value, axes, split_axis=0, concat_axis=0, axis_index_group...  9.41 us
    ppermute x1, starting transfers between devices, on_device(): got = lax.ppermute(sent, 'core', [(0, 1), (1, 0)])  8.79 us
    pallas_call x1, Pallas kernels, pair_partial(): pl.pallas_call(pair_kernel, in_specs=[VMEM, VMEM, VMEM], out_specs=HBM, o...  5.33 us
    pallas_call x1, Pallas kernels, own_part(): pl.pallas_call(own_kernel, in_specs=[SMEM, HBM, HBM], out_specs=[HBM, VME...  3.45 us
    ppermute x1, starting transfers between devices, on_device(): packed = lax.ppermute(packed, ALL, pairs)  1.91 us
  transfers between devices with their start and end apart: 3, of which 3 were waited for; matrix products, arithmetic and copies ran while one was open for 0% of the time, Pallas kernels for 6%

profile of v6, /device:TPU:1, one launch (start us, length us, event | category | flops | bytes accessed | tf_op | source)
XLA Modules:
  0.0 94.9 jit_solution(13260760009164454267)
XLA Ops:
  0.6 0.0 copy-start
  0.6 0.0 copy-start.8
  0.7 0.0 copy-start.1
  0.7 1.0 %copy-done.1 = bf16[192,512]{1,0:T(8,128)(2,1)S(1)} copy-done((bf16[192,512]{1,0:T(8,128)(2,1)S(1)}, bf16[192,512]{1,0:T(8,128)(2,1)}, u32[]{:S(2)}) %copy-start.1) | copy-done | bytes 196632
  1.6 3.5 %shard_map.145 = (bf16[192,4608]{1,0:T(8,128)(2,1)}, bf16[192,4096]{1,0:T(8,128)(2,1)S(1)}, bf16[192,512]{1,0:T(8,128)(2,1)S(1)}) custom-call(s32[1]{0:T(128)} %bitcast.core_ref, bf16[192,8192]{1,0:T(8,128)(2,1)} %own_ref.1, bf16[192,512]{1,0:T(8,128)(2,1)S(1)} %copy-done.1), custom_call_target="tpu_custom_call" | custom-call | flops 6291456 | bytes 5242880 | tf_op jit(solution)/shard_map/pallas_call | solution.py:160
  5.1 8.8 %collective-permute-start = (bf16[192,4608]{1,0:T(8,128)(2,1)}, bf16[192,4608]{1,0:T(8,128)(2,1)}, u32[]{:S(2)}, u32[]{:S(2)}) collective-permute-start(bf16[192,4608]{1,0:T(8,128)(2,1)} %get-tuple-element.13), channel_id=1, source_target_pairs={{0,16},{16,0},{1,17},{17,1},{2,18},{18,2},{3,19},{19,3},{4,20},{20... | collective-permute-start | bytes 5308424 | tf_op jit(solution)/shard_map/ppermute | solution.py:277
  13.9 0.0 copy-done.8
  13.9 0.1 dynamic_slice.7
  14.0 0.1 broadcast_in_dim.2
  14.1 1.9 %collective-permute-start.1 = (bf16[16,640]{1,0:T(8,128)(2,1)S(1)}, bf16[16,640]{1,0:T(8,128)(2,1)S(1)}, u32[]{:S(2)}, u32[]{:S(2)}) collective-permute-start(bf16[16,640]{1,0:T(8,128)(2,1)S(1)} %pad_maximum_fusion), channel_id=1, source_target_pairs={{0,0},{1,32},{2,64},{3,96},{4,128},{5,160},{6,192},{7,224},{8,256}... | collective-permute-start | bytes 61448 | tf_op jit(solution)/shard_map/ppermute | solution.py:278
  16.0 1.5 %collective-permute-done.got_ref = bf16[192,4608]{1,0:T(8,128)(2,1)} collective-permute-done((bf16[192,4608]{1,0:T(8,128)(2,1)}, bf16[192,4608]{1,0:T(8,128)(2,1)}, u32[]{:S(2)}, u32[]{:S(2)}) %collective-permute-start) | collective-permute-done | bytes 1769504 | tf_op jit(solution)/shard_map/ppermute | solution.py:277
  17.5 5.3 %shard_map.146 = bf16[2,2,2,4,2,4,16,512]{7,6,5,4,3,2,1,0:T(8,128)(2,1)} custom-call(bf16[192,4096]{1,0:T(8,128)(2,1)S(1)} %get-tuple-element.11.kept_ref, bf16[192,512]{1,0:T(8,128)(2,1)S(1)} %get-tuple-element.12.scaled_ref, bf16[192,4608]{1,0:T(8,128)(2,1)} %collective-permute-done.got_ref), custom_call_target="tpu_custom_call" | custom-call | flops 1610612736 | bytes 9437184 | tf_op jit(solution)/shard_map/pallas_call | solution.py:187
  22.9 0.2 collective-permute-done.1
  23.1 39.7 %all_to_all.10.value_ref = bf16[8,32,16,512]{3,2,1,0:T(8,128)(2,1)S(1)} all-to-all(bf16[8,32,16,512]{3,2,1,0:T(8,128)(2,1)} %bitcast.2), channel_id=1, replica_groups={{0,2,1,3,64,66,65,67},{4,6,5,7,68,70,69,71},{8,10,9,11,72,74,73,75},{12..., dimensions={0} | all-to-all | bytes 8388608 | tf_op jit(solution)/shard_map/all_to_all | solution.py:246
  62.8 0.0 copy-start.6
  62.9 0.0 copy-start.7
  62.9 1.4 %shard_map.147 = bf16[32,16,512]{2,1,0:T(8,128)(2,1)} custom-call(bf16[8,32,16,512]{3,2,1,0:T(8,128)(2,1)S(1)} %all_to_all.10.value_ref), custom_call_target="tpu_custom_call" | custom-call | flops 2097152 | bytes 5242880 | tf_op jit(solution)/shard_map/pallas_call | solution.py:229
  64.3 9.4 %all-to-all-start.1 = ((bf16[32,16,512]{2,1,0:T(8,128)(2,1)}), bf16[32,16,512]{2,1,0:T(8,128)(2,1)S(1)}, u32[]{:S(2)}, u32[]{:S(2)}) async-start(bf16[32,16,512]{2,1,0:T(8,128)(2,1)} %shard_map.147), calls=%async_computation.1 | async-start | bytes 1048576 | tf_op jit(solution)/shard_map/all_to_all | solution.py:246
  73.7 0.1 slice_reduce_fusion
  73.8 19.6 %all-to-all-done.1 = bf16[32,16,512]{2,1,0:T(8,128)(2,1)S(1)} async-done(((bf16[32,16,512]{2,1,0:T(8,128)(2,1)}), bf16[32,16,512]{2,1,0:T(8,128)(2,1)S(1)}, u32[]{:S(2)}, u32[]{:S(2)}) %all-to-all-start.1) | async-done | bytes 524320 | tf_op jit(solution)/shard_map/all_to_all | solution.py:246
  93.4 0.1 convert_reduce_fusion
  93.4 0.0 copy-done.2
  93.5 0.8 multiply_subtract_fusion
  94.3 0.5 multiply_subtract_fusion.1
  (13 shorter events, 0.0 us)
Async XLA Ops:
  0.6 13.4 %copy-start = (bf16[512,512]{1,0:T(8,128)(2,1)S(1)}, bf16[512,512]{1,0:T(8,128)(2,1)}, u32[]{:S(2)}) copy-start(bf16[512,512]{1,0:T(8,128)(2,1)} %param.13) | copy-start | bytes 1572868
  0.6 13.3 %copy-start.8 = (bf16[512]{0:T(512)(128)(2,1)S(1)}, bf16[512]{0:T(512)(128)(2,1)}, u32[]{:S(2)}) copy-start(bf16[512]{0:T(512)(128)(2,1)} %param.12) | copy-start | bytes 3076
  0.7 1.0 %copy-start.1 = (bf16[192,512]{1,0:T(8,128)(2,1)S(1)}, bf16[192,512]{1,0:T(8,128)(2,1)}, u32[]{:S(2)}) copy-start(bf16[192,512]{1,0:T(8,128)(2,1)} %key_ref.1) | copy-start | bytes 589828
  5.1 12.4 %collective-permute-start = (bf16[192,4608]{1,0:T(8,128)(2,1)}, bf16[192,4608]{1,0:T(8,128)(2,1)}, u32[]{:S(2)}, u32[]{:S(2)}) collective-permute-start(bf16[192,4608]{1,0:T(8,128)(2,1)} %get-tuple-element.13), channel_id=1, source_target_pairs={{0,16},{16,0},{1,17},{17,1},{2,18},{18,2},{3,19},{19,3},{4,20},{20... | collective-permute-start | bytes 5308424 | tf_op jit(solution)/shard_map/ppermute | solution.py:277
  14.1 9.0 %collective-permute-start.1 = (bf16[16,640]{1,0:T(8,128)(2,1)S(1)}, bf16[16,640]{1,0:T(8,128)(2,1)S(1)}, u32[]{:S(2)}, u32[]{:S(2)}) collective-permute-start(bf16[16,640]{1,0:T(8,128)(2,1)S(1)} %pad_maximum_fusion), channel_id=1, source_target_pairs={{0,0},{1,32},{2,64},{3,96},{4,128},{5,160},{6,192},{7,224},{8,256}... | collective-permute-start | bytes 61448 | tf_op jit(solution)/shard_map/ppermute | solution.py:278
  62.8 30.6 %copy-start.2 = (f32[16,512]{1,0:T(8,128)S(1)}, f32[16,512]{1,0:T(8,128)}, u32[]{:S(2)}) copy-start(f32[16,512]{1,0:T(8,128)} %param.14) | copy-start | bytes 98308
  62.8 30.6 %copy-start.3 = (f32[16,512]{1,0:T(8,128)S(1)}, f32[16,512]{1,0:T(8,128)}, u32[]{:S(2)}) copy-start(f32[16,512]{1,0:T(8,128)} %param.15) | copy-start | bytes 98308
  62.8 30.6 %copy-start.4 = (f32[16,512]{1,0:T(8,128)S(1)}, f32[16,512]{1,0:T(8,128)}, u32[]{:S(2)}) copy-start(f32[16,512]{1,0:T(8,128)} %param.16) | copy-start | bytes 98308
  62.8 31.5 %copy-start.5 = (f32[16]{0:T(128)S(1)}, f32[16]{0:T(128)}, u32[]{:S(2)}) copy-start(f32[16]{0:T(128)} %param.17) | copy-start | bytes 196
  62.8 31.5 %copy-start.6 = (f32[16]{0:T(128)S(1)}, f32[16]{0:T(128)}, u32[]{:S(2)}) copy-start(f32[16]{0:T(128)} %param.18) | copy-start | bytes 196
  62.9 31.5 %copy-start.7 = (f32[16]{0:T(128)S(1)}, f32[16]{0:T(128)}, u32[]{:S(2)}) copy-start(f32[16]{0:T(128)} %param.19) | copy-start | bytes 196
  64.3 29.1 %all-to-all-start.1 = ((bf16[32,16,512]{2,1,0:T(8,128)(2,1)}), bf16[32,16,512]{2,1,0:T(8,128)(2,1)S(1)}, u32[]{:S(2)}, u32[]{:S(2)}) async-start(bf16[32,16,512]{2,1,0:T(8,128)(2,1)} %shard_map.147), calls=%async_computation.1 | async-start | bytes 1048576 | tf_op jit(solution)/shard_map/all_to_all | solution.py:246

commit v7 on v5

--- a/solution.py
+++ b/solution.py
@@ -1,3 +1,5 @@
+import functools
+
 import jax
 import jax.numpy as jnp
 from jax import lax
@@ -114,39 +116,42 @@
         store(piece).wait()
 
 
-def pair_kernel(kept_ref, scaled_ref, got_ref, out_ref, keys, out, out_sems):
+def pair_kernel(other_y, place_ref, kept_ref, scaled_ref, got_ref, *rest):
+    out_refs, (keys, out, out_sems) = rest[:4], rest[4:]
     tokens, kept = kept_ref.shape
-
-    def store(yh, yl):
-        return pltpu.make_async_copy(
-            out.at[yl, :, :, yh], out_ref.at[yl, :, :, yh], out_sems.at[yl, yh]
-        )
+    yl, xl, zl = place_ref[1], place_ref[2], place_ref[3]
+    if other_y:
+        yl = 1 - yl
+
+    def store(yh, near):
+        source = out.at[lax.rem(xl + near // 2, 2), lax.rem(zl + near % 2, 2), yh]
+        return pltpu.make_async_copy(source, out_refs[near].at[yh], out_sems.at[near, yh])
 
     keys[:tokens, :] = scaled_ref[...]
     keys[tokens:, :] = got_ref[:, kept:]
 
     def step(yh, carry):
-        for yl in range(2):
-            for xh in range(2):
-                start = pl.multiple_of((yh * 2 + yl) * 512 + xh * 256, 256)
-                columns = pl.ds(start, 256)
-                product = lax.dot_general(
-                    jnp.concatenate([kept_ref[:, columns], got_ref[:, columns]], axis=0),
-                    keys[...],
-                    (((0,), (0,)), ((), ())),
-                    preferred_element_type=jnp.float32,
-                )
-                product = product.astype(jnp.bfloat16).reshape(4, 2, 2, 16, 512)
-                for zl in range(2):
-                    for xl in range(2):
-                        out[yl, xl, zl, yh, xh] = product[:, zl, xl]
-            store(yh, yl).start()
+        for xh in range(2):
+            start = pl.multiple_of((yh * 2 + yl) * 512 + xh * 256, 256)
+            columns = pl.ds(start, 256)
+            product = lax.dot_general(
+                jnp.concatenate([kept_ref[:, columns], got_ref[:, columns]], axis=0),
+                keys[...],
+                (((0,), (0,)), ((), ())),
+                preferred_element_type=jnp.float32,
+            )
+            product = product.astype(jnp.bfloat16).reshape(4, 2, 2, 16, 512)
+            for z in range(2):
+                for x in range(2):
+                    out[x, z, yh, xh] = product[:, z, x]
+        for near in range(4):
+            store(yh, near).start()
         return carry
 
     lax.fori_loop(0, 4, step, 0)
     for yh in range(4):
-        for yl in range(2):
-            store(yh, yl).wait()
+        for near in range(4):
+            store(yh, near).wait()
 
 
 SMEM = pl.BlockSpec(memory_space=pltpu.MemorySpace.SMEM)
@@ -180,29 +185,30 @@
     )(core, own, key)
 
 
-def pair_partial(kept, scaled, got):
+def pair_partial(place, kept, scaled, got, other_y):
     tokens, width = kept.shape
     proj = scaled.shape[1]
-    shape = (2, 2, 2, 4, 2, 4, 16, proj)
+    shape = (4, 2, 4, 16, proj)
     return pl.pallas_call(
-        pair_kernel,
-        in_specs=[VMEM, VMEM, VMEM],
-        out_specs=HBM,
-        out_shape=jax.ShapeDtypeStruct(shape, jnp.bfloat16),
+        functools.partial(pair_kernel, other_y),
+        in_specs=[SMEM, VMEM, VMEM, VMEM],
+        out_specs=[HBM] * 4,
+        out_shape=[jax.ShapeDtypeStruct(shape, jnp.bfloat16)] * 4,
         scratch_shapes=[
             pltpu.VMEM((2 * tokens, proj), jnp.bfloat16),
-            pltpu.VMEM(shape, jnp.bfloat16),
-            pltpu.SemaphoreType.DMA((2, 4)),
+            pltpu.VMEM((2, 2) + shape, jnp.bfloat16),
+            pltpu.SemaphoreType.DMA((4, 4)),
         ],
-        compiler_params=pltpu.CompilerParams(vmem_limit_bytes=48 * 1024 * 1024),
+        compiler_params=pltpu.CompilerParams(vmem_limit_bytes=16 * 1024 * 1024),
         cost_estimate=pl.CostEstimate(
-            flops=4 * tokens * width * proj, bytes_accessed=9 * 1024 * 1024, transcendentals=0
+            flops=2 * tokens * width * proj, bytes_accessed=5 * 1024 * 1024, transcendentals=0
         ),
-    )(kept, scaled, got)
-
-
-def sum_kernel(value_ref, out_ref, out, out_sems):
-    sources, blocks = value_ref.shape[:2]
+    )(place, kept, scaled, got)
+
+
+def sum_kernel(*refs):
+    value_refs, (out_ref, out, out_sems) = refs[:-3], refs[-3:]
+    blocks = out.shape[0]
     part = blocks // PIECES
 
     def store(piece):
@@ -213,9 +219,9 @@
 
         def add(i, carry):
             place = piece * part + i
-            total = value_ref[0, place].astype(jnp.float32)
-            for source in range(1, sources):
-                total = total + value_ref[source, place].astype(jnp.float32)
+            total = value_refs[0][place].astype(jnp.float32)
+            for value_ref in value_refs[1:]:
+                total = total + value_ref[place].astype(jnp.float32)
             out[place] = total.astype(jnp.bfloat16)
             return carry
 
@@ -225,27 +231,31 @@
         store(piece).wait()
 
 
-def near_sum(value):
+def near_sum(values):
+    value = values[0]
     return pl.pallas_call(
         sum_kernel,
-        in_specs=[VMEM],
+        in_specs=[VMEM] * len(values),
         out_specs=HBM,
-        out_shape=jax.ShapeDtypeStruct(value.shape[1:], jnp.bfloat16),
+        out_shape=jax.ShapeDtypeStruct(value.shape, jnp.bfloat16),
         scratch_shapes=[
-            pltpu.VMEM(value.shape[1:], jnp.bfloat16),
+            pltpu.VMEM(value.shape, jnp.bfloat16),
             pltpu.SemaphoreType.DMA((PIECES,)),
         ],
         compiler_params=pltpu.CompilerParams(vmem_limit_bytes=12 * 1024 * 1024),
         cost_estimate=pl.CostEstimate(
-            flops=value.size, bytes_accessed=5 * 1024 * 1024, transcendentals=0
+            flops=8 * value.size, bytes_accessed=5 * 1024 * 1024, transcendentals=0
         ),
-    )(value)
-
-
-def exchange(value, axes, groups=None):
-    return lax.all_to_all(
-        value, axes, split_axis=0, concat_axis=0, axis_index_groups=groups, tiled=True
-    )
+    )(*values)
+
+
+def exchange(value, axes):
+    return lax.all_to_all(value, axes, split_axis=0, concat_axis=0, tiled=True)
+
+
+def near_exchange(value, groups, near):
+    pairs = [(g[i], g[i ^ near]) for g in groups for i in range(8)]
+    return lax.ppermute(value, ALL, pairs)
 
 
 def summed(value):
@@ -272,12 +282,18 @@
     ]
     packed = jnp.concatenate([rows, jnp.broadcast_to(gains[:, None], (16, 128))], axis=1)
 
-    core = lax.axis_index("core").astype(jnp.int32).reshape(1)
-    sent, kept, scaled = own_part(core, hidden_in, key_grad)
+    place = jnp.stack([lax.axis_index(name) for name in ("core", "yl", "xl", "zl")])
+    place = place.astype(jnp.int32)
+    sent, kept, scaled = own_part(place, hidden_in, key_grad)
     got = lax.ppermute(sent, "core", [(0, 1), (1, 0)])
     packed = lax.ppermute(packed, ALL, pairs)
-    partial_value = pair_partial(kept, scaled, got)
-    near = exchange(partial_value.reshape(8, 32, 16, 512), ALL, near_groups())
+    far_y = pair_partial(place, kept, scaled, got, True)
+    near_y = pair_partial(place, kept, scaled, got, False)
+    groups = near_groups()
+    blocks = [near_y[0]]
+    blocks += [near_exchange(far_y[i], groups, 4 + i) for i in (3, 2, 1, 0)]
+    blocks += [near_exchange(near_y[i], groups, i) for i in (3, 2, 1)]
+    near = [block.reshape(32, 16, 512) for block in blocks]
     scaled_grad = summed(exchange(near_sum(near), FAR))
 
     packed = packed.astype(jnp.float32)

time: 92.6 us -> 104 us (1.12)
  blocking collectives: 39.9 us -> 0 us
  starting transfers between devices: 16.1 us -> 48.4 us
  waiting for transfers between devices: 23.3 us -> 34.5 us
  Pallas kernels: 7.5 us -> 15 us
    all_to_all x1 -> x0, blocking collectives: 39.9 us -> none  [exchange(): lax.all_to_all(value, axes, split_axis=0, concat_axis=0, axis_index_group...]
    ppermute x0 -> x7, starting transfers between devices: none -> 29.6 us  [near_exchange(): return lax.ppermute(value, ALL, pairs)]
    ppermute x0 -> x7, waiting for transfers between devices: none -> 11 us  [near_exchange(): return lax.ppermute(value, ALL, pairs)]
    pallas_call x2 -> x3, Pallas kernels: 5.27 us -> 12.3 us  [the longest x2 10.9 us: pair_partial(): pl.pallas_call(functools.partial(pair_kernel, other_y), in_specs=[SMEM, V...]
    all_to_all x1, starting transfers between devices: 5.39 us -> 8.05 us  [exchange(): return lax.all_to_all(value, axes, split_axis=0, concat_axis=0, tiled=True)]
    all_to_all x1, waiting for transfers between devices: 6.14 us -> 8.18 us  [exchange(): return lax.all_to_all(value, axes, split_axis=0, concat_axis=0, tiled=True)]
    ppermute x1, waiting for transfers between devices: 13.9 us -> 12 us  [on_device(): packed = lax.ppermute(packed, ALL, pairs)]
  transfers between devices with their start and end apart: 3 -> 10, of which waited for: 3 -> 6; matrix products, arithmetic and copies ran while one was open for 0% -> 0% of each run, Pallas kernels for 0% -> 5%
where the time goes in v7:
time: 104 us
  starting transfers between devices  48.4 us (47%)
  waiting for transfers between devices  34.5 us (33%)
  Pallas kernels  15 us (14%)
  local copies, waits for them, and re-layouts  3.19 us (3%)
  other arithmetic  1.54 us (1%)
    ppermute x7, starting transfers between devices, near_exchange(): return lax.ppermute(value, ALL, pairs)  29.6 us
    ppermute x1, waiting for transfers between devices, on_device(): packed = lax.ppermute(packed, ALL, pairs)  12 us
    ppermute x7, waiting for transfers between devices, near_exchange(): return lax.ppermute(value, ALL, pairs)  11 us
    pallas_call x2, Pallas kernels, pair_partial(): pl.pallas_call(functools.partial(pair_kernel, other_y), in_specs=[SMEM, V...  10.9 us
    ppermute x1, starting transfers between devices, on_device(): got = lax.ppermute(sent, 'core', [(0, 1), (1, 0)])  8.8 us
    all_to_all x1, waiting for transfers between devices, exchange(): return lax.all_to_all(value, axes, split_axis=0, concat_axis=0, tiled=True)  8.18 us
    all_to_all x1, starting transfers between devices, exchange(): return lax.all_to_all(value, axes, split_axis=0, concat_axis=0, tiled=True)  8.05 us
    ppermute x1, waiting for transfers between devices, on_device(): got = lax.ppermute(sent, 'core', [(0, 1), (1, 0)])  3.3 us
  transfers between devices with their start and end apart: 10, of which 6 were waited for; matrix products, arithmetic and copies ran while one was open for 0% of the time, Pallas kernels for 5%

profile of v7, /device:TPU:1, one launch (start us, length us, event | category | flops | bytes accessed | tf_op | source)
XLA Modules:
  0.0 103.6 jit_solution(4662492900866595045)
XLA Ops:
  0.7 1.9 %copy-done.1 = bf16[192,8192]{1,0:T(8,128)(2,1)S(1)} copy-done((bf16[192,8192]{1,0:T(8,128)(2,1)S(1)}, bf16[192,8192]{1,0:T(8,128)(2,1)}, u32[]{:S(2)}) %copy-start.1) | copy-done | bytes 3145752
  2.7 0.9 copy-done.2
  3.6 2.8 %shard_map.145 = (bf16[192,4608]{1,0:T(8,128)(2,1)S(1)}, bf16[192,4096]{1,0:T(8,128)(2,1)S(1)}, bf16[192,512]{1,0:T(8,128)(2,1)S(1)}) custom-call(s32[4]{0:T(128)S(1)} %pad_add_fusion.core_ref.place_ref, bf16[192,8192]{1,0:T(8,128)(2,1)S(1)} %copy-done.1, bf16[192,512]{1,0:T(8,128)(2,1)S(1)} %copy-done.2), custom_call_target="tpu_custom_call" | custom-call | flops 6291456 | bytes 5242880 | tf_op jit(solution)/shard_map/pallas_call | solution.py:165
  6.4 8.8 %collective-permute-start = (bf16[192,4608]{1,0:T(8,128)(2,1)S(1)}, bf16[192,4608]{1,0:T(8,128)(2,1)S(1)}, u32[]{:S(2)}, u32[]{:S(2)}) collective-permute-start(bf16[192,4608]{1,0:T(8,128)(2,1)S(1)} %get-tuple-element.19), channel_id=1, source_target_pairs={{0,16},{16,0},{1,17},{17,1},{2,18},{18,2},{3,19},{19,3},{4,20},{20... | collective-permute-start | bytes 5308424 | tf_op jit(solution)/shard_map/ppermute | solution.py:288
  15.2 3.3 %collective-permute-done.got_ref = bf16[192,4608]{1,0:T(8,128)(2,1)S(1)} collective-permute-done((bf16[192,4608]{1,0:T(8,128)(2,1)S(1)}, bf16[192,4608]{1,0:T(8,128)(2,1)S(1)}, u32[]{:S(2)}, u32[]{:S(2)}) %collective-permute-start) | collective-permute-done | bytes 1769504 | tf_op jit(solution)/shard_map/ppermute | solution.py:288
  18.5 5.4 %shard_map.147 = (bf16[4,2,4,16,512]{4,3,2,1,0:T(8,128)(2,1)S(1)}, bf16[4,2,4,16,512]{4,3,2,1,0:T(8,128)(2,1)S(1)}, bf16[4,2,4,16,512]{4,3,2,1,0:T(8,128)(2,1)S(1)}, bf16[4,2,4,16,512]{4,3,2,1,0:T(8,128)(2,1)S(1)}) custom-call(s32[4]{0:T(128)S(1)} %pad_add_fusion.core_ref.place_ref, bf16[192,4096]{1,0:T(8,128)(2,1)S(1)} %get-tuple-element.17.kept_ref, ...), custom_call_target="tpu_custom_call" | custom-call | flops 805306368 | bytes 5242880 | tf_op jit(solution)/shard_map/pallas_call | solution.py:192
  23.9 10.4 %collective-permute-start.1 = (bf16[4,2,4,16,512]{4,3,2,1,0:T(8,128)(2,1)S(1)}, bf16[4,2,4,16,512]{4,3,2,1,0:T(8,128)(2,1)S(1)}, u32[]{:S(2)}, u32[]{:S(2)}) collective-permute-start(bf16[4,2,4,16,512]{4,3,2,1,0:T(8,128)(2,1)S(1)} %get-tuple-element.21), channel_id=1, source_target_pairs={{0,67},{2,65},{1,66},{3,64},{64,3},{66,1},{65,2},{67,0},{4,71},{6,... | collective-permute-start | bytes 1572872 | tf_op jit(solution)/shard_map/ppermute | solution.py:258
  34.3 1.9 %collective-permute-start.2 = (bf16[4,2,4,16,512]{4,3,2,1,0:T(8,128)(2,1)S(1)}, bf16[4,2,4,16,512]{4,3,2,1,0:T(8,128)(2,1)S(1)}, u32[]{:S(2)}, u32[]{:S(2)}) collective-permute-start(bf16[4,2,4,16,512]{4,3,2,1,0:T(8,128)(2,1)S(1)} %get-tuple-element.22), channel_id=1, source_target_pairs={{0,65},{2,67},{1,64},{3,66},{64,1},{66,3},{65,0},{67,2},{4,69},{6,... | collective-permute-start | bytes 1572872 | tf_op jit(solution)/shard_map/ppermute | solution.py:258
  36.3 1.9 %collective-permute-start.3 = (bf16[4,2,4,16,512]{4,3,2,1,0:T(8,128)(2,1)S(1)}, bf16[4,2,4,16,512]{4,3,2,1,0:T(8,128)(2,1)S(1)}, u32[]{:S(2)}, u32[]{:S(2)}) collective-permute-start(bf16[4,2,4,16,512]{4,3,2,1,0:T(8,128)(2,1)S(1)} %get-tuple-element.23), channel_id=1, source_target_pairs={{0,66},{2,64},{1,67},{3,65},{64,2},{66,0},{65,3},{67,1},{4,70},{6,... | collective-permute-start | bytes 1572872 | tf_op jit(solution)/shard_map/ppermute | solution.py:258
  38.2 4.6 %collective-permute-start.4 = (bf16[4,2,4,16,512]{4,3,2,1,0:T(8,128)(2,1)S(1)}, bf16[4,2,4,16,512]{4,3,2,1,0:T(8,128)(2,1)S(1)}, u32[]{:S(2)}, u32[]{:S(2)}) collective-permute-start(bf16[4,2,4,16,512]{4,3,2,1,0:T(8,128)(2,1)S(1)} %get-tuple-element.24), channel_id=1, source_target_pairs={{0,64},{2,66},{1,65},{3,67},{64,0},{66,2},{65,1},{67,3},{4,68},{6,... | collective-permute-start | bytes 1572872 | tf_op jit(solution)/shard_map/ppermute | solution.py:258
  42.8 5.4 %shard_map.146 = (bf16[4,2,4,16,512]{4,3,2,1,0:T(8,128)(2,1)S(1)}, bf16[4,2,4,16,512]{4,3,2,1,0:T(8,128)(2,1)S(1)}, bf16[4,2,4,16,512]{4,3,2,1,0:T(8,128)(2,1)S(1)}, bf16[4,2,4,16,512]{4,3,2,1,0:T(8,128)(2,1)S(1)}) custom-call(s32[4]{0:T(128)S(1)} %pad_add_fusion.core_ref.place_ref, bf16[192,4096]{1,0:T(8,128)(2,1)S(1)} %get-tuple-element.17.kept_ref, ...), custom_call_target="tpu_custom_call" | custom-call | flops 805306368 | bytes 5242880 | tf_op jit(solution)/shard_map/pallas_call | solution.py:192
  48.2 4.3 %collective-permute-start.6 = (bf16[4,2,4,16,512]{4,3,2,1,0:T(8,128)(2,1)S(1)}, bf16[4,2,4,16,512]{4,3,2,1,0:T(8,128)(2,1)S(1)}, u32[]{:S(2)}, u32[]{:S(2)}) collective-permute-start(bf16[4,2,4,16,512]{4,3,2,1,0:T(8,128)(2,1)S(1)} %get-tuple-element.26), channel_id=1, source_target_pairs={{0,1},{2,3},{1,0},{3,2},{64,65},{66,67},{65,64},{67,66},{4,5},{6,7... | collective-permute-start | bytes 1572872 | tf_op jit(solution)/shard_map/ppermute | solution.py:258
  52.5 4.3 %collective-permute-start.7 = (bf16[4,2,4,16,512]{4,3,2,1,0:T(8,128)(2,1)S(1)}, bf16[4,2,4,16,512]{4,3,2,1,0:T(8,128)(2,1)S(1)}, u32[]{:S(2)}, u32[]{:S(2)}) collective-permute-start(bf16[4,2,4,16,512]{4,3,2,1,0:T(8,128)(2,1)S(1)} %get-tuple-element.27), channel_id=1, source_target_pairs={{0,2},{2,0},{1,3},{3,1},{64,66},{66,64},{65,67},{67,65},{4,6},{6,4... | collective-permute-start | bytes 1572872 | tf_op jit(solution)/shard_map/ppermute | solution.py:258
  56.8 2.2 %collective-permute-start.5 = (bf16[4,2,4,16,512]{4,3,2,1,0:T(8,128)(2,1)S(1)}, bf16[4,2,4,16,512]{4,3,2,1,0:T(8,128)(2,1)S(1)}, u32[]{:S(2)}, u32[]{:S(2)}) collective-permute-start(bf16[4,2,4,16,512]{4,3,2,1,0:T(8,128)(2,1)S(1)} %get-tuple-element.25), channel_id=1, source_target_pairs={{0,3},{2,1},{1,2},{3,0},{64,67},{66,65},{65,66},{67,64},{4,7},{6,5... | collective-permute-start | bytes 1572872 | tf_op jit(solution)/shard_map/ppermute | solution.py:258
  59.1 0.4 collective-permute-done.6
  59.5 4.2 %collective-permute-done.7 = bf16[4,2,4,16,512]{4,3,2,1,0:T(8,128)(2,1)S(1)} collective-permute-done((bf16[4,2,4,16,512]{4,3,2,1,0:T(8,128)(2,1)S(1)}, bf16[4,2,4,16,512]{4,3,2,1,0:T(8,128)(2,1)S(1)}, u32[]{:S(2)}, u32[]{:S(2)}) %collective-permute-start.7) | collective-permute-done | bytes 524320 | tf_op jit(solution)/shard_map/ppermute | solution.py:258
  63.7 6.4 %collective-permute-done.5 = bf16[4,2,4,16,512]{4,3,2,1,0:T(8,128)(2,1)S(1)} collective-permute-done((bf16[4,2,4,16,512]{4,3,2,1,0:T(8,128)(2,1)S(1)}, bf16[4,2,4,16,512]{4,3,2,1,0:T(8,128)(2,1)S(1)}, u32[]{:S(2)}, u32[]{:S(2)}) %collective-permute-start.5) | collective-permute-done | bytes 524320 | tf_op jit(solution)/shard_map/ppermute | solution.py:258
  70.1 1.4 %shard_map.148 = bf16[32,16,512]{2,1,0:T(8,128)(2,1)} custom-call(bf16[32,16,512]{2,1,0:T(8,128)(2,1)S(1)} %bitcast.16, bf16[32,16,512]{2,1,0:T(8,128)(2,1)S(1)} %bitcast.12, bf16[32,16,512]{2,1,0:T(8,128)(2,1)S(1)} %bitcast.13, bf16[32,16,512]{2,1,0:T(8,128)(2,1)S(1)} %bitcast.14, bf16[32,16,512]{2,1,0:T(8,128)(2,1)S(1)} %bitcast.15, ...), custom_call_target="tpu_custom_call" | custom-call | flops 2097152 | bytes 5242880 | tf_op jit(solution)/shard_map/pallas_call | solution.py:236
  71.6 8.0 %all-to-all-start = ((bf16[32,16,512]{2,1,0:T(8,128)(2,1)}), bf16[32,16,512]{2,1,0:T(8,128)(2,1)S(1)}, u32[]{:S(2)}, u32[]{:S(2)}) async-start(bf16[32,16,512]{2,1,0:T(8,128)(2,1)} %shard_map.148), calls=%async_computation | async-start | bytes 1048576 | tf_op jit(solution)/shard_map/all_to_all | solution.py:253
  79.8 1.9 %collective-permute-start.8 = (bf16[16,640]{1,0:T(8,128)(2,1)S(1)}, bf16[16,640]{1,0:T(8,128)(2,1)S(1)}, u32[]{:S(2)}, u32[]{:S(2)}) collective-permute-start(bf16[16,640]{1,0:T(8,128)(2,1)S(1)} %pad_maximum_fusion), channel_id=1, source_target_pairs={{0,0},{1,32},{2,64},{3,96},{4,128},{5,160},{6,192},{7,224},{8,256}... | collective-permute-start | bytes 61448 | tf_op jit(solution)/shard_map/ppermute | solution.py:289
  81.7 12.0 %collective-permute-done.8 = bf16[16,640]{1,0:T(8,128)(2,1)S(1)} collective-permute-done((bf16[16,640]{1,0:T(8,128)(2,1)S(1)}, bf16[16,640]{1,0:T(8,128)(2,1)S(1)}, u32[]{:S(2)}, u32[]{:S(2)}) %collective-permute-start.8) | collective-permute-done | bytes 20512 | tf_op jit(solution)/shard_map/ppermute | solution.py:289
  93.9 8.2 %all-to-all-done = bf16[32,16,512]{2,1,0:T(8,128)(2,1)S(1)} async-done(((bf16[32,16,512]{2,1,0:T(8,128)(2,1)}), bf16[32,16,512]{2,1,0:T(8,128)(2,1)S(1)}, u32[]{:S(2)}, u32[]{:S(2)}) %all-to-all-start) | async-done | bytes 524320 | tf_op jit(solution)/shard_map/all_to_all | solution.py:253
  102.2 0.8 multiply_subtract_fusion
  103.0 0.5 multiply_subtract_fusion.1
  (30 shorter events, 0.5 us)
Async XLA Ops:
  0.6 79.1 %copy-start = (bf16[512,512]{1,0:T(8,128)(2,1)S(1)}, bf16[512,512]{1,0:T(8,128)(2,1)}, u32[]{:S(2)}) copy-start(bf16[512,512]{1,0:T(8,128)(2,1)} %param.13) | copy-start | bytes 1572868
  0.7 1.9 %copy-start.1 = (bf16[192,8192]{1,0:T(8,128)(2,1)S(1)}, bf16[192,8192]{1,0:T(8,128)(2,1)}, u32[]{:S(2)}) copy-start(bf16[192,8192]{1,0:T(8,128)(2,1)} %own_ref.1) | copy-start | bytes 9437188
  2.7 0.9 copy-start.2
  6.4 12.1 %collective-permute-start = (bf16[192,4608]{1,0:T(8,128)(2,1)S(1)}, bf16[192,4608]{1,0:T(8,128)(2,1)S(1)}, u32[]{:S(2)}, u32[]{:S(2)}) collective-permute-start(bf16[192,4608]{1,0:T(8,128)(2,1)S(1)} %get-tuple-element.19), channel_id=1, source_target_pairs={{0,16},{16,0},{1,17},{17,1},{2,18},{18,2},{3,19},{19,3},{4,20},{20... | collective-permute-start | bytes 5308424 | tf_op jit(solution)/shard_map/ppermute | solution.py:288
  23.9 28.6 %collective-permute-start.1 = (bf16[4,2,4,16,512]{4,3,2,1,0:T(8,128)(2,1)S(1)}, bf16[4,2,4,16,512]{4,3,2,1,0:T(8,128)(2,1)S(1)}, u32[]{:S(2)}, u32[]{:S(2)}) collective-permute-start(bf16[4,2,4,16,512]{4,3,2,1,0:T(8,128)(2,1)S(1)} %get-tuple-element.21), channel_id=1, source_target_pairs={{0,67},{2,65},{1,66},{3,64},{64,3},{66,1},{65,2},{67,0},{4,71},{6,... | collective-permute-start | bytes 1572872 | tf_op jit(solution)/shard_map/ppermute | solution.py:258
  34.3 22.5 %collective-permute-start.2 = (bf16[4,2,4,16,512]{4,3,2,1,0:T(8,128)(2,1)S(1)}, bf16[4,2,4,16,512]{4,3,2,1,0:T(8,128)(2,1)S(1)}, u32[]{:S(2)}, u32[]{:S(2)}) collective-permute-start(bf16[4,2,4,16,512]{4,3,2,1,0:T(8,128)(2,1)S(1)} %get-tuple-element.22), channel_id=1, source_target_pairs={{0,65},{2,67},{1,64},{3,66},{64,1},{66,3},{65,0},{67,2},{4,69},{6,... | collective-permute-start | bytes 1572872 | tf_op jit(solution)/shard_map/ppermute | solution.py:258
  36.3 22.8 %collective-permute-start.3 = (bf16[4,2,4,16,512]{4,3,2,1,0:T(8,128)(2,1)S(1)}, bf16[4,2,4,16,512]{4,3,2,1,0:T(8,128)(2,1)S(1)}, u32[]{:S(2)}, u32[]{:S(2)}) collective-permute-start(bf16[4,2,4,16,512]{4,3,2,1,0:T(8,128)(2,1)S(1)} %get-tuple-element.23), channel_id=1, source_target_pairs={{0,66},{2,64},{1,67},{3,65},{64,2},{66,0},{65,3},{67,1},{4,70},{6,... | collective-permute-start | bytes 1572872 | tf_op jit(solution)/shard_map/ppermute | solution.py:258
  38.2 20.9 %collective-permute-start.4 = (bf16[4,2,4,16,512]{4,3,2,1,0:T(8,128)(2,1)S(1)}, bf16[4,2,4,16,512]{4,3,2,1,0:T(8,128)(2,1)S(1)}, u32[]{:S(2)}, u32[]{:S(2)}) collective-permute-start(bf16[4,2,4,16,512]{4,3,2,1,0:T(8,128)(2,1)S(1)} %get-tuple-element.24), channel_id=1, source_target_pairs={{0,64},{2,66},{1,65},{3,67},{64,0},{66,2},{65,1},{67,3},{4,68},{6,... | collective-permute-start | bytes 1572872 | tf_op jit(solution)/shard_map/ppermute | solution.py:258
  48.2 11.3 %collective-permute-start.6 = (bf16[4,2,4,16,512]{4,3,2,1,0:T(8,128)(2,1)S(1)}, bf16[4,2,4,16,512]{4,3,2,1,0:T(8,128)(2,1)S(1)}, u32[]{:S(2)}, u32[]{:S(2)}) collective-permute-start(bf16[4,2,4,16,512]{4,3,2,1,0:T(8,128)(2,1)S(1)} %get-tuple-element.26), channel_id=1, source_target_pairs={{0,1},{2,3},{1,0},{3,2},{64,65},{66,67},{65,64},{67,66},{4,5},{6,7... | collective-permute-start | bytes 1572872 | tf_op jit(solution)/shard_map/ppermute | solution.py:258
  52.5 11.1 %collective-permute-start.7 = (bf16[4,2,4,16,512]{4,3,2,1,0:T(8,128)(2,1)S(1)}, bf16[4,2,4,16,512]{4,3,2,1,0:T(8,128)(2,1)S(1)}, u32[]{:S(2)}, u32[]{:S(2)}) collective-permute-start(bf16[4,2,4,16,512]{4,3,2,1,0:T(8,128)(2,1)S(1)} %get-tuple-element.27), channel_id=1, source_target_pairs={{0,2},{2,0},{1,3},{3,1},{64,66},{66,64},{65,67},{67,65},{4,6},{6,4... | collective-permute-start | bytes 1572872 | tf_op jit(solution)/shard_map/ppermute | solution.py:258
  56.8 13.2 %collective-permute-start.5 = (bf16[4,2,4,16,512]{4,3,2,1,0:T(8,128)(2,1)S(1)}, bf16[4,2,4,16,512]{4,3,2,1,0:T(8,128)(2,1)S(1)}, u32[]{:S(2)}, u32[]{:S(2)}) collective-permute-start(bf16[4,2,4,16,512]{4,3,2,1,0:T(8,128)(2,1)S(1)} %get-tuple-element.25), channel_id=1, source_target_pairs={{0,3},{2,1},{1,2},{3,0},{64,67},{66,65},{65,66},{67,64},{4,7},{6,5... | collective-permute-start | bytes 1572872 | tf_op jit(solution)/shard_map/ppermute | solution.py:258
  70.1 9.6 %copy-start.9 = (bf16[512]{0:T(512)(128)(2,1)S(1)}, bf16[512]{0:T(512)(128)(2,1)}, u32[]{:S(2)}) copy-start(bf16[512]{0:T(512)(128)(2,1)} %param.12) | copy-start | bytes 3076
  71.5 30.7 %copy-start.3 = (f32[16,512]{1,0:T(8,128)S(1)}, f32[16,512]{1,0:T(8,128)}, u32[]{:S(2)}) copy-start(f32[16,512]{1,0:T(8,128)} %param.14) | copy-start | bytes 98308
  71.5 30.7 %copy-start.4 = (f32[16,512]{1,0:T(8,128)S(1)}, f32[16,512]{1,0:T(8,128)}, u32[]{:S(2)}) copy-start(f32[16,512]{1,0:T(8,128)} %param.15) | copy-start | bytes 98308
  71.5 30.7 %copy-start.5 = (f32[16,512]{1,0:T(8,128)S(1)}, f32[16,512]{1,0:T(8,128)}, u32[]{:S(2)}) copy-start(f32[16,512]{1,0:T(8,128)} %param.16) | copy-start | bytes 98308
  71.5 31.5 %copy-start.6 = (f32[16]{0:T(128)S(1)}, f32[16]{0:T(128)}, u32[]{:S(2)}) copy-start(f32[16]{0:T(128)} %param.17) | copy-start | bytes 196
  71.6 31.5 %copy-start.7 = (f32[16]{0:T(128)S(1)}, f32[16]{0:T(128)}, u32[]{:S(2)}) copy-start(f32[16]{0:T(128)} %param.18) | copy-start | bytes 196
  71.6 31.5 %copy-start.8 = (f32[16]{0:T(128)S(1)}, f32[16]{0:T(128)}, u32[]{:S(2)}) copy-start(f32[16]{0:T(128)} %param.19) | copy-start | bytes 196
  71.6 30.5 %all-to-all-start = ((bf16[32,16,512]{2,1,0:T(8,128)(2,1)}), bf16[32,16,512]{2,1,0:T(8,128)(2,1)S(1)}, u32[]{:S(2)}, u32[]{:S(2)}) async-start(bf16[32,16,512]{2,1,0:T(8,128)(2,1)} %shard_map.148), calls=%async_computation | async-start | bytes 1048576 | tf_op jit(solution)/shard_map/all_to_all | solution.py:253
  79.8 13.9 %collective-permute-start.8 = (bf16[16,640]{1,0:T(8,128)(2,1)S(1)}, bf16[16,640]{1,0:T(8,128)(2,1)S(1)}, u32[]{:S(2)}, u32[]{:S(2)}) collective-permute-start(bf16[16,640]{1,0:T(8,128)(2,1)S(1)} %pad_maximum_fusion), channel_id=1, source_target_pairs={{0,0},{1,32},{2,64},{3,96},{4,128},{5,160},{6,192},{7,224},{8,256}... | collective-permute-start | bytes 61448 | tf_op jit(solution)/shard_map/ppermute | solution.py:289

commit v8 on v5

--- a/solution.py
+++ b/solution.py
@@ -17,25 +17,28 @@
 SIZES = (4, 2, 2, 2, 4, 2, 2)
 ALL = ("yh", "yl", "xh", "core", "zh", "zl", "xl")
 NODE, GROUP = ALL[:4], ALL[4:]
-FAR = ("yh", "xh", "zh")
-
-
-def near_groups():
-    groups = []
-    for core in range(2):
-        for ky in range(core, 8, 2):
-            for kx in range(core, 4, 2):
-                for kz in range(core, 8, 2):
-                    members = []
-                    for yl in range(2):
-                        for xl in range(2):
-                            for zl in range(2):
-                                y = (ky + (yl != core)) % 8
-                                x = (kx + (xl != core)) % 4
-                                z = (kz + (zl != core)) % 8
-                                members.append((((y * 2 + x // 2) * 2 + core) * 8 + z) * 2 + x % 2)
-                    groups.append(members)
-    return groups
+
+
+def side(place):
+    return (place + place // 2 + place // 4) % 2
+
+
+def exchange_groups():
+    near, far = {}, {}
+    for y in range(8):
+        for x in range(4):
+            for core in range(2):
+                for z in range(8):
+                    device = (((y * 2 + x // 2) * 2 + core) * 8 + z) * 2 + x % 2
+                    places = ((y - core) % 8, (x - core) % 4, (z - core) % 8)
+                    pair = tuple(place // 2 for place in places)
+                    sides = tuple(side(place) for place in places)
+                    near.setdefault((core,) + pair, []).append((sides, device))
+                    far.setdefault((core,) + sides, []).append((pair, device))
+    return [
+        [[device for _, device in sorted(members)] for members in groups.values()]
+        for groups in (near, far)
+    ]
 
 
 def adam_update(weights, moment_one, moment_two, gradient):
@@ -114,39 +117,49 @@
         store(piece).wait()
 
 
-def pair_kernel(kept_ref, scaled_ref, got_ref, out_ref, keys, out, out_sems):
+def pair_kernel(core_ref, kept_ref, scaled_ref, got_ref, out_ref, keys, out, out_sems):
     tokens, kept = kept_ref.shape
-
-    def store(yh, yl):
+    core = core_ref[0]
+
+    def store(side_y, pair_y):
         return pltpu.make_async_copy(
-            out.at[yl, :, :, yh], out_ref.at[yl, :, :, yh], out_sems.at[yl, yh]
+            out.at[side_y, :, pair_y], out_ref.at[side_y, :, pair_y], out_sems.at[side_y, pair_y]
         )
 
     keys[:tokens, :] = scaled_ref[...]
     keys[tokens:, :] = got_ref[:, kept:]
-
-    def step(yh, carry):
-        for yl in range(2):
+    places_x = [lax.rem(x + 4 - core, 4) for x in range(4)]
+    places_z = [lax.rem(z + 8 - core, 8) for z in range(8)]
+    sides_x, pairs_x = [side(p) for p in places_x], [p // 2 for p in places_x]
+    sides_z, pairs_z = [side(p) for p in places_z], [p // 2 for p in places_z]
+
+    def step(pair_y, carry):
+        for member in range(2):
+            place_y = pair_y * 2 + member
+            side_y = side(place_y)
+            row = lax.rem(place_y + core, 8)
             for xh in range(2):
-                start = pl.multiple_of((yh * 2 + yl) * 512 + xh * 256, 256)
-                columns = pl.ds(start, 256)
+                columns = pl.ds(pl.multiple_of(row * 512 + xh * 256, 256), 256)
                 product = lax.dot_general(
                     jnp.concatenate([kept_ref[:, columns], got_ref[:, columns]], axis=0),
                     keys[...],
                     (((0,), (0,)), ((), ())),
                     preferred_element_type=jnp.float32,
                 )
-                product = product.astype(jnp.bfloat16).reshape(4, 2, 2, 16, 512)
-                for zl in range(2):
+                product = product.astype(jnp.bfloat16).reshape(8, 2, 16, 512)
+                for z in range(8):
                     for xl in range(2):
-                        out[yl, xl, zl, yh, xh] = product[:, zl, xl]
-            store(yh, yl).start()
+                        x = xh * 2 + xl
+                        near = sides_x[x] * 2 + sides_z[z]
+                        far = pairs_x[x] * 4 + pairs_z[z]
+                        out[side_y, near, pair_y, far] = product[z, xl]
+            store(side_y, pair_y).start()
         return carry
 
     lax.fori_loop(0, 4, step, 0)
-    for yh in range(4):
-        for yl in range(2):
-            store(yh, yl).wait()
+    for pair_y in range(4):
+        for side_y in range(2):
+            store(side_y, pair_y).wait()
 
 
 SMEM = pl.BlockSpec(memory_space=pltpu.MemorySpace.SMEM)
@@ -180,13 +193,13 @@
     )(core, own, key)
 
 
-def pair_partial(kept, scaled, got):
+def pair_partial(core, kept, scaled, got):
     tokens, width = kept.shape
     proj = scaled.shape[1]
-    shape = (2, 2, 2, 4, 2, 4, 16, proj)
+    shape = (2, 4, 4, 8, 16, proj)
     return pl.pallas_call(
         pair_kernel,
-        in_specs=[VMEM, VMEM, VMEM],
+        in_specs=[SMEM, VMEM, VMEM, VMEM],
         out_specs=HBM,
         out_shape=jax.ShapeDtypeStruct(shape, jnp.bfloat16),
         scratch_shapes=[
@@ -198,7 +211,7 @@
         cost_estimate=pl.CostEstimate(
             flops=4 * tokens * width * proj, bytes_accessed=9 * 1024 * 1024, transcendentals=0
         ),
-    )(kept, scaled, got)
+    )(core, kept, scaled, got)
 
 
 def sum_kernel(value_ref, out_ref, out, out_sems):
@@ -242,9 +255,9 @@
     )(value)
 
 
-def exchange(value, axes, groups=None):
+def exchange(value, groups):
     return lax.all_to_all(
-        value, axes, split_axis=0, concat_axis=0, axis_index_groups=groups, tiled=True
+        value, ALL, split_axis=0, concat_axis=0, axis_index_groups=groups, tiled=True
     )
 
 
@@ -276,9 +289,10 @@
     sent, kept, scaled = own_part(core, hidden_in, key_grad)
     got = lax.ppermute(sent, "core", [(0, 1), (1, 0)])
     packed = lax.ppermute(packed, ALL, pairs)
-    partial_value = pair_partial(kept, scaled, got)
-    near = exchange(partial_value.reshape(8, 32, 16, 512), ALL, near_groups())
-    scaled_grad = summed(exchange(near_sum(near), FAR))
+    partial_value = pair_partial(core, kept, scaled, got)
+    near_groups, far_groups = exchange_groups()
+    near = exchange(partial_value.reshape(8, 32, 16, 512), near_groups)
+    scaled_grad = summed(exchange(near_sum(near), far_groups))
 
     packed = packed.astype(jnp.float32)
     rows, gains = packed[:, :512], packed[:, 512:513]

time: 92.6 us -> 86.1 us (0.930)
  the two profiles are of different devices: /device:TPU:1 before, /device:TPU:6 now
where the time goes in v8:
time: 86.1 us; the launch traced here: 85.8 us
  blocking collectives  32.6 us (38%)
  starting transfers between devices  20.3 us (24%)
  waiting for transfers between devices  19.7 us (23%)
  Pallas kernels  7.68 us (9%)
  local copies, waits for them, and re-layouts  3.18 us (4%)
  other arithmetic  1.46 us (2%)
    all_to_all x1, blocking collectives, exchange(): lax.all_to_all(value, ALL, split_axis=0, concat_axis=0, axis_index_groups...  32.6 us
    all_to_all x1, starting transfers between devices, exchange(): lax.all_to_all(value, ALL, split_axis=0, concat_axis=0, axis_index_groups...  16.5 us
    all_to_all x1, waiting for transfers between devices, exchange(): lax.all_to_all(value, ALL, split_axis=0, concat_axis=0, axis_index_groups...  8.52 us
    ppermute x1, waiting for transfers between devices, on_device(): packed = lax.ppermute(packed, ALL, pairs)  7.53 us
    pallas_call x1, Pallas kernels, pair_partial(): pl.pallas_call(pair_kernel, in_specs=[SMEM, VMEM, VMEM, VMEM], out_specs=...  4.06 us
    ppermute x1, waiting for transfers between devices, on_device(): got = lax.ppermute(sent, 'core', [(0, 1), (1, 0)])  3.66 us
    unnamed x20, local copies, waits for them, and re-layouts  2.91 us
    pallas_call x1, Pallas kernels, own_part(): pl.pallas_call(own_kernel, in_specs=[SMEM, HBM, HBM], out_specs=[HBM, VME...  2.23 us
  transfers between devices with their start and end apart: 3, of which 3 were waited for; matrix products, arithmetic and copies ran while one was open for 0% of the time, Pallas kernels for 0%

profile of v8, /device:TPU:6, one launch (start us, length us, event | category | flops | bytes accessed | tf_op | source)
XLA Modules:
  0.0 85.8 jit_solution(3925593786635124280)
XLA Ops:
  0.6 0.0 copy-start
  0.7 1.9 %copy-done.1 = bf16[192,8192]{1,0:T(8,128)(2,1)S(1)} copy-done((bf16[192,8192]{1,0:T(8,128)(2,1)S(1)}, bf16[192,8192]{1,0:T(8,128)(2,1)}, u32[]{:S(2)}) %copy-start.1) | copy-done | bytes 3145752
  2.6 0.9 %copy-done.2 = bf16[192,512]{1,0:T(8,128)(2,1)S(1)} copy-done((bf16[192,512]{1,0:T(8,128)(2,1)S(1)}, bf16[192,512]{1,0:T(8,128)(2,1)}, u32[]{:S(2)}) %copy-start.2) | copy-done | bytes 196632
  3.5 2.2 %shard_map.145 = (bf16[192,4608]{1,0:T(8,128)(2,1)S(1)}, bf16[192,4096]{1,0:T(8,128)(2,1)S(1)}, bf16[192,512]{1,0:T(8,128)(2,1)S(1)}) custom-call(s32[1]{0:T(128)} %bitcast.core_ref, bf16[192,8192]{1,0:T(8,128)(2,1)S(1)} %copy-done.1, bf16[192,512]{1,0:T(8,128)(2,1)S(1)} %copy-done.2), custom_call_target="tpu_custom_call" | custom-call | flops 6291456 | bytes 5242880 | tf_op jit(solution)/shard_map/pallas_call | solution.py:173
  5.8 1.9 %collective-permute-start = (bf16[192,4608]{1,0:T(8,128)(2,1)S(1)}, bf16[192,4608]{1,0:T(8,128)(2,1)S(1)}, u32[]{:S(2)}, u32[]{:S(2)}) collective-permute-start(bf16[192,4608]{1,0:T(8,128)(2,1)S(1)} %get-tuple-element.11), channel_id=1, source_target_pairs={{0,16},{16,0},{1,17},{17,1},{2,18},{18,2},{3,19},{19,3},{4,20},{20... | collective-permute-start | bytes 5308424 | tf_op jit(solution)/shard_map/ppermute | solution.py:290
  7.7 3.7 %collective-permute-done.got_ref = bf16[192,4608]{1,0:T(8,128)(2,1)S(1)} collective-permute-done((bf16[192,4608]{1,0:T(8,128)(2,1)S(1)}, bf16[192,4608]{1,0:T(8,128)(2,1)S(1)}, u32[]{:S(2)}, u32[]{:S(2)}) %collective-permute-start) | collective-permute-done | bytes 1769504 | tf_op jit(solution)/shard_map/ppermute | solution.py:290
  11.3 4.1 %shard_map.146 = bf16[2,4,4,8,16,512]{5,4,3,2,1,0:T(8,128)(2,1)} custom-call(s32[1]{0:T(128)} %bitcast.core_ref, bf16[192,4096]{1,0:T(8,128)(2,1)S(1)} %get-tuple-element.9.kept_ref, bf16[192,512]{1,0:T(8,128)(2,1)S(1)} %get-tuple-element.10.scaled_ref, bf16[192,4608]{1,0:T(8,128)(2,1)S(1)} %collective-permute-done.got_ref), custom_call_target="tpu_custom_call" | custom-call | flops 1610612736 | bytes 9437184 | tf_op jit(solution)/shard_map/pallas_call | solution.py:200
  15.4 32.6 %all_to_all.10.value_ref = bf16[8,32,16,512]{3,2,1,0:T(8,128)(2,1)S(1)} all-to-all(bf16[8,32,16,512]{3,2,1,0:T(8,128)(2,1)} %bitcast.2), channel_id=1, replica_groups={{0,2,1,3,64,66,65,67},{6,4,7,5,70,68,71,69},{10,8,11,9,74,72,75,73},{12..., dimensions={0} | all-to-all | bytes 8388608 | tf_op jit(solution)/shard_map/all_to_all | solution.py:259
  48.0 0.0 copy-start.6
  48.1 0.0 copy-start.7
  48.1 0.0 copy-start.8
  48.1 1.4 %shard_map.147 = bf16[32,16,512]{2,1,0:T(8,128)(2,1)} custom-call(bf16[8,32,16,512]{3,2,1,0:T(8,128)(2,1)S(1)} %all_to_all.10.value_ref), custom_call_target="tpu_custom_call" | custom-call | flops 2097152 | bytes 5242880 | tf_op jit(solution)/shard_map/pallas_call | solution.py:242
  49.5 16.5 %all-to-all-start.1 = ((bf16[32,16,512]{2,1,0:T(8,128)(2,1)}), bf16[32,16,512]{2,1,0:T(8,128)(2,1)S(1)}, u32[]{:S(2)}, u32[]{:S(2)}) async-start(bf16[32,16,512]{2,1,0:T(8,128)(2,1)} %shard_map.147), calls=%async_computation.1 | async-start | bytes 1048576 | tf_op jit(solution)/shard_map/all_to_all | solution.py:259
  66.0 0.0 copy-done.9
  66.0 0.1 dynamic_slice.7
  66.1 0.0 copy-done
  66.1 0.1 broadcast_in_dim.2
  66.2 1.9 %collective-permute-start.1 = (bf16[16,640]{1,0:T(8,128)(2,1)S(1)}, bf16[16,640]{1,0:T(8,128)(2,1)S(1)}, u32[]{:S(2)}, u32[]{:S(2)}) collective-permute-start(bf16[16,640]{1,0:T(8,128)(2,1)S(1)} %pad_maximum_fusion), channel_id=1, source_target_pairs={{0,0},{1,32},{2,64},{3,96},{4,128},{5,160},{6,192},{7,224},{8,256}... | collective-permute-start | bytes 61448 | tf_op jit(solution)/shard_map/ppermute | solution.py:291
  68.1 7.5 %collective-permute-done.1 = bf16[16,640]{1,0:T(8,128)(2,1)S(1)} collective-permute-done((bf16[16,640]{1,0:T(8,128)(2,1)S(1)}, bf16[16,640]{1,0:T(8,128)(2,1)S(1)}, u32[]{:S(2)}, u32[]{:S(2)}) %collective-permute-start.1) | collective-permute-done | bytes 20512 | tf_op jit(solution)/shard_map/ppermute | solution.py:291
  75.6 0.1 slice_reduce_fusion
  75.7 8.5 %all-to-all-done.1 = bf16[32,16,512]{2,1,0:T(8,128)(2,1)S(1)} async-done(((bf16[32,16,512]{2,1,0:T(8,128)(2,1)}), bf16[32,16,512]{2,1,0:T(8,128)(2,1)S(1)}, u32[]{:S(2)}, u32[]{:S(2)}) %all-to-all-start.1) | async-done | bytes 524320 | tf_op jit(solution)/shard_map/all_to_all | solution.py:259
  84.3 0.1 convert_reduce_fusion
  84.4 0.8 multiply_subtract_fusion
  85.2 0.5 multiply_subtract_fusion.1
  (15 shorter events, 0.0 us)
Async XLA Ops:
  0.6 65.5 %copy-start = (bf16[512,512]{1,0:T(8,128)(2,1)S(1)}, bf16[512,512]{1,0:T(8,128)(2,1)}, u32[]{:S(2)}) copy-start(bf16[512,512]{1,0:T(8,128)(2,1)} %param.13) | copy-start | bytes 1572868
  0.7 1.9 %copy-start.1 = (bf16[192,8192]{1,0:T(8,128)(2,1)S(1)}, bf16[192,8192]{1,0:T(8,128)(2,1)}, u32[]{:S(2)}) copy-start(bf16[192,8192]{1,0:T(8,128)(2,1)} %own_ref.1) | copy-start | bytes 9437188
  2.6 0.9 %copy-start.2 = (bf16[192,512]{1,0:T(8,128)(2,1)S(1)}, bf16[192,512]{1,0:T(8,128)(2,1)}, u32[]{:S(2)}) copy-start(bf16[192,512]{1,0:T(8,128)(2,1)} %key_ref.1) | copy-start | bytes 589828
  5.8 5.6 %collective-permute-start = (bf16[192,4608]{1,0:T(8,128)(2,1)S(1)}, bf16[192,4608]{1,0:T(8,128)(2,1)S(1)}, u32[]{:S(2)}, u32[]{:S(2)}) collective-permute-start(bf16[192,4608]{1,0:T(8,128)(2,1)S(1)} %get-tuple-element.11), channel_id=1, source_target_pairs={{0,16},{16,0},{1,17},{17,1},{2,18},{18,2},{3,19},{19,3},{4,20},{20... | collective-permute-start | bytes 5308424 | tf_op jit(solution)/shard_map/ppermute | solution.py:290
  48.0 18.0 %copy-start.9 = (bf16[512]{0:T(512)(128)(2,1)S(1)}, bf16[512]{0:T(512)(128)(2,1)}, u32[]{:S(2)}) copy-start(bf16[512]{0:T(512)(128)(2,1)} %param.12) | copy-start | bytes 3076
  48.0 36.3 %copy-start.3 = (f32[16,512]{1,0:T(8,128)S(1)}, f32[16,512]{1,0:T(8,128)}, u32[]{:S(2)}) copy-start(f32[16,512]{1,0:T(8,128)} %param.14) | copy-start | bytes 98308
  48.0 36.3 %copy-start.4 = (f32[16,512]{1,0:T(8,128)S(1)}, f32[16,512]{1,0:T(8,128)}, u32[]{:S(2)}) copy-start(f32[16,512]{1,0:T(8,128)} %param.15) | copy-start | bytes 98308
  48.0 36.3 %copy-start.5 = (f32[16,512]{1,0:T(8,128)S(1)}, f32[16,512]{1,0:T(8,128)}, u32[]{:S(2)}) copy-start(f32[16,512]{1,0:T(8,128)} %param.16) | copy-start | bytes 98308
  48.0 37.2 %copy-start.6 = (f32[16]{0:T(128)S(1)}, f32[16]{0:T(128)}, u32[]{:S(2)}) copy-start(f32[16]{0:T(128)} %param.17) | copy-start | bytes 196
  48.1 37.2 %copy-start.7 = (f32[16]{0:T(128)S(1)}, f32[16]{0:T(128)}, u32[]{:S(2)}) copy-start(f32[16]{0:T(128)} %param.18) | copy-start | bytes 196
  48.1 37.2 %copy-start.8 = (f32[16]{0:T(128)S(1)}, f32[16]{0:T(128)}, u32[]{:S(2)}) copy-start(f32[16]{0:T(128)} %param.19) | copy-start | bytes 196
  49.5 34.8 %all-to-all-start.1 = ((bf16[32,16,512]{2,1,0:T(8,128)(2,1)}), bf16[32,16,512]{2,1,0:T(8,128)(2,1)S(1)}, u32[]{:S(2)}, u32[]{:S(2)}) async-start(bf16[32,16,512]{2,1,0:T(8,128)(2,1)} %shard_map.147), calls=%async_computation.1 | async-start | bytes 1048576 | tf_op jit(solution)/shard_map/all_to_all | solution.py:259
  66.2 9.4 %collective-permute-start.1 = (bf16[16,640]{1,0:T(8,128)(2,1)S(1)}, bf16[16,640]{1,0:T(8,128)(2,1)S(1)}, u32[]{:S(2)}, u32[]{:S(2)}) collective-permute-start(bf16[16,640]{1,0:T(8,128)(2,1)S(1)} %pad_maximum_fusion), channel_id=1, source_target_pairs={{0,0},{1,32},{2,64},{3,96},{4,128},{5,160},{6,192},{7,224},{8,256}... | collective-permute-start | bytes 61448 | tf_op jit(solution)/shard_map/ppermute | solution.py:291

commit v9 on v8

--- a/solution.py
+++ b/solution.py
@@ -16,7 +16,7 @@
 
 SIZES = (4, 2, 2, 2, 4, 2, 2)
 ALL = ("yh", "yl", "xh", "core", "zh", "zl", "xl")
-NODE, GROUP = ALL[:4], ALL[4:]
+GROUP = ALL[4:]
 
 
 def side(place):
@@ -186,7 +186,7 @@
             pltpu.SemaphoreType.DMA((PIECES + 1,)),
             pltpu.SemaphoreType.DMA((PIECES + 1,)),
         ],
-        compiler_params=pltpu.CompilerParams(vmem_limit_bytes=12 * 1024 * 1024),
+        compiler_params=pltpu.CompilerParams(vmem_limit_bytes=50 * 1024 * 1024),
         cost_estimate=pl.CostEstimate(
             flops=4 * tokens * width, bytes_accessed=5 * 1024 * 1024, transcendentals=0
         ),
@@ -277,11 +277,18 @@
     gain_m,
     gain_v,
 ):
-    node = lax.axis_index(NODE)
-    rows = lax.dynamic_slice_in_dim(weight_second, node * 16, 16, 0)
-    gains = lax.dynamic_slice_in_dim(gain_second, node * 16, 16, 0)
+    y = lax.axis_index(("yh", "yl"))
+    target = (lax.axis_index("core") * 8 + lax.rem(y + 4, 8)) * 2 + lax.axis_index("xh")
+    rows = lax.dynamic_slice_in_dim(weight_second, target * 16, 16, 0)
+    gains = lax.dynamic_slice_in_dim(gain_second, target * 16, 16, 0)
+    number = lambda y, xh, core, z, xl: (((y * 2 + xh) * 2 + core) * 8 + z) * 2 + xl
     pairs = [
-        (m * 16 + g, (2 * g + m // 16) * 16 + m % 16) for m in range(32) for g in range(16)
+        (number((z + 4) % 8, xl, core, y, xh), number(y, xh, core, z, xl))
+        for y in range(8)
+        for xh in range(2)
+        for core in range(2)
+        for z in range(8)
+        for xl in range(2)
     ]
     packed = jnp.concatenate([rows, jnp.broadcast_to(gains[:, None], (16, 128))], axis=1)
 

time: 86.1 us -> 84.8 us (0.985)
  waiting for transfers between devices: 19.7 us -> 15.6 us
  starting transfers between devices: 20.3 us -> 24.4 us
  local copies, waits for them, and re-layouts: 3.18 us -> 1.29 us
    ppermute x1, starting transfers between devices: 1.91 us -> 6.02 us  [on_device(): packed = lax.ppermute(packed, ALL, pairs)]
    all_to_all x1, waiting for transfers between devices: 8.52 us -> 6.23 us  [exchange(): lax.all_to_all(value, ALL, split_axis=0, concat_axis=0, axis_index_groups...]
    unnamed x20 -> x18, local copies, waits for them, and re-layouts: 2.91 us -> 1.02 us
    ppermute x1, waiting for transfers between devices: 7.53 us -> 5.7 us  [on_device(): packed = lax.ppermute(packed, ALL, pairs)]
where the time goes in v9:
time: 84.8 us; the launch traced here: 84.5 us
  blocking collectives  32.6 us (38%)
  starting transfers between devices  24.4 us (29%)
  waiting for transfers between devices  15.6 us (18%)
  Pallas kernels  8.27 us (10%)
  other arithmetic  1.46 us (2%)
  local copies, waits for them, and re-layouts  1.29 us (2%)
    all_to_all x1, blocking collectives, exchange(): lax.all_to_all(value, ALL, split_axis=0, concat_axis=0, axis_index_groups...  32.6 us
    all_to_all x1, starting transfers between devices, exchange(): lax.all_to_all(value, ALL, split_axis=0, concat_axis=0, axis_index_groups...  16.5 us
    all_to_all x1, waiting for transfers between devices, exchange(): lax.all_to_all(value, ALL, split_axis=0, concat_axis=0, axis_index_groups...  6.23 us
    ppermute x1, starting transfers between devices, on_device(): packed = lax.ppermute(packed, ALL, pairs)  6.02 us
    ppermute x1, waiting for transfers between devices, on_device(): packed = lax.ppermute(packed, ALL, pairs)  5.7 us
    pallas_call x1, Pallas kernels, pair_partial(): pl.pallas_call(pair_kernel, in_specs=[SMEM, VMEM, VMEM, VMEM], out_specs=...  4.04 us
    ppermute x1, waiting for transfers between devices, on_device(): got = lax.ppermute(sent, 'core', [(0, 1), (1, 0)])  3.66 us
    pallas_call x1, Pallas kernels, own_part(): pl.pallas_call(own_kernel, in_specs=[SMEM, HBM, HBM], out_specs=[HBM, VME...  2.83 us
  transfers between devices with their start and end apart: 3, of which 3 were waited for; matrix products, arithmetic and copies ran while one was open for 0% of the time, Pallas kernels for 0%

profile of v9, /device:TPU:6, one launch (start us, length us, event | category | flops | bytes accessed | tf_op | source)
XLA Modules:
  0.0 84.5 jit_solution(16932882219614299206)
XLA Ops:
  0.6 0.0 copy-start
  0.7 1.0 %copy-done.1 = bf16[192,512]{1,0:T(8,128)(2,1)S(1)} copy-done((bf16[192,512]{1,0:T(8,128)(2,1)S(1)}, bf16[192,512]{1,0:T(8,128)(2,1)}, u32[]{:S(2)}) %copy-start.1) | copy-done | bytes 196632
  1.6 2.8 %shard_map.145 = (bf16[192,4608]{1,0:T(8,128)(2,1)S(1)}, bf16[192,4096]{1,0:T(8,128)(2,1)S(1)}, bf16[192,512]{1,0:T(8,128)(2,1)S(1)}) custom-call(s32[1]{0:T(128)} %bitcast.core_ref, bf16[192,8192]{1,0:T(8,128)(2,1)} %own_ref.1, bf16[192,512]{1,0:T(8,128)(2,1)S(1)} %copy-done.1), custom_call_target="tpu_custom_call" | custom-call | flops 6291456 | bytes 5242880 | tf_op jit(solution)/shard_map/pallas_call | solution.py:173
  4.5 1.9 %collective-permute-start = (bf16[192,4608]{1,0:T(8,128)(2,1)S(1)}, bf16[192,4608]{1,0:T(8,128)(2,1)S(1)}, u32[]{:S(2)}, u32[]{:S(2)}) collective-permute-start(bf16[192,4608]{1,0:T(8,128)(2,1)S(1)} %get-tuple-element.11), channel_id=1, source_target_pairs={{0,16},{16,0},{1,17},{17,1},{2,18},{18,2},{3,19},{19,3},{4,20},{20... | collective-permute-start | bytes 5308424 | tf_op jit(solution)/shard_map/ppermute | solution.py:297
  6.4 3.7 %collective-permute-done.got_ref = bf16[192,4608]{1,0:T(8,128)(2,1)S(1)} collective-permute-done((bf16[192,4608]{1,0:T(8,128)(2,1)S(1)}, bf16[192,4608]{1,0:T(8,128)(2,1)S(1)}, u32[]{:S(2)}, u32[]{:S(2)}) %collective-permute-start) | collective-permute-done | bytes 1769504 | tf_op jit(solution)/shard_map/ppermute | solution.py:297
  10.1 4.0 %shard_map.146 = bf16[2,4,4,8,16,512]{5,4,3,2,1,0:T(8,128)(2,1)} custom-call(s32[1]{0:T(128)} %bitcast.core_ref, bf16[192,4096]{1,0:T(8,128)(2,1)S(1)} %get-tuple-element.9.kept_ref, bf16[192,512]{1,0:T(8,128)(2,1)S(1)} %get-tuple-element.10.scaled_ref, bf16[192,4608]{1,0:T(8,128)(2,1)S(1)} %collective-permute-done.got_ref), custom_call_target="tpu_custom_call" | custom-call | flops 1610612736 | bytes 9437184 | tf_op jit(solution)/shard_map/pallas_call | solution.py:200
  14.1 32.6 %all_to_all.10.value_ref = bf16[8,32,16,512]{3,2,1,0:T(8,128)(2,1)S(1)} all-to-all(bf16[8,32,16,512]{3,2,1,0:T(8,128)(2,1)} %bitcast.2), channel_id=1, replica_groups={{0,2,1,3,64,66,65,67},{6,4,7,5,70,68,71,69},{10,8,11,9,74,72,75,73},{12..., dimensions={0} | all-to-all | bytes 8388608 | tf_op jit(solution)/shard_map/all_to_all | solution.py:259
  46.7 0.0 copy-start.5
  46.8 0.0 copy-start.6
  46.8 0.0 copy-start.7
  46.8 1.4 %shard_map.147 = bf16[32,16,512]{2,1,0:T(8,128)(2,1)} custom-call(bf16[8,32,16,512]{3,2,1,0:T(8,128)(2,1)S(1)} %all_to_all.10.value_ref), custom_call_target="tpu_custom_call" | custom-call | flops 2097152 | bytes 5242880 | tf_op jit(solution)/shard_map/pallas_call | solution.py:242
  48.2 16.5 %all-to-all-start.1 = ((bf16[32,16,512]{2,1,0:T(8,128)(2,1)}), bf16[32,16,512]{2,1,0:T(8,128)(2,1)S(1)}, u32[]{:S(2)}, u32[]{:S(2)}) async-start(bf16[32,16,512]{2,1,0:T(8,128)(2,1)} %shard_map.147), calls=%async_computation.1 | async-start | bytes 1048576 | tf_op jit(solution)/shard_map/all_to_all | solution.py:259
  64.7 0.0 copy-done.8
  64.7 0.1 dynamic_slice.7
  64.8 0.0 copy-done
  64.8 0.1 broadcast_in_dim.2
  64.9 6.0 %collective-permute-start.1 = (bf16[16,640]{1,0:T(8,128)(2,1)S(1)}, bf16[16,640]{1,0:T(8,128)(2,1)S(1)}, u32[]{:S(2)}, u32[]{:S(2)}) collective-permute-start(bf16[16,640]{1,0:T(8,128)(2,1)S(1)} %pad_maximum_fusion), channel_id=1, source_target_pairs={{256,0},{288,1},{320,2},{352,3},{384,4},{416,5},{448,6},{480,7},{0... | collective-permute-start | bytes 61448 | tf_op jit(solution)/shard_map/ppermute | solution.py:298
  70.9 5.7 %collective-permute-done.1 = bf16[16,640]{1,0:T(8,128)(2,1)S(1)} collective-permute-done((bf16[16,640]{1,0:T(8,128)(2,1)S(1)}, bf16[16,640]{1,0:T(8,128)(2,1)S(1)}, u32[]{:S(2)}, u32[]{:S(2)}) %collective-permute-start.1) | collective-permute-done | bytes 20512 | tf_op jit(solution)/shard_map/ppermute | solution.py:298
  76.6 0.1 slice_reduce_fusion
  76.7 6.2 %all-to-all-done.1 = bf16[32,16,512]{2,1,0:T(8,128)(2,1)S(1)} async-done(((bf16[32,16,512]{2,1,0:T(8,128)(2,1)}), bf16[32,16,512]{2,1,0:T(8,128)(2,1)S(1)}, u32[]{:S(2)}, u32[]{:S(2)}) %all-to-all-start.1) | async-done | bytes 524320 | tf_op jit(solution)/shard_map/all_to_all | solution.py:259
  83.0 0.1 convert_reduce_fusion
  83.1 0.0 copy-done.3
  83.1 0.8 multiply_subtract_fusion
  83.9 0.5 multiply_subtract_fusion.1
  (13 shorter events, 0.0 us)
Async XLA Ops:
  0.6 64.2 %copy-start = (bf16[512,512]{1,0:T(8,128)(2,1)S(1)}, bf16[512,512]{1,0:T(8,128)(2,1)}, u32[]{:S(2)}) copy-start(bf16[512,512]{1,0:T(8,128)(2,1)} %param.13) | copy-start | bytes 1572868
  0.7 1.0 %copy-start.1 = (bf16[192,512]{1,0:T(8,128)(2,1)S(1)}, bf16[192,512]{1,0:T(8,128)(2,1)}, u32[]{:S(2)}) copy-start(bf16[192,512]{1,0:T(8,128)(2,1)} %key_ref.1) | copy-start | bytes 589828
  4.5 5.6 %collective-permute-start = (bf16[192,4608]{1,0:T(8,128)(2,1)S(1)}, bf16[192,4608]{1,0:T(8,128)(2,1)S(1)}, u32[]{:S(2)}, u32[]{:S(2)}) collective-permute-start(bf16[192,4608]{1,0:T(8,128)(2,1)S(1)} %get-tuple-element.11), channel_id=1, source_target_pairs={{0,16},{16,0},{1,17},{17,1},{2,18},{18,2},{3,19},{19,3},{4,20},{20... | collective-permute-start | bytes 5308424 | tf_op jit(solution)/shard_map/ppermute | solution.py:297
  46.7 18.0 %copy-start.8 = (bf16[512]{0:T(512)(128)(2,1)S(1)}, bf16[512]{0:T(512)(128)(2,1)}, u32[]{:S(2)}) copy-start(bf16[512]{0:T(512)(128)(2,1)} %param.12) | copy-start | bytes 3076
  46.7 36.3 %copy-start.2 = (f32[16,512]{1,0:T(8,128)S(1)}, f32[16,512]{1,0:T(8,128)}, u32[]{:S(2)}) copy-start(f32[16,512]{1,0:T(8,128)} %param.14) | copy-start | bytes 98308
  46.7 36.3 %copy-start.3 = (f32[16,512]{1,0:T(8,128)S(1)}, f32[16,512]{1,0:T(8,128)}, u32[]{:S(2)}) copy-start(f32[16,512]{1,0:T(8,128)} %param.15) | copy-start | bytes 98308
  46.7 36.3 %copy-start.4 = (f32[16,512]{1,0:T(8,128)S(1)}, f32[16,512]{1,0:T(8,128)}, u32[]{:S(2)}) copy-start(f32[16,512]{1,0:T(8,128)} %param.16) | copy-start | bytes 98308
  46.7 37.2 %copy-start.5 = (f32[16]{0:T(128)S(1)}, f32[16]{0:T(128)}, u32[]{:S(2)}) copy-start(f32[16]{0:T(128)} %param.17) | copy-start | bytes 196
  46.8 37.2 %copy-start.6 = (f32[16]{0:T(128)S(1)}, f32[16]{0:T(128)}, u32[]{:S(2)}) copy-start(f32[16]{0:T(128)} %param.18) | copy-start | bytes 196
  46.8 37.2 %copy-start.7 = (f32[16]{0:T(128)S(1)}, f32[16]{0:T(128)}, u32[]{:S(2)}) copy-start(f32[16]{0:T(128)} %param.19) | copy-start | bytes 196
  48.2 34.8 %all-to-all-start.1 = ((bf16[32,16,512]{2,1,0:T(8,128)(2,1)}), bf16[32,16,512]{2,1,0:T(8,128)(2,1)S(1)}, u32[]{:S(2)}, u32[]{:S(2)}) async-start(bf16[32,16,512]{2,1,0:T(8,128)(2,1)} %shard_map.147), calls=%async_computation.1 | async-start | bytes 1048576 | tf_op jit(solution)/shard_map/all_to_all | solution.py:259
  64.9 11.7 %collective-permute-start.1 = (bf16[16,640]{1,0:T(8,128)(2,1)S(1)}, bf16[16,640]{1,0:T(8,128)(2,1)S(1)}, u32[]{:S(2)}, u32[]{:S(2)}) collective-permute-start(bf16[16,640]{1,0:T(8,128)(2,1)S(1)} %pad_maximum_fusion), channel_id=1, source_target_pairs={{256,0},{288,1},{320,2},{352,3},{384,4},{416,5},{448,6},{480,7},{0... | collective-permute-start | bytes 61448 | tf_op jit(solution)/shard_map/ppermute | solution.py:298

commit v10 on v9

--- a/solution.py
+++ b/solution.py
@@ -293,6 +293,7 @@
     packed = jnp.concatenate([rows, jnp.broadcast_to(gains[:, None], (16, 128))], axis=1)
 
     core = lax.axis_index("core").astype(jnp.int32).reshape(1)
+    core, packed = lax.optimization_barrier((core, packed))
     sent, kept, scaled = own_part(core, hidden_in, key_grad)
     got = lax.ppermute(sent, "core", [(0, 1), (1, 0)])
     packed = lax.ppermute(packed, ALL, pairs)

time: 84.8 us -> 86.7 us (1.022)
  local copies, waits for them, and re-layouts: 1.29 us -> 2.92 us
    unnamed x18 -> x16, local copies, waits for them, and re-layouts: 1.02 us -> 1.98 us
where the time goes in v10:
time: 86.7 us; the launch traced here: 86.3 us
  blocking collectives  32.6 us (38%)
  starting transfers between devices  24.4 us (28%)
  waiting for transfers between devices  15.8 us (18%)
  Pallas kernels  8.28 us (10%)
  local copies, waits for them, and re-layouts  2.92 us (3%)
  other arithmetic  1.46 us (2%)
    all_to_all x1, blocking collectives, exchange(): lax.all_to_all(value, ALL, split_axis=0, concat_axis=0, axis_index_groups...  32.6 us
    all_to_all x1, starting transfers between devices, exchange(): lax.all_to_all(value, ALL, split_axis=0, concat_axis=0, axis_index_groups...  16.5 us
    all_to_all x1, waiting for transfers between devices, exchange(): lax.all_to_all(value, ALL, split_axis=0, concat_axis=0, axis_index_groups...  6.23 us
    ppermute x1, starting transfers between devices, on_device(): packed = lax.ppermute(packed, ALL, pairs)  6.03 us
    ppermute x1, waiting for transfers between devices, on_device(): packed = lax.ppermute(packed, ALL, pairs)  5.89 us
    pallas_call x1, Pallas kernels, pair_partial(): pl.pallas_call(pair_kernel, in_specs=[SMEM, VMEM, VMEM, VMEM], out_specs=...  4.06 us
    ppermute x1, waiting for transfers between devices, on_device(): got = lax.ppermute(sent, 'core', [(0, 1), (1, 0)])  3.66 us
    pallas_call x1, Pallas kernels, own_part(): pl.pallas_call(own_kernel, in_specs=[SMEM, HBM, HBM], out_specs=[HBM, VME...  2.83 us
  transfers between devices with their start and end apart: 3, of which 3 were waited for; matrix products, arithmetic and copies ran while one was open for 0% of the time, Pallas kernels for 0%

profile of v10, /device:TPU:6, one launch (start us, length us, event | category | flops | bytes accessed | tf_op | source)
XLA Modules:
  0.0 86.3 jit_solution(6599883793244813847)
XLA Ops:
  0.6 0.0 copy-start
  0.7 1.0 %copy-done = bf16[512,512]{1,0:T(8,128)(2,1)S(1)} copy-done((bf16[512,512]{1,0:T(8,128)(2,1)S(1)}, bf16[512,512]{1,0:T(8,128)(2,1)}, u32[]{:S(2)}) %copy-start) | copy-done | bytes 524312
  1.7 0.8 dynamic_slice.7
  2.4 0.1 broadcast_in_dim.2
  2.5 0.9 %copy-done.1 = bf16[192,512]{1,0:T(8,128)(2,1)S(1)} copy-done((bf16[192,512]{1,0:T(8,128)(2,1)S(1)}, bf16[192,512]{1,0:T(8,128)(2,1)}, u32[]{:S(2)}) %copy-start.1) | copy-done | bytes 196632
  3.4 2.8 %shard_map.145 = (bf16[192,4608]{1,0:T(8,128)(2,1)S(1)}, bf16[192,4096]{1,0:T(8,128)(2,1)S(1)}, bf16[192,512]{1,0:T(8,128)(2,1)S(1)}) custom-call(s32[1]{0:T(128)} %bitcast.core_ref, bf16[192,8192]{1,0:T(8,128)(2,1)} %own_ref.1, bf16[192,512]{1,0:T(8,128)(2,1)S(1)} %copy-done.1), custom_call_target="tpu_custom_call" | custom-call | flops 6291456 | bytes 5242880 | tf_op jit(solution)/shard_map/pallas_call | solution.py:173
  6.3 1.9 %collective-permute-start = (bf16[192,4608]{1,0:T(8,128)(2,1)S(1)}, bf16[192,4608]{1,0:T(8,128)(2,1)S(1)}, u32[]{:S(2)}, u32[]{:S(2)}) collective-permute-start(bf16[192,4608]{1,0:T(8,128)(2,1)S(1)} %get-tuple-element.14), channel_id=1, source_target_pairs={{0,16},{16,0},{1,17},{17,1},{2,18},{18,2},{3,19},{19,3},{4,20},{20... | collective-permute-start | bytes 5308424 | tf_op jit(solution)/shard_map/ppermute | solution.py:298
  8.2 3.7 %collective-permute-done.got_ref = bf16[192,4608]{1,0:T(8,128)(2,1)S(1)} collective-permute-done((bf16[192,4608]{1,0:T(8,128)(2,1)S(1)}, bf16[192,4608]{1,0:T(8,128)(2,1)S(1)}, u32[]{:S(2)}, u32[]{:S(2)}) %collective-permute-start) | collective-permute-done | bytes 1769504 | tf_op jit(solution)/shard_map/ppermute | solution.py:298
  11.9 4.1 %shard_map.146 = bf16[2,4,4,8,16,512]{5,4,3,2,1,0:T(8,128)(2,1)} custom-call(s32[1]{0:T(128)} %bitcast.core_ref, bf16[192,4096]{1,0:T(8,128)(2,1)S(1)} %get-tuple-element.12.kept_ref, bf16[192,512]{1,0:T(8,128)(2,1)S(1)} %get-tuple-element.13.scaled_ref, bf16[192,4608]{1,0:T(8,128)(2,1)S(1)} %collective-permute-done.got_ref), custom_call_target="tpu_custom_call" | custom-call | flops 1610612736 | bytes 9437184 | tf_op jit(solution)/shard_map/pallas_call | solution.py:200
  15.9 32.6 %all_to_all.10.value_ref = bf16[8,32,16,512]{3,2,1,0:T(8,128)(2,1)S(1)} all-to-all(bf16[8,32,16,512]{3,2,1,0:T(8,128)(2,1)} %bitcast.2), channel_id=1, replica_groups={{0,2,1,3,64,66,65,67},{6,4,7,5,70,68,71,69},{10,8,11,9,74,72,75,73},{12..., dimensions={0} | all-to-all | bytes 8388608 | tf_op jit(solution)/shard_map/all_to_all | solution.py:259
  48.6 0.0 copy-start.6
  48.6 0.0 copy-start.7
  48.6 1.4 %shard_map.147 = bf16[32,16,512]{2,1,0:T(8,128)(2,1)} custom-call(bf16[8,32,16,512]{3,2,1,0:T(8,128)(2,1)S(1)} %all_to_all.10.value_ref), custom_call_target="tpu_custom_call" | custom-call | flops 2097152 | bytes 5242880 | tf_op jit(solution)/shard_map/pallas_call | solution.py:242
  50.0 16.5 %all-to-all-start.1 = ((bf16[32,16,512]{2,1,0:T(8,128)(2,1)}), bf16[32,16,512]{2,1,0:T(8,128)(2,1)S(1)}, u32[]{:S(2)}, u32[]{:S(2)}) async-start(bf16[32,16,512]{2,1,0:T(8,128)(2,1)} %shard_map.147), calls=%async_computation.1 | async-start | bytes 1048576 | tf_op jit(solution)/shard_map/all_to_all | solution.py:259
  66.5 6.0 %collective-permute-start.1 = (bf16[16,640]{1,0:T(8,128)(2,1)S(1)}, bf16[16,640]{1,0:T(8,128)(2,1)S(1)}, u32[]{:S(2)}, u32[]{:S(2)}) collective-permute-start(bf16[16,640]{1,0:T(8,128)(2,1)S(1)} %pad_maximum_fusion), channel_id=1, source_target_pairs={{256,0},{288,1},{320,2},{352,3},{384,4},{416,5},{448,6},{480,7},{0... | collective-permute-start | bytes 61448 | tf_op jit(solution)/shard_map/ppermute | solution.py:299
  72.5 5.9 %collective-permute-done.1 = bf16[16,640]{1,0:T(8,128)(2,1)S(1)} collective-permute-done((bf16[16,640]{1,0:T(8,128)(2,1)S(1)}, bf16[16,640]{1,0:T(8,128)(2,1)S(1)}, u32[]{:S(2)}, u32[]{:S(2)}) %collective-permute-start.1) | collective-permute-done | bytes 20512 | tf_op jit(solution)/shard_map/ppermute | solution.py:299
  78.4 0.1 slice_reduce_fusion
  78.5 6.2 %all-to-all-done.1 = bf16[32,16,512]{2,1,0:T(8,128)(2,1)S(1)} async-done(((bf16[32,16,512]{2,1,0:T(8,128)(2,1)}), bf16[32,16,512]{2,1,0:T(8,128)(2,1)S(1)}, u32[]{:S(2)}, u32[]{:S(2)}) %all-to-all-start.1) | async-done | bytes 524320 | tf_op jit(solution)/shard_map/all_to_all | solution.py:259
  84.8 0.1 convert_reduce_fusion
  84.9 0.0 copy-done.2
  84.9 0.0 copy-done.3
  84.9 0.0 copy-done.4
  84.9 0.8 multiply_subtract_fusion
  85.7 0.5 multiply_subtract_fusion.1
  (11 shorter events, 0.0 us)
Async XLA Ops:
  0.6 1.0 %copy-start = (bf16[512,512]{1,0:T(8,128)(2,1)S(1)}, bf16[512,512]{1,0:T(8,128)(2,1)}, u32[]{:S(2)}) copy-start(bf16[512,512]{1,0:T(8,128)(2,1)} %param.13) | copy-start | bytes 1572868
  2.5 0.9 %copy-start.1 = (bf16[192,512]{1,0:T(8,128)(2,1)S(1)}, bf16[192,512]{1,0:T(8,128)(2,1)}, u32[]{:S(2)}) copy-start(bf16[192,512]{1,0:T(8,128)(2,1)} %key_ref.1) | copy-start | bytes 589828
  6.3 5.6 %collective-permute-start = (bf16[192,4608]{1,0:T(8,128)(2,1)S(1)}, bf16[192,4608]{1,0:T(8,128)(2,1)S(1)}, u32[]{:S(2)}, u32[]{:S(2)}) collective-permute-start(bf16[192,4608]{1,0:T(8,128)(2,1)S(1)} %get-tuple-element.14), channel_id=1, source_target_pairs={{0,16},{16,0},{1,17},{17,1},{2,18},{18,2},{3,19},{19,3},{4,20},{20... | collective-permute-start | bytes 5308424 | tf_op jit(solution)/shard_map/ppermute | solution.py:298
  48.6 36.3 %copy-start.2 = (f32[16,512]{1,0:T(8,128)S(1)}, f32[16,512]{1,0:T(8,128)}, u32[]{:S(2)}) copy-start(f32[16,512]{1,0:T(8,128)} %param.14) | copy-start | bytes 98308
  48.6 36.3 %copy-start.3 = (f32[16,512]{1,0:T(8,128)S(1)}, f32[16,512]{1,0:T(8,128)}, u32[]{:S(2)}) copy-start(f32[16,512]{1,0:T(8,128)} %param.15) | copy-start | bytes 98308
  48.6 36.3 %copy-start.4 = (f32[16,512]{1,0:T(8,128)S(1)}, f32[16,512]{1,0:T(8,128)}, u32[]{:S(2)}) copy-start(f32[16,512]{1,0:T(8,128)} %param.16) | copy-start | bytes 98308
  48.6 37.2 %copy-start.5 = (f32[16]{0:T(128)S(1)}, f32[16]{0:T(128)}, u32[]{:S(2)}) copy-start(f32[16]{0:T(128)} %param.17) | copy-start | bytes 196
  48.6 37.2 %copy-start.6 = (f32[16]{0:T(128)S(1)}, f32[16]{0:T(128)}, u32[]{:S(2)}) copy-start(f32[16]{0:T(128)} %param.18) | copy-start | bytes 196
  48.6 37.2 %copy-start.7 = (f32[16]{0:T(128)S(1)}, f32[16]{0:T(128)}, u32[]{:S(2)}) copy-start(f32[16]{0:T(128)} %param.19) | copy-start | bytes 196
  50.0 34.8 %all-to-all-start.1 = ((bf16[32,16,512]{2,1,0:T(8,128)(2,1)}), bf16[32,16,512]{2,1,0:T(8,128)(2,1)S(1)}, u32[]{:S(2)}, u32[]{:S(2)}) async-start(bf16[32,16,512]{2,1,0:T(8,128)(2,1)} %shard_map.147), calls=%async_computation.1 | async-start | bytes 1048576 | tf_op jit(solution)/shard_map/all_to_all | solution.py:259
  66.5 11.9 %collective-permute-start.1 = (bf16[16,640]{1,0:T(8,128)(2,1)S(1)}, bf16[16,640]{1,0:T(8,128)(2,1)S(1)}, u32[]{:S(2)}, u32[]{:S(2)}) collective-permute-start(bf16[16,640]{1,0:T(8,128)(2,1)S(1)} %pad_maximum_fusion), channel_id=1, source_target_pairs={{256,0},{288,1},{320,2},{352,3},{384,4},{416,5},{448,6},{480,7},{0... | collective-permute-start | bytes 61448 | tf_op jit(solution)/shard_map/ppermute | solution.py:299

commit v11 on v9

--- a/solution.py
+++ b/solution.py
@@ -48,7 +48,7 @@
     return (weights - learn_rate * (direction + weight_decay * weights), moment_new, square_new)
 
 
-PIECES = 4
+PIECES = 8
 
 
 def own_kernel(

time: 84.8 us -> 84.7 us (level)
  no operation moved by 1% of the time
where the time goes in v11:
time: 84.7 us; the launch traced here: 84.4 us
  blocking collectives  32.6 us (38%)
  starting transfers between devices  24.4 us (29%)
  waiting for transfers between devices  15.6 us (18%)
  Pallas kernels  8.2 us (10%)
  other arithmetic  1.46 us (2%)
  local copies, waits for them, and re-layouts  1.29 us (2%)
    all_to_all x1, blocking collectives, exchange(): lax.all_to_all(value, ALL, split_axis=0, concat_axis=0, axis_index_groups...  32.6 us
    all_to_all x1, starting transfers between devices, exchange(): lax.all_to_all(value, ALL, split_axis=0, concat_axis=0, axis_index_groups...  16.5 us
    all_to_all x1, waiting for transfers between devices, exchange(): lax.all_to_all(value, ALL, split_axis=0, concat_axis=0, axis_index_groups...  6.24 us
    ppermute x1, starting transfers between devices, on_device(): packed = lax.ppermute(packed, ALL, pairs)  6.02 us
    ppermute x1, waiting for transfers between devices, on_device(): packed = lax.ppermute(packed, ALL, pairs)  5.7 us
    pallas_call x1, Pallas kernels, pair_partial(): pl.pallas_call(pair_kernel, in_specs=[SMEM, VMEM, VMEM, VMEM], out_specs=...  4.04 us
    ppermute x1, waiting for transfers between devices, on_device(): got = lax.ppermute(sent, 'core', [(0, 1), (1, 0)])  3.66 us
    pallas_call x1, Pallas kernels, own_part(): pl.pallas_call(own_kernel, in_specs=[SMEM, HBM, HBM], out_specs=[HBM, VME...  2.76 us
  transfers between devices with their start and end apart: 3, of which 3 were waited for; matrix products, arithmetic and copies ran while one was open for 0% of the time, Pallas kernels for 0%

profile of v11, /device:TPU:6, one launch (start us, length us, event | category | flops | bytes accessed | tf_op | source)
XLA Modules:
  0.0 84.4 jit_solution(9338209391790147079)
XLA Ops:
  0.6 0.0 copy-start
  0.7 0.0 copy-start.1
  0.7 1.0 %copy-done.1 = bf16[192,512]{1,0:T(8,128)(2,1)S(1)} copy-done((bf16[192,512]{1,0:T(8,128)(2,1)S(1)}, bf16[192,512]{1,0:T(8,128)(2,1)}, u32[]{:S(2)}) %copy-start.1) | copy-done | bytes 196632
  1.6 2.8 %shard_map.145 = (bf16[192,4608]{1,0:T(8,128)(2,1)S(1)}, bf16[192,4096]{1,0:T(8,128)(2,1)S(1)}, bf16[192,512]{1,0:T(8,128)(2,1)S(1)}) custom-call(s32[1]{0:T(128)} %bitcast.core_ref, bf16[192,8192]{1,0:T(8,128)(2,1)} %own_ref.1, bf16[192,512]{1,0:T(8,128)(2,1)S(1)} %copy-done.1), custom_call_target="tpu_custom_call" | custom-call | flops 6291456 | bytes 5242880 | tf_op jit(solution)/shard_map/pallas_call | solution.py:173
  4.4 1.9 %collective-permute-start = (bf16[192,4608]{1,0:T(8,128)(2,1)S(1)}, bf16[192,4608]{1,0:T(8,128)(2,1)S(1)}, u32[]{:S(2)}, u32[]{:S(2)}) collective-permute-start(bf16[192,4608]{1,0:T(8,128)(2,1)S(1)} %get-tuple-element.11), channel_id=1, source_target_pairs={{0,16},{16,0},{1,17},{17,1},{2,18},{18,2},{3,19},{19,3},{4,20},{20... | collective-permute-start | bytes 5308424 | tf_op jit(solution)/shard_map/ppermute | solution.py:297
  6.3 3.7 %collective-permute-done.got_ref = bf16[192,4608]{1,0:T(8,128)(2,1)S(1)} collective-permute-done((bf16[192,4608]{1,0:T(8,128)(2,1)S(1)}, bf16[192,4608]{1,0:T(8,128)(2,1)S(1)}, u32[]{:S(2)}, u32[]{:S(2)}) %collective-permute-start) | collective-permute-done | bytes 1769504 | tf_op jit(solution)/shard_map/ppermute | solution.py:297
  10.0 4.0 %shard_map.146 = bf16[2,4,4,8,16,512]{5,4,3,2,1,0:T(8,128)(2,1)} custom-call(s32[1]{0:T(128)} %bitcast.core_ref, bf16[192,4096]{1,0:T(8,128)(2,1)S(1)} %get-tuple-element.9.kept_ref, bf16[192,512]{1,0:T(8,128)(2,1)S(1)} %get-tuple-element.10.scaled_ref, bf16[192,4608]{1,0:T(8,128)(2,1)S(1)} %collective-permute-done.got_ref), custom_call_target="tpu_custom_call" | custom-call | flops 1610612736 | bytes 9437184 | tf_op jit(solution)/shard_map/pallas_call | solution.py:200
  14.0 32.6 %all_to_all.10.value_ref = bf16[8,32,16,512]{3,2,1,0:T(8,128)(2,1)S(1)} all-to-all(bf16[8,32,16,512]{3,2,1,0:T(8,128)(2,1)} %bitcast.2), channel_id=1, replica_groups={{0,2,1,3,64,66,65,67},{6,4,7,5,70,68,71,69},{10,8,11,9,74,72,75,73},{12..., dimensions={0} | all-to-all | bytes 8388608 | tf_op jit(solution)/shard_map/all_to_all | solution.py:259
  46.7 0.0 copy-start.5
  46.7 0.0 copy-start.6
  46.7 0.0 copy-start.7
  46.7 1.4 %shard_map.147 = bf16[32,16,512]{2,1,0:T(8,128)(2,1)} custom-call(bf16[8,32,16,512]{3,2,1,0:T(8,128)(2,1)S(1)} %all_to_all.10.value_ref), custom_call_target="tpu_custom_call" | custom-call | flops 2097152 | bytes 5242880 | tf_op jit(solution)/shard_map/pallas_call | solution.py:242
  48.1 16.5 %all-to-all-start.1 = ((bf16[32,16,512]{2,1,0:T(8,128)(2,1)}), bf16[32,16,512]{2,1,0:T(8,128)(2,1)S(1)}, u32[]{:S(2)}, u32[]{:S(2)}) async-start(bf16[32,16,512]{2,1,0:T(8,128)(2,1)} %shard_map.147), calls=%async_computation.1 | async-start | bytes 1048576 | tf_op jit(solution)/shard_map/all_to_all | solution.py:259
  64.6 0.0 copy-done.8
  64.6 0.1 dynamic_slice.7
  64.7 0.1 broadcast_in_dim.2
  64.8 6.0 %collective-permute-start.1 = (bf16[16,640]{1,0:T(8,128)(2,1)S(1)}, bf16[16,640]{1,0:T(8,128)(2,1)S(1)}, u32[]{:S(2)}, u32[]{:S(2)}) collective-permute-start(bf16[16,640]{1,0:T(8,128)(2,1)S(1)} %pad_maximum_fusion), channel_id=1, source_target_pairs={{256,0},{288,1},{320,2},{352,3},{384,4},{416,5},{448,6},{480,7},{0... | collective-permute-start | bytes 61448 | tf_op jit(solution)/shard_map/ppermute | solution.py:298
  70.8 5.7 %collective-permute-done.1 = bf16[16,640]{1,0:T(8,128)(2,1)S(1)} collective-permute-done((bf16[16,640]{1,0:T(8,128)(2,1)S(1)}, bf16[16,640]{1,0:T(8,128)(2,1)S(1)}, u32[]{:S(2)}, u32[]{:S(2)}) %collective-permute-start.1) | collective-permute-done | bytes 20512 | tf_op jit(solution)/shard_map/ppermute | solution.py:298
  76.5 0.1 slice_reduce_fusion
  76.7 6.2 %all-to-all-done.1 = bf16[32,16,512]{2,1,0:T(8,128)(2,1)S(1)} async-done(((bf16[32,16,512]{2,1,0:T(8,128)(2,1)}), bf16[32,16,512]{2,1,0:T(8,128)(2,1)S(1)}, u32[]{:S(2)}, u32[]{:S(2)}) %all-to-all-start.1) | async-done | bytes 524320 | tf_op jit(solution)/shard_map/all_to_all | solution.py:259
  82.9 0.1 convert_reduce_fusion
  83.0 0.0 copy-done.2
  83.0 0.8 multiply_subtract_fusion
  83.9 0.5 multiply_subtract_fusion.1
  (13 shorter events, 0.0 us)
Async XLA Ops:
  0.6 64.1 %copy-start = (bf16[512,512]{1,0:T(8,128)(2,1)S(1)}, bf16[512,512]{1,0:T(8,128)(2,1)}, u32[]{:S(2)}) copy-start(bf16[512,512]{1,0:T(8,128)(2,1)} %param.13) | copy-start | bytes 1572868
  0.7 1.0 %copy-start.1 = (bf16[192,512]{1,0:T(8,128)(2,1)S(1)}, bf16[192,512]{1,0:T(8,128)(2,1)}, u32[]{:S(2)}) copy-start(bf16[192,512]{1,0:T(8,128)(2,1)} %key_ref.1) | copy-start | bytes 589828
  4.4 5.6 %collective-permute-start = (bf16[192,4608]{1,0:T(8,128)(2,1)S(1)}, bf16[192,4608]{1,0:T(8,128)(2,1)S(1)}, u32[]{:S(2)}, u32[]{:S(2)}) collective-permute-start(bf16[192,4608]{1,0:T(8,128)(2,1)S(1)} %get-tuple-element.11), channel_id=1, source_target_pairs={{0,16},{16,0},{1,17},{17,1},{2,18},{18,2},{3,19},{19,3},{4,20},{20... | collective-permute-start | bytes 5308424 | tf_op jit(solution)/shard_map/ppermute | solution.py:297
  46.7 18.0 %copy-start.8 = (bf16[512]{0:T(512)(128)(2,1)S(1)}, bf16[512]{0:T(512)(128)(2,1)}, u32[]{:S(2)}) copy-start(bf16[512]{0:T(512)(128)(2,1)} %param.12) | copy-start | bytes 3076
  46.7 36.3 %copy-start.2 = (f32[16,512]{1,0:T(8,128)S(1)}, f32[16,512]{1,0:T(8,128)}, u32[]{:S(2)}) copy-start(f32[16,512]{1,0:T(8,128)} %param.14) | copy-start | bytes 98308
  46.7 36.3 %copy-start.3 = (f32[16,512]{1,0:T(8,128)S(1)}, f32[16,512]{1,0:T(8,128)}, u32[]{:S(2)}) copy-start(f32[16,512]{1,0:T(8,128)} %param.15) | copy-start | bytes 98308
  46.7 36.3 %copy-start.4 = (f32[16,512]{1,0:T(8,128)S(1)}, f32[16,512]{1,0:T(8,128)}, u32[]{:S(2)}) copy-start(f32[16,512]{1,0:T(8,128)} %param.16) | copy-start | bytes 98308
  46.7 37.2 %copy-start.5 = (f32[16]{0:T(128)S(1)}, f32[16]{0:T(128)}, u32[]{:S(2)}) copy-start(f32[16]{0:T(128)} %param.17) | copy-start | bytes 196
  46.7 37.2 %copy-start.6 = (f32[16]{0:T(128)S(1)}, f32[16]{0:T(128)}, u32[]{:S(2)}) copy-start(f32[16]{0:T(128)} %param.18) | copy-start | bytes 196
  46.7 37.2 %copy-start.7 = (f32[16]{0:T(128)S(1)}, f32[16]{0:T(128)}, u32[]{:S(2)}) copy-start(f32[16]{0:T(128)} %param.19) | copy-start | bytes 196
  48.1 34.8 %all-to-all-start.1 = ((bf16[32,16,512]{2,1,0:T(8,128)(2,1)}), bf16[32,16,512]{2,1,0:T(8,128)(2,1)S(1)}, u32[]{:S(2)}, u32[]{:S(2)}) async-start(bf16[32,16,512]{2,1,0:T(8,128)(2,1)} %shard_map.147), calls=%async_computation.1 | async-start | bytes 1048576 | tf_op jit(solution)/shard_map/all_to_all | solution.py:259
  64.8 11.7 %collective-permute-start.1 = (bf16[16,640]{1,0:T(8,128)(2,1)S(1)}, bf16[16,640]{1,0:T(8,128)(2,1)S(1)}, u32[]{:S(2)}, u32[]{:S(2)}) collective-permute-start(bf16[16,640]{1,0:T(8,128)(2,1)S(1)} %pad_maximum_fusion), channel_id=1, source_target_pairs={{256,0},{288,1},{320,2},{352,3},{384,4},{416,5},{448,6},{480,7},{0... | collective-permute-start | bytes 61448 | tf_op jit(solution)/shard_map/ppermute | solution.py:298
